TPU v7x, 32 devices: a whole 2x2x4 slice. The times are simulated.
32 devices in a mesh: ka: 4 (over z), mode: 2 (over y), row: 4 (over x, core).
Axes of the slice: x: 2, y: 2, z: 4, core: 2. Of those that a mesh axis runs over, the one named last changes fastest.
Arguments:
- vectors: float32 [4, 8, 16, 16, 8, 512], P('ka', None, 'mode', 'row'), may hold values from -6 to 6
- previous: float32 [4, 8, 16, 16, 8, 512], P('ka', None, 'mode', 'row'), may hold values from -6 to 6
- beta: float32 [8, 8], replicated, may hold values from -2 to 2
- potential: float32 [16, 16, 8, 512], P('mode', 'row'), may hold values from 0.1 to 10
- coriolis_fn: float32 [16, 16, 8, 512], P('mode', 'row'), may hold values from 0.5 to 2
- second_fn: float32 [16, 16, 8, 512], P('mode', 'row'), may hold values from 0.5 to 2
- rot_const: float32 [4], replicated, may hold values from 0.02 to 0.06
- coupling: float32 [2, 4], replicated, may hold values from 0.3 to 1.5
- kin_one: float32 [16, 16], replicated, may hold values from -1.5 to 1.5
- kin_two: float32 [16, 16], replicated, may hold values from -1.5 to 1.5
- kin_three: float32 [8, 8], replicated, may hold values from -2 to 2
- kin_four: float32 [8, 8], replicated, may hold values from -2 to 2
- kin_five: float32 [8, 8], replicated, may hold values from -2 to 2
- kin_six: float32 [8, 8], replicated, may hold values from -2 to 2
- coriolis_derivative: float32 [8, 8], replicated, may hold values from -2 to 2
Outputs:
- basis: float32 [4, 8, 16, 16, 8, 512], P('ka', None, 'mode', 'row')
- alpha: float32 [8, 8], replicated
- lower_factor: float32 [8, 8], replicated
All inputs are finite; a program needn't handle non-finite values.
Results may differ from a plain program's by a relative error of at most 0.0003.
Values sent between devices are 32-bit elements; how exact they have to be, the bound alone decides.
No kernel may reach another device: no remote copies, remote signals or barrier semaphores. Data moves between devices by JAX's collectives and lax.ppermute only.
A program may use at most 256 MiB of HBM per device.

v0:
```python
import functools

import jax
import jax.numpy as jnp
from jax import lax
from jax.experimental import pallas as pl
from jax.experimental.pallas import tpu as pltpu
from jax.sharding import PartitionSpec as P

precise_mode = lax.Precision.HIGHEST
ALL_AXES = ("ka", "mode", "row")
VMEM_BYTES = 32 * 1024 * 1024
SMALL_VMEM_BYTES = 16 * 1024 * 1024
FULL_VMEM_BYTES = 56 * 1024 * 1024
LANES = 128
HOP_WEIGHT = 25_000_000_000
SUBLANES = 8


def precise_dot(left, right):
    return jnp.dot(left, right, precision=precise_mode, preferred_element_type=jnp.float32)


def whole_spec(shape):
    return pl.BlockSpec(shape, lambda *_: (0,) * len(shape))


def pair_exchange(value, axis, first):
    peers = lax.axis_size(axis)
    pairs = []
    for low in range(first, peers - 1, 2):
        pairs += [(low, low + 1), (low + 1, low)]
    return lax.ppermute(value, axis, pairs)


def vector_groups(nvec):
    return [tuple(range(at, min(at + 4, nvec))) for at in range(0, nvec, 4)]


def tiles(rows, width):
    return [
        (slice(r, r + SUBLANES), slice(c, c + LANES))
        for r in range(0, rows, SUBLANES)
        for c in range(0, width, LANES)
    ]


def packed_columns(sums, nvec, offset, lane):
    packed = jnp.zeros((nvec, LANES), jnp.float32)
    for j in range(nvec):
        stacked = jnp.stack([sums(i, j) for i in range(nvec)])
        column = jnp.sum(jnp.sum(stacked, axis=1), axis=1, keepdims=True)
        packed = packed + jnp.where(lane == offset + j, column, 0.0)
    return packed


def add_products(nvec, left_ref, right_ref, sums, number, places, symmetric):
    groups = vector_groups(nvec)
    for ours in groups:
        for other in groups:
            pairs = [(i, j) for i in ours for j in other if i <= j or not symmetric]
            if not pairs:
                continue
            totals = {pair: sums[number, pair[0] * nvec + pair[1]] for pair in pairs}
            for place in places:
                lefts = {i: left_ref[(i, *place)] for i in {p[0] for p in pairs}}
                rights = {j: right_ref[(j, *place)] for j in {p[1] for p in pairs}}
                for i, j in pairs:
                    totals[i, j] = totals[i, j] + lefts[i] * rights[j]
            for i, j in pairs:
                sums[number, i * nvec + j] = totals[i, j]


def resident_kernel(nvec, vec_ref, fn_ref, *refs):
    out_ref, copy_ref, fn_copy_ref, sums = refs[-4:]
    step = pl.program_id(0)

    @pl.when(step == 0)
    def _():
        sums[...] = jnp.zeros_like(sums)

    copy_ref[...] = vec_ref[...]
    fn_copy_ref[...] = fn_ref[...]
    add_products(nvec, vec_ref, vec_ref, sums, 0, tiles(*vec_ref.shape[1:]), True)

    @pl.when(step == pl.num_programs(0) - 1)
    def _():
        lane = lax.broadcasted_iota(jnp.int32, (nvec, LANES), 1)
        out_ref[...] = packed_columns(
            lambda i, j: sums[0, min(i, j) * nvec + max(i, j)], nvec, 2 * nvec, lane
        )


def resident(vec, skip_fn, after, block_rows):
    nvec, rows, width = vec.shape
    block = pl.BlockSpec((nvec, block_rows, width), lambda s: (0, s, 0))
    fn_block = pl.BlockSpec((block_rows, width), lambda s: (s, 0))
    return pl.pallas_call(
        functools.partial(resident_kernel, nvec),
        grid=(rows // block_rows,),
        in_specs=[block, fn_block] + [pl.BlockSpec(memory_space=pl.ANY)] * len(after),
        out_specs=[whole_spec((nvec, LANES)), block, fn_block],
        out_shape=[
            jax.ShapeDtypeStruct((nvec, LANES), jnp.float32),
            jax.ShapeDtypeStruct(vec.shape, jnp.float32),
            jax.ShapeDtypeStruct(skip_fn.shape, jnp.float32),
        ],
        scratch_shapes=[pltpu.VMEM((1, nvec * nvec, SUBLANES, LANES), jnp.float32)],
        compiler_params=pltpu.CompilerParams(vmem_limit_bytes=VMEM_BYTES),
        cost_estimate=pl.CostEstimate(
            flops=nvec * (nvec + 1) * rows * width, bytes_accessed=8 * vec.size, transcendentals=0
        ),
        name="resident",
    )(vec, skip_fn, *after)


def split_kernel(start, vec_ref, out_ref, held, sems):
    count, rows, _ = out_ref.shape
    loads = [
        pltpu.make_async_copy(vec_ref.at[i, pl.ds(start, rows)], held.at[i], sems.at[0, i])
        for i in range(count)
    ]
    stores = [
        pltpu.make_async_copy(held.at[i], out_ref.at[i], sems.at[1, i]) for i in range(count)
    ]
    for load in loads:
        load.start()
    for load, store in zip(loads, stores):
        load.wait()
        store.start()
    for store in stores:
        store.wait()


def split_rows(vec, start, stop):
    nvec, _, width = vec.shape
    shape = (nvec, stop - start, width)
    return pl.pallas_call(
        functools.partial(split_kernel, start),
        in_specs=[pl.BlockSpec(memory_space=pl.ANY)],
        out_specs=pl.BlockSpec(memory_space=pl.ANY),
        out_shape=jax.ShapeDtypeStruct(shape, jnp.float32),
        scratch_shapes=[
            pltpu.VMEM(shape, jnp.float32),
            pltpu.SemaphoreType.DMA((2, nvec)),
        ],
        compiler_params=pltpu.CompilerParams(vmem_limit_bytes=FULL_VMEM_BYTES),
        cost_estimate=pl.CostEstimate(
            flops=0, bytes_accessed=8 * nvec * (stop - start) * width, transcendentals=0
        ),
        name="split_rows",
    )(vec)


def handed_on(array, weight, after=()):
    return pl.pallas_call(
        lambda *_: None,
        in_specs=[pl.BlockSpec(memory_space=pl.ANY)] * (1 + len(after)),
        out_specs=pl.BlockSpec(memory_space=pl.ANY),
        out_shape=jax.ShapeDtypeStruct(array.shape, array.dtype),
        input_output_aliases={0: 0},
        cost_estimate=pl.CostEstimate(flops=weight, bytes_accessed=0, transcendentals=0),
        name="handed_on",
    )(array, *after)


def kron_term(matrix, size, stride, extent, row_offset=0, column_offset=0, sign=1.0):
    points = matrix.shape[0]

    def digits(shape, axis):
        index = lax.broadcasted_iota(jnp.int32, shape, axis)
        return index, lax.rem(lax.div(index, stride), size)

    def picks(offset):
        _, digit = digits((extent, points), 0)
        point = lax.broadcasted_iota(jnp.int32, (extent, points), 1)
        return jnp.where(digit + offset == point, 1.0, 0.0)

    def transposed_dot(one, two):
        return lax.dot_general(
            one, two, (((1,), (1,)), ((), ())), precision=precise_mode,
            preferred_element_type=jnp.float32,
        )

    picked = picks(row_offset)
    picked = 0.5 * (precise_dot(picked, matrix) + sign * transposed_dot(picked, matrix))
    spread = transposed_dot(picked, picks(column_offset))
    row, row_digit = digits((extent, extent), 0)
    column, column_digit = digits((extent, extent), 1)
    same = (row - row_digit * stride) == (column - column_digit * stride)
    return jnp.where(same, spread, 0.0)


def operators_kernel(
    points, group, at_ref, coupling_ref, one_ref, two_ref, three_ref, four_ref, five_ref, six_ref,
    der_ref, *refs,
):
    left_ref, mode_ref, tail_ref, near_ref = refs[-4:]
    points_one, points_two, points_three = points
    rows = points_one * points_two * points_three
    stride = points_two * points_three
    mine = at_ref[1] * points_two
    left_ref[0] = kron_term(two_ref[...], points_two, points_three, rows, mine, mine) + kron_term(
        three_ref[...], points_three, 1, rows
    )
    if group > 1:
        sibling = at_ref[2] * points_two
        left_ref[1] = kron_term(two_ref[...], points_two, points_three, rows, mine, sibling)
    mode_ref[...] = kron_term(one_ref[...], one_ref.shape[0], stride, mode_ref.shape[0])
    width = tail_ref.shape[0]
    fives, sixes = five_ref.shape[0], six_ref.shape[0]
    tail_ref[...] = (
        kron_term(four_ref[...], four_ref.shape[0], fives * sixes, width)
        + kron_term(five_ref[...], fives, sixes, width)
        + kron_term(six_ref[...], sixes, 1, width)
    )
    twist = kron_term(der_ref[...], sixes, 1, near_ref.shape[1], sign=-1.0)
    block = at_ref[0]
    even = lax.rem(block, 2) == 0
    from_above = -coupling_ref[0, block]
    from_below = coupling_ref[0, jnp.maximum(block - 1, 0)]
    near_ref[0] = jnp.where(even, from_above, from_below) * twist
    near_ref[1] = jnp.where(even, from_below, from_above) * twist


def operators(points, group, mode_extent, width, span, at, coupling, matrices, after):
    rows = points[0] * points[1] * points[2]
    shapes = [
        (group, rows, rows), (mode_extent, mode_extent), (width, width), (2, span, span)
    ]
    smem = pl.BlockSpec(memory_space=pltpu.SMEM)
    return pl.pallas_call(
        functools.partial(operators_kernel, points, group),
        in_specs=[smem, smem]
        + [pl.BlockSpec(memory_space=pltpu.VMEM)] * len(matrices)
        + [pl.BlockSpec(memory_space=pl.ANY)] * len(after),
        out_specs=[pl.BlockSpec(memory_space=pltpu.VMEM)] * len(shapes),
        out_shape=[jax.ShapeDtypeStruct(shape, jnp.float32) for shape in shapes],
        compiler_params=pltpu.CompilerParams(vmem_limit_bytes=VMEM_BYTES),
        cost_estimate=pl.CostEstimate(
            flops=500_000_000, bytes_accessed=4_000_000, transcendentals=0
        ),
        name="operators",
    )(at, coupling, *matrices, *after)


def crossing_kernel(points, group, at_ref, two_ref, *refs):
    points_one, points_two, points_three = points
    held_refs, out_refs = refs[:group], refs[group:]
    owners = [at_ref[1], at_ref[2]][:group]
    peers = two_ref.shape[0] // points_two
    stride = points_two * points_three
    for number, out_ref in enumerate(out_refs):
        target = lax.rem(at_ref[1] + group * (number + 1), peers) * points_two
        coefs = {
            (a, k, b): 0.5
            * (
                two_ref[target + a, owners[k] * points_two + b]
                + two_ref[owners[k] * points_two + b, target + a]
            )
            for a in range(points_two)
            for k in range(group)
            for b in range(points_two)
        }
        for start in range(0, points_one * stride, stride):
            for _, lanes in tiles(SUBLANES, out_ref.shape[2]):
                for inner in range(0, points_three, SUBLANES):
                    values = {
                        (k, b): held_refs[k][0, pl.ds(start + b * points_three + inner, SUBLANES), lanes]
                        for k in range(group)
                        for b in range(points_two)
                    }
                    for a in range(points_two):
                        total = None
                        for (k, b), value in values.items():
                            term = coefs[a, k, b] * value
                            total = term if total is None else total + term
                        out_ref[0, pl.ds(start + a * points_three + inner, SUBLANES), lanes] = total


def crossing(points, at, two, held, count):
    nvec, rows, width = held[0].shape
    one = pl.BlockSpec((1, rows, width), lambda i: (i, 0, 0))
    smem = pl.BlockSpec(memory_space=pltpu.SMEM)
    return pl.pallas_call(
        functools.partial(crossing_kernel, points, len(held)),
        grid=(nvec,),
        in_specs=[smem, smem] + [one] * len(held),
        out_specs=[one] * count,
        out_shape=[jax.ShapeDtypeStruct(held[0].shape, jnp.float32)] * count,
        compiler_params=pltpu.CompilerParams(vmem_limit_bytes=VMEM_BYTES),
        cost_estimate=pl.CostEstimate(
            flops=2 * held[0].size * points[1] * len(held) * count,
            bytes_accessed=4 * held[0].size * (len(held) + count),
            transcendentals=0,
        ),
        name="crossing",
    )(at, two, *held)


def local_kernel(nvec, nblocks, group, at_ref, rot_ref, beta_ref, *refs):
    held_refs = refs[:group]
    old_ref, pot_ref, left_ref, tail_ref, out_ref = refs[group:]
    me = pl.program_id(0)
    block = at_ref[0]
    level = (block - nblocks // 2).astype(jnp.float32)
    current = held_refs[0][0]
    total = (pot_ref[...] + rot_ref[block] * level * level) * current
    for j in range(nvec):
        total = total - beta_ref[me, j] * old_ref[j]
    total = total + precise_dot(current, tail_ref[...])
    for number, held_ref in enumerate(held_refs):
        total = total + precise_dot(left_ref[number], held_ref[0])
    out_ref[0] = total


def local_terms(nblocks, at, rot_const, beta, held, old, pot, left, tail):
    nvec, rows, width = old.shape
    one = pl.BlockSpec((1, rows, width), lambda i: (i, 0, 0))
    smem = pl.BlockSpec(memory_space=pltpu.SMEM)
    return pl.pallas_call(
        functools.partial(local_kernel, nvec, nblocks, len(held)),
        grid=(nvec,),
        in_specs=[smem, smem, smem]
        + [one] * len(held)
        + [
            whole_spec(old.shape),
            whole_spec(pot.shape),
            pl.BlockSpec((len(held), rows, rows), lambda i: (0, 0, 0)),
            whole_spec(tail.shape),
        ],
        out_specs=one,
        out_shape=jax.ShapeDtypeStruct(old.shape, jnp.float32),
        compiler_params=pltpu.CompilerParams(vmem_limit_bytes=VMEM_BYTES),
        cost_estimate=pl.CostEstimate(
            flops=12 * old.size * (rows * len(held) + width),
            bytes_accessed=4 * old.size * (2 + len(held)),
            transcendentals=0,
        ),
        name="local_terms",
    )(at, rot_const, beta, *held, old, pot, left, tail)


def mode_kinetic_kernel(peers, in_ref, mat_ref, out_ref):
    rows = in_ref.shape[2]
    field = jnp.concatenate([in_ref[peer, 0] for peer in range(peers)], axis=0)
    field = precise_dot(mat_ref[...], field)
    for peer in range(peers):
        out_ref[peer, 0] = field[peer * rows : (peer + 1) * rows]


def mode_kinetic(field, matrix, peers):
    nvec, rows, width = field.shape
    held = nvec // peers
    block = pl.BlockSpec((peers, 1, rows, width), lambda q: (0, q, 0, 0))
    out = pl.pallas_call(
        functools.partial(mode_kinetic_kernel, peers),
        grid=(held,),
        in_specs=[block, whole_spec(matrix.shape)],
        out_specs=block,
        out_shape=jax.ShapeDtypeStruct((peers, held, rows, width), jnp.float32),
        compiler_params=pltpu.CompilerParams(vmem_limit_bytes=VMEM_BYTES),
        cost_estimate=pl.CostEstimate(
            flops=12 * field.size * matrix.shape[0], bytes_accessed=8 * field.size, transcendentals=0
        ),
        name="mode_kinetic",
    )(field.reshape(peers, held, rows, width), matrix)
    return out.reshape(field.shape)


def join_kernel(starts, sum_count, at_ref, work_ref, cor_ref, near_ref, *refs):
    pieces = len(starts)
    first_refs, second_refs = refs[:pieces], refs[pieces : 2 * pieces]
    sum_refs = refs[2 * pieces : 2 * pieces + sum_count]
    out_ref = refs[-1]
    span = near_ref.shape[1]
    even = lax.rem(at_ref[0], 2) == 0
    for start, first_ref, second_ref in zip(starts, first_refs, second_refs):
        place = slice(start, start + first_ref.shape[1])
        for at in range(0, work_ref.shape[2], span):
            part = slice(at, at + span)
            total = work_ref[0, place, part]
            for sum_ref in sum_refs:
                total = total + sum_ref[0, place, part]
            twist_fn = cor_ref[place, part]
            if_even = jnp.where(even, twist_fn, 1.0)
            if_odd = jnp.where(even, 1.0, twist_fn)
            total = total + if_even * precise_dot(
                if_odd * first_ref[0, :, part], near_ref[0]
            )
            out_ref[0, place, part] = total + if_odd * precise_dot(
                if_even * second_ref[0, :, part], near_ref[1]
            )


def join_terms(at, work, cor, near, starts, first, second, sums):
    nvec, rows, width = work.shape
    one = pl.BlockSpec((1, rows, width), lambda i: (i, 0, 0))
    pieces = [pl.BlockSpec((1, b.shape[1], width), lambda i: (i, 0, 0)) for b in first]
    return pl.pallas_call(
        functools.partial(join_kernel, tuple(starts), len(sums)),
        grid=(nvec,),
        in_specs=[
            pl.BlockSpec(memory_space=pltpu.SMEM), one, whole_spec(cor.shape), whole_spec(near.shape)
        ]
        + pieces
        + pieces
        + [one] * len(sums),
        out_specs=one,
        out_shape=jax.ShapeDtypeStruct(work.shape, jnp.float32),
        compiler_params=pltpu.CompilerParams(vmem_limit_bytes=VMEM_BYTES),
        cost_estimate=pl.CostEstimate(
            flops=24 * work.size * near.shape[1], bytes_accessed=24 * work.size, transcendentals=0
        ),
        name="join_terms",
    )(at, work, cor, near, *first, *second, *sums)


def far_terms_kernel(
    nvec, start, coef_ref, work_ref, first_ref, second_ref, fn_ref, vec_ref, before_ref, out_ref,
    sum_ref, sums,
):
    del work_ref
    step = pl.program_id(0)
    _, block_rows, width = first_ref.shape

    @pl.when(step == 0)
    def _():
        sums[...] = jnp.zeros_like(sums)

    at = pl.multiple_of(start + step * block_rows, SUBLANES)
    places = []
    for rows_here, lanes in tiles(block_rows, width):
        place = (pl.ds(at + rows_here.start, SUBLANES), lanes)
        places.append(place)
        skip_fn = fn_ref[place]
        first_fn = coef_ref[0] * skip_fn
        second_fn = coef_ref[1] * skip_fn
        for i in range(nvec):
            out_ref[(i, *place)] = (
                out_ref[(i, *place)]
                + first_fn * first_ref[i, rows_here, lanes]
                + second_fn * second_ref[i, rows_here, lanes]
            )
    add_products(nvec, vec_ref, out_ref, sums, 0, places, False)
    add_products(nvec, out_ref, out_ref, sums, 1, places, True)

    @pl.when(step == pl.num_programs(0) - 1)
    def _():
        lane = lax.broadcasted_iota(jnp.int32, (nvec, LANES), 1)
        packed = before_ref[...]
        packed = packed + packed_columns(lambda i, j: sums[0, j * nvec + i], nvec, 0, lane)
        packed = packed + packed_columns(
            lambda i, j: sums[1, min(i, j) * nvec + max(i, j)], nvec, nvec, lane
        )
        sum_ref[...] = jnp.broadcast_to(packed[None], sum_ref.shape)


def far_terms(coef, work, first, second, skip_fn, vec, before, start, block_rows, copies):
    nvec, _, width = work.shape
    rows = first.shape[1]
    whole = pl.BlockSpec(memory_space=pltpu.VMEM)
    block = pl.BlockSpec((nvec, block_rows, width), lambda s: (0, s, 0))
    work, skip_fn, vec = (
        pltpu.with_memory_space_constraint(array, pltpu.VMEM) for array in (work, skip_fn, vec)
    )
    return pl.pallas_call(
        functools.partial(far_terms_kernel, nvec, start),
        grid=(rows // block_rows,),
        in_specs=[
            pl.BlockSpec(memory_space=pltpu.SMEM), whole, block, block, whole, whole, whole
        ],
        out_specs=[whole, whole],
        out_shape=[
            jax.ShapeDtypeStruct(work.shape, jnp.float32),
            jax.ShapeDtypeStruct((copies, nvec, LANES), jnp.float32),
        ],
        scratch_shapes=[pltpu.VMEM((2, nvec * nvec, SUBLANES, LANES), jnp.float32)],
        input_output_aliases={1: 0},
        compiler_params=pltpu.CompilerParams(vmem_limit_bytes=SMALL_VMEM_BYTES),
        cost_estimate=pl.CostEstimate(
            flops=3 * nvec * nvec * rows * width,
            bytes_accessed=20 * first.size,
            transcendentals=0,
        ),
        name="far_terms",
    )(coef, work, first, second, skip_fn, vec, before)


def small_dot(left, right):
    terms = [left[:, k : k + 1] * right[k : k + 1, :] for k in range(right.shape[0])]
    while len(terms) > 1:
        terms = [sum(terms[k + 1 : k + 2], terms[k]) for k in range(0, len(terms), 2)]
    return terms[0]


def small_algebra(nvec, count, packed):
    packed = packed * (1.0 / count)
    cross = packed.T[0:nvec, :]
    cross_turned = packed[:, 0:nvec]
    work_gram = packed[:, nvec : 2 * nvec]
    vec_gram = packed[:, 2 * nvec : 3 * nvec]
    total = 2.0 * cross - small_dot(vec_gram, cross)
    total_turned = 2.0 * cross_turned - small_dot(cross_turned, vec_gram)
    gram = work_gram - small_dot(total_turned, cross) - small_dot(cross_turned, total)
    gram = gram + small_dot(total_turned, small_dot(vec_gram, total))
    row = lax.broadcasted_iota(jnp.int32, (nvec, nvec), 0)
    column = lax.broadcasted_iota(jnp.int32, (nvec, nvec), 1)
    inverse = jnp.where(row == column, 1.0, 0.0)
    lower = jnp.zeros((nvec, nvec), jnp.float32)
    for at in range(nvec):
        pivot = gram[at : at + 1, at : at + 1]
        scale = lax.rsqrt(pivot)
        scale = scale * (1.5 - 0.5 * pivot * scale * scale)
        scaled = gram[:, at : at + 1] * scale
        lower = jnp.where((column == at) & (row >= at), scaled, lower)
        pivot_row = inverse[at : at + 1, :] * scale
        factor = jnp.where(row > at, scaled, 0.0)
        inverse = jnp.where(row == at, pivot_row, inverse - factor * pivot_row)
        gram = gram - factor * (gram[at : at + 1, :] * scale)
    return total, lower, inverse, -small_dot(inverse, total_turned)


def basis_kernel(nvec, count, sum_ref, work_ref, vec_ref, out_ref, alpha_ref, lower_ref, coefs):
    @pl.when(pl.program_id(0) == 0)
    def _():
        packed = sum_ref[0]
        for other in range(1, sum_ref.shape[0]):
            packed = packed + sum_ref[other]
        total, lower, inverse, mixing = small_algebra(nvec, count, packed)
        alpha_ref[...] = total
        lower_ref[...] = lower
        for number, matrix in enumerate((inverse, mixing)):
            for i in range(nvec):
                for j in range(nvec):
                    coefs[number, i * nvec + j] = jnp.broadcast_to(
                        matrix[i : i + 1, j : j + 1], (SUBLANES, LANES)
                    )

    start = pl.multiple_of(pl.program_id(0) * out_ref.shape[1], out_ref.shape[1])
    places = tiles(*out_ref.shape[1:])
    for at in range(0, len(places), 4):
        group = places[at : at + 4]
        held = [(pl.ds(start + place.start, SUBLANES), lanes) for place, lanes in group]
        for ours in vector_groups(nvec):
            totals = {}
            for number, ref in ((1, vec_ref), (0, work_ref)):
                for j in range(nvec):
                    outs = [i for i in ours if number == 1 or j <= i]
                    if not outs:
                        continue
                    values = [ref[(j, *place)] for place in held]
                    for i in outs:
                        coef = coefs[number, i * nvec + j]
                        for spot, value in enumerate(values):
                            term = coef * value
                            here = (i, spot)
                            totals[here] = totals[here] + term if here in totals else term
            for i in ours:
                for spot, place in enumerate(group):
                    out_ref[(i, *place)] = totals[i, spot]


def basis_of(count, sums, work, vec, block_rows):
    nvec, rows, width = work.shape
    block = pl.BlockSpec((nvec, block_rows, width), lambda s: (0, s, 0))
    small = jax.ShapeDtypeStruct((nvec, nvec), jnp.float32)
    whole = pl.BlockSpec(memory_space=pltpu.VMEM)
    work, vec = (pltpu.with_memory_space_constraint(array, pltpu.VMEM) for array in (work, vec))
    return pl.pallas_call(
        functools.partial(basis_kernel, nvec, count),
        grid=(rows // block_rows,),
        in_specs=[whole, whole, whole],
        out_specs=[block, whole_spec(small.shape), whole_spec(small.shape)],
        out_shape=[jax.ShapeDtypeStruct(work.shape, jnp.float32), small, small],
        scratch_shapes=[pltpu.VMEM((2, nvec * nvec, SUBLANES, LANES), jnp.float32)],
        compiler_params=pltpu.CompilerParams(vmem_limit_bytes=SMALL_VMEM_BYTES),
        cost_estimate=pl.CostEstimate(
            flops=4 * nvec * work.size, bytes_accessed=12 * work.size, transcendentals=0
        ),
        name="basis",
    )(sums, work, vec)


def shards(
    vectors,
    previous,
    beta,
    potential,
    coriolis_fn,
    second_fn,
    rot_const,
    coupling,
    kin_one,
    kin_two,
    kin_three,
    kin_four,
    kin_five,
    kin_six,
    coriolis_derivative,
):
    _, nvec, *points, width = vectors.shape
    rows = points[0] * points[1] * points[2]
    devices = lax.axis_size(ALL_AXES)
    block_index = lax.axis_index("ka")
    nblocks = lax.axis_size("ka")
    row_peers = lax.axis_size("row")
    mode_peers = lax.axis_size("mode")
    row_at = lax.axis_index("row")
    current = vectors.reshape(nvec, rows, width)
    older = previous.reshape(nvec, rows, width)
    block_rows = min(32, rows // 2)

    cut = rows * 3 // 4 // block_rows * block_rows or rows // 2
    starts, stops = [0, cut], [cut, rows]
    parts = [split_rows(current, start, stop) for start, stop in zip(starts, stops)]
    near_first = [pair_exchange(part, "ka", 0) for part in parts]
    near_second = [pair_exchange(part, "ka", 1) for part in parts]
    at = jnp.stack([block_index, row_at, row_at ^ 1]).astype(jnp.int32)
    group = 2 - row_peers % 2
    held = [current]
    if group == 2:
        held.append(lax.ppermute(current, "row", [(i, i ^ 1) for i in range(row_peers)]))
    away = row_peers // group - 1
    row_parts = crossing(tuple(points), at, kin_two, held, away) if away else []
    row_sums = [
        lax.ppermute(
            part, "row", [(i, (i + group * (number + 1)) % row_peers) for i in range(row_peers)]
        )
        for number, part in enumerate(row_parts)
    ]

    span = next((s for s in (256, 128) if width % s == 0 and s % kin_six.shape[0] == 0), width)
    left, mode_mat, tail, near = operators(
        tuple(points),
        group,
        mode_peers * rows,
        width,
        span,
        at,
        coupling,
        (kin_one, kin_two, kin_three, kin_four, kin_five, kin_six, coriolis_derivative),
        row_parts,
    )
    near_first[0] = handed_on(near_first[0], HOP_WEIGHT, [*row_parts, mode_mat])
    near_second[0] = handed_on(near_second[0], HOP_WEIGHT, [*row_parts, mode_mat])
    far_first = [pair_exchange(part, "ka", 0) for part in near_second]
    far_second = [pair_exchange(part, "ka", 1) for part in near_first]
    lower_two = jnp.maximum(block_index - 2, 0)
    far_above, far_below = coupling[1, block_index], coupling[1, lower_two]
    even = block_index % 2 == 0
    far_pair = jnp.stack(
        [jnp.where(even, far_above, far_below), jnp.where(even, far_below, far_above)]
    )
    sums, vec, skip_fn = resident(
        current, second_fn.reshape(rows, width), held[1:], block_rows
    )
    mode_shares = lax.all_to_all(vec, "mode", split_axis=0, concat_axis=0, tiled=True)
    mode_shares = mode_kinetic(mode_shares, mode_mat, mode_peers)
    mode_sum = lax.all_to_all(mode_shares, "mode", split_axis=0, concat_axis=0, tiled=True)
    work = local_terms(
        nblocks, at, rot_const, beta, held, older, potential.reshape(rows, width), left, tail
    )
    work = join_terms(
        at,
        work,
        coriolis_fn.reshape(rows, width),
        near,
        starts,
        near_first,
        near_second,
        [mode_sum, *row_sums],
    )
    for number, start in enumerate(starts):
        work, copied = far_terms(
            far_pair,
            work,
            far_first[number],
            far_second[number],
            skip_fn,
            vec,
            sums,
            start,
            block_rows,
            devices if number == len(starts) - 1 else 1,
        )
        sums = copied[0]
    every_sum = lax.all_to_all(copied, ALL_AXES, split_axis=0, concat_axis=0, tiled=True)
    count = float(devices * rows * width)
    basis, alpha, lower = basis_of(count, every_sum, work, vec, block_rows)
    return (basis.reshape(vectors.shape), alpha, lower)


def solution(mesh):
    return jax.shard_map(
        shards,
        mesh=mesh,
        in_specs=(
            P("ka", None, "mode", "row", None, None),
            P("ka", None, "mode", "row", None, None),
            P(),
            P("mode", "row", None, None),
            P("mode", "row", None, None),
            P("mode", "row", None, None),
            P(),
            P(),
            P(),
            P(),
            P(),
            P(),
            P(),
            P(),
            P(),
        ),
        out_specs=(P("ka", None, "mode", "row", None, None), P(), P()),
        check_vma=False,
    )
```

profile of v0, /device:TPU:0, one launch (start us, length us, event | category | flops | bytes accessed | tf_op | source)
XLA Modules:
  0.0 212.8 jit_solution(2510095108434315079)
XLA Ops:
  0.6 0.5 collective-permute-start
  1.1 2.8 %split_rows.2 = f32[8,192,512]{2,1,0:T(8,128)} custom-call(f32[8,256,512]{2,1,0:T(8,128)} %bitcast.17), custom_call_target="tpu_custom_call" | custom-call | bytes 6291456 | tf_op jit(solution)/shard_map/split_rows/pallas_call | solution.py:138
  3.9 0.9 collective-permute-start.3
  4.8 5.3 %collective-permute-start.1 = (f32[8,192,512]{2,1,0:T(8,128)}, f32[8,192,512]{2,1,0:T(8,128)}, u32[]{:S(2)}, u32[]{:S(2)}) collective-permute-start(f32[8,192,512]{2,1,0:T(8,128)} %split_rows.2), channel_id=1, source_target_pairs={{0,8},{8,0},{16,24},{24,16},{1,9},{9,1},{17,25},{25,17},{2,10},{10... | collective-permute-start | bytes 9437192 | tf_op jit(solution)/shard_map/ppermute | solution.py:33
  10.1 2.1 split_rows.3
  12.2 1.6 collective-permute-start.4
  14.0 2.2 %copy-done = f32[1,8,8,4,8,512]{5,4,3,2,1,0:T(8,128)S(1)} copy-done((f32[1,8,8,4,8,512]{5,4,3,2,1,0:T(8,128)S(1)}, f32[1,8,8,4,8,512]{5,4,3,2,1,0:T(8,128)}, u32[]{:S(2)}) %copy-start) | copy-done | bytes 4194328
  16.2 1.0 copy-done.12
  17.2 2.6 %resident.1 = (f32[8,128]{1,0:T(8,128)S(1)}, f32[8,256,512]{2,1,0:T(8,128)S(1)}, f32[256,512]{1,0:T(8,128)S(1)}) custom-call(f32[8,256,512]{2,1,0:T(8,128)S(1)} %bitcast.19, f32[256,512]{1,0:T(8,128)S(1)} %bitcast.23, f32[8,256,512]{2,1,0:T(8,128)} %collective-permute-done.refs_1_.refs_0_), custom_call_target="tpu_custom_call" | custom-call | flops 9437184 | bytes 8388608 | tf_op jit(solution)/shard_map/resident/pallas_call | solution.py:98
  19.8 2.0 copy-done.3
  21.8 0.8 copy-done.10
  22.6 5.7 %all-to-all-start = ((f32[8,256,512]{2,1,0:T(8,128)}), f32[8,256,512]{2,1,0:T(8,128)}, u32[]{:S(2)}, u32[]{:S(2)}) async-start(f32[8,256,512]{2,1,0:T(8,128)} %copy-done.3), calls=%async_computation | async-start | bytes 8388608 | tf_op jit(solution)/shard_map/all_to_all | solution.py:658
  28.3 2.2 %copy-done.1 = f32[1,8,8,4,8,512]{5,4,3,2,1,0:T(8,128)S(1)} copy-done((f32[1,8,8,4,8,512]{5,4,3,2,1,0:T(8,128)S(1)}, f32[1,8,8,4,8,512]{5,4,3,2,1,0:T(8,128)}, u32[]{:S(2)}) %copy-start.1) | copy-done | bytes 4194328
  30.5 7.6 %crossing.1.refs_0_.__1_ = f32[8,256,512]{2,1,0:T(8,128)} custom-call(s32[3]{0:T(128)S(1)} %pad_add_fusion.at_ref, f32[16,16]{1,0:T(8,128)S(1)} %copy-done.16, f32[8,256,512]{2,1,0:T(8,128)S(1)} %bitcast.20, f32[8,256,512]{2,1,0:T(8,128)} %collective-permute-done.refs_1_.refs_0_), custom_call_target="tpu_custom_call" | custom-call | flops 16777216 | bytes 12582912 | tf_op jit(solution)/shard_map/crossing/pallas_call | solution.py:285
  38.1 1.5 collective-permute-start.5
  39.7 9.7 %operators.1 = (f32[2,256,256]{2,1,0:T(8,128)S(1)}, f32[512,512]{1,0:T(8,128)S(1)}, f32[512,512]{1,0:T(8,128)S(1)}, f32[2,256,256]{2,1,0:T(8,128)S(1)}) custom-call(s32[3]{0:T(128)S(1)} %pad_add_fusion.at_ref, f32[2,4]{1,0:T(2,128)S(1)} %copy-done.23, f32[16,16]{1,0:T(8,128)S(1)} %copy-done.17, f32[16,16]{1,0:T(8,128)S(1)} %copy-done.16, ...), custom_call_target="tpu_custom_call" | custom-call | flops 500000000 | bytes 4000000 | tf_op jit(solution)/shard_map/operators/pallas_call | solution.py:232
  49.3 0.8 copy-done.14
  50.2 1.0 copy-done.25
  51.1 1.0 copy-done.27
  52.1 0.8 copy-done.30
  52.9 1.7 copy-done.8
  54.7 26.6 %collective-permute-start.6 = (f32[8,192,512]{2,1,0:T(8,128)}, f32[8,192,512]{2,1,0:T(8,128)S(1)}, u32[]{:S(2)}, u32[]{:S(2)}) collective-permute-start(f32[8,192,512]{2,1,0:T(8,128)} %handed_on.3.refs_2_), channel_id=1, source_target_pairs={{0,8},{8,0},{16,24},{24,16},{1,9},{9,1},{17,25},{25,17},{2,10},{10... | collective-permute-start | bytes 9437192 | tf_op jit(solution)/shard_map/ppermute | solution.py:33
  81.3 2.3 %collective-permute-start.7 = (f32[8,192,512]{2,1,0:T(8,128)}, f32[8,192,512]{2,1,0:T(8,128)}, u32[]{:S(2)}, u32[]{:S(2)}) collective-permute-start(f32[8,192,512]{2,1,0:T(8,128)} %handed_on.2.refs_0_), channel_id=1, source_target_pairs={{8,16},{16,8},{9,17},{17,9},{10,18},{18,10},{11,19},{19,11},{12,20... | collective-permute-start | bytes 9437192 | tf_op jit(solution)/shard_map/ppermute | solution.py:33
  83.6 1.2 copy-done.28
  84.8 8.8 %mode_kinetic.1 = f32[2,4,256,512]{3,2,1,0:T(8,128)S(1)} custom-call(f32[2,4,256,512]{3,2,1,0:T(8,128)} %bitcast.12.in_ref, f32[512,512]{1,0:T(8,128)S(1)} %copy-done.28), custom_call_target="tpu_custom_call" | custom-call | flops 6442450944 | bytes 8388608 | tf_op jit(solution)/shard_map/mode_kinetic/pallas_call | solution.py:356
  93.6 2.0 copy-done.5
  95.6 5.7 %all-to-all-start.1 = ((f32[8,256,512]{2,1,0:T(8,128)}), f32[8,256,512]{2,1,0:T(8,128)}, u32[]{:S(2)}, u32[]{:S(2)}) async-start(f32[8,256,512]{2,1,0:T(8,128)} %bitcast.22), calls=%async_computation.1 | async-start | bytes 8388608 | tf_op jit(solution)/shard_map/all_to_all | solution.py:660
  101.3 0.6 constant_dynamic-slice_fusion.1
  104.6 1.2 collective-permute-start.8
  105.8 1.6 collective-permute-start.9
  107.5 2.2 %copy-done.2 = f32[1,8,8,4,8,512]{5,4,3,2,1,0:T(8,128)S(1)} copy-done((f32[1,8,8,4,8,512]{5,4,3,2,1,0:T(8,128)S(1)}, f32[1,8,8,4,8,512]{5,4,3,2,1,0:T(8,128)}, u32[]{:S(2)}) %copy-start.2) | copy-done | bytes 4194328
  109.7 2.2 %copy-done.24 = f32[1,8,8,4,8,512]{5,4,3,2,1,0:T(8,128)S(1)} copy-done((f32[1,8,8,4,8,512]{5,4,3,2,1,0:T(8,128)S(1)}, f32[1,8,8,4,8,512]{5,4,3,2,1,0:T(8,128)}, u32[]{:S(2)}) %copy-start.24) | copy-done | bytes 4194328
  111.9 1.2 copy-done.26
  113.1 1.0 copy-done.29
  114.1 1.0 copy-done.31
  115.2 18.1 %local_terms.1.work_ref = f32[8,256,512]{2,1,0:T(8,128)S(1)} custom-call(s32[3]{0:T(128)S(1)} %pad_add_fusion.at_ref, f32[4]{0:T(128)S(1)} %copy-done.33, f32[8,8]{1,0:T(8,128)S(1)} %copy-done.32, f32[8,256,512]{2,1,0:T(8,128)S(1)} %bitcast.21, f32[8,256,512]{2,1,0:T(8,128)} %collective-permute-done.refs_1_.refs_0_, f32[8,256,512]{2,1,0:T(8,128)S(1)} %bitcast.26, ...), custom_call_target="tpu_custom_call" | custom-call | flops 12884901888 | bytes 16777216 | tf_op jit(solution)/shard_map/local_terms/pallas_call | solution.py:321
  133.3 2.0 copy-done.6
  135.3 13.0 %all-to-all-done.1.refs_4_ = f32[8,256,512]{2,1,0:T(8,128)} async-done(((f32[8,256,512]{2,1,0:T(8,128)}), f32[8,256,512]{2,1,0:T(8,128)}, u32[]{:S(2)}, u32[]{:S(2)}) %all-to-all-start.1) | async-done | bytes 4194336 | tf_op jit(solution)/shard_map/all_to_all | solution.py:660
  148.3 2.2 %copy-done.7 = f32[8,256,512]{2,1,0:T(8,128)S(1)} copy-done((f32[8,256,512]{2,1,0:T(8,128)S(1)}, f32[8,256,512]{2,1,0:T(8,128)}, u32[]{:S(2)}) %copy-start.7) | copy-done | bytes 4194328
  150.5 1.9 copy-done.9
  152.4 1.0 copy-done.13
  153.4 1.0 copy-done.15
  154.5 15.3 %join_terms.1.work_ref = f32[8,256,512]{2,1,0:T(8,128)S(1)} custom-call(s32[3]{0:T(128)S(1)} %pad_add_fusion.at_ref, f32[8,256,512]{2,1,0:T(8,128)S(1)} %copy-done.7, f32[256,512]{1,0:T(8,128)S(1)} %bitcast.24, f32[2,256,256]{2,1,0:T(8,128)S(1)} %copy-done.15, f32[8,192,512]{2,1,0:T(8,128)} %handed_on.2.refs_0_, ...), custom_call_target="tpu_custom_call" | custom-call | flops 6442450944 | bytes 25165824 | tf_op jit(solution)/shard_map/join_terms/pallas_call | solution.py:400
  169.8 5.9 %far_terms.2 = (f32[8,256,512]{2,1,0:T(8,128)S(1)}, f32[1,8,128]{2,1,0:T(8,128)S(1)}) custom-call(f32[2]{0:T(128)S(1)} %pad_maximum_fusion.coef_ref, f32[8,256,512]{2,1,0:T(8,128)S(1)} %join_terms.1.work_ref, f32[8,192,512]{2,1,0:T(8,128)S(1)} %collective-permute-done.6.first_ref, ...), custom_call_target="tpu_custom_call", output_to_operand_aliasing={{0}: (1, {})} | custom-call | flops 18874368 | bytes 15728640 | tf_op jit(solution)/shard_map/far_terms/pallas_call | solution.py:467
  175.7 15.5 %collective-permute-done.8.first_ref = f32[8,64,512]{2,1,0:T(8,128)} collective-permute-done((f32[8,64,512]{2,1,0:T(8,128)}, f32[8,64,512]{2,1,0:T(8,128)}, u32[]{:S(2)}, u32[]{:S(2)}) %collective-permute-start.8) | collective-permute-done | bytes 1048608 | tf_op jit(solution)/shard_map/ppermute | solution.py:33
  191.2 2.6 %far_terms.3 = (f32[8,256,512]{2,1,0:T(8,128)S(1)}, f32[32,8,128]{2,1,0:T(8,128)S(1)}) custom-call(f32[2]{0:T(128)S(1)} %pad_maximum_fusion.coef_ref, f32[8,256,512]{2,1,0:T(8,128)S(1)} %get-tuple-element.24.work_ref, f32[8,64,512]{2,1,0:T(8,128)} %collective-permute-done.8.first_ref, ...), custom_call_target="tpu_custom_call", output_to_operand_aliasing={{0}: (1, {})} | custom-call | flops 6291456 | bytes 5242880 | tf_op jit(solution)/shard_map/far_terms/pallas_call | solution.py:467
  193.8 12.0 %all_to_all.15.sum_ref = f32[32,8,128]{2,1,0:T(8,128)S(1)} all-to-all(f32[32,8,128]{2,1,0:T(8,128)S(1)} %get-tuple-element.26), channel_id=1, replica_groups=mesh['ka'=4,'mode'=2,'row'=4] {'ka','mode','row'}, dimensions={0} | all-to-all | bytes 262144 | tf_op jit(solution)/shard_map/all_to_all | solution.py:688
  205.8 7.0 %basis.1 = (f32[8,256,512]{2,1,0:T(8,128)}, f32[8,8]{1,0:T(8,128)}, f32[8,8]{1,0:T(8,128)}) custom-call(f32[32,8,128]{2,1,0:T(8,128)S(1)} %all_to_all.15.sum_ref, f32[8,256,512]{2,1,0:T(8,128)S(1)} %get-tuple-element.27.work_ref, f32[8,256,512]{2,1,0:T(8,128)S(1)} %copy-done.4), custom_call_target="tpu_custom_call" | custom-call | flops 33554432 | bytes 12582912 | tf_op jit(solution)/shard_map/basis/pallas_call | solution.py:570
  (61 shorter events, 0.4 us)
Async XLA Ops:
  0.6 13.3 %collective-permute-start = (f32[8,256,512]{2,1,0:T(8,128)}, f32[8,256,512]{2,1,0:T(8,128)}, u32[]{:S(2)}, u32[]{:S(2)}) collective-permute-start(f32[8,256,512]{2,1,0:T(8,128)} %bitcast.16), channel_id=1, source_target_pairs={{0,1},{1,0},{2,3},{3,2},{4,5},{5,4},{6,7},{7,6},{8,9},{9,8},{10,11... | collective-permute-start | bytes 12582920 | tf_op jit(solution)/shard_map/ppermute | solution.py:623
  3.9 49.0 %collective-permute-start.3 = (f32[8,192,512]{2,1,0:T(8,128)}, f32[8,192,512]{2,1,0:T(8,128)S(1)}, u32[]{:S(2)}, u32[]{:S(2)}) collective-permute-start(f32[8,192,512]{2,1,0:T(8,128)} %split_rows.2), channel_id=1, source_target_pairs={{8,16},{16,8},{9,17},{17,9},{10,18},{18,10},{11,19},{19,11},{12,20... | collective-permute-start | bytes 9437192 | tf_op jit(solution)/shard_map/ppermute | solution.py:33
  4.8 76.5 %collective-permute-start.1 = (f32[8,192,512]{2,1,0:T(8,128)}, f32[8,192,512]{2,1,0:T(8,128)}, u32[]{:S(2)}, u32[]{:S(2)}) collective-permute-start(f32[8,192,512]{2,1,0:T(8,128)} %split_rows.2), channel_id=1, source_target_pairs={{0,8},{8,0},{16,24},{24,16},{1,9},{9,1},{17,25},{25,17},{2,10},{10... | collective-permute-start | bytes 9437192 | tf_op jit(solution)/shard_map/ppermute | solution.py:33
  12.2 93.7 %collective-permute-start.2 = (f32[8,64,512]{2,1,0:T(8,128)}, f32[8,64,512]{2,1,0:T(8,128)}, u32[]{:S(2)}, u32[]{:S(2)}) collective-permute-start(f32[8,64,512]{2,1,0:T(8,128)} %split_rows.3), channel_id=1, source_target_pairs={{0,8},{8,0},{16,24},{24,16},{1,9},{9,1},{17,25},{25,17},{2,10},{10... | collective-permute-start | bytes 3145736 | tf_op jit(solution)/shard_map/ppermute | solution.py:33
  12.2 92.4 %collective-permute-start.4 = (f32[8,64,512]{2,1,0:T(8,128)}, f32[8,64,512]{2,1,0:T(8,128)}, u32[]{:S(2)}, u32[]{:S(2)}) collective-permute-start(f32[8,64,512]{2,1,0:T(8,128)} %split_rows.3), channel_id=1, source_target_pairs={{8,16},{16,8},{9,17},{17,9},{10,18},{18,10},{11,19},{19,11},{12,20... | collective-permute-start | bytes 3145736 | tf_op jit(solution)/shard_map/ppermute | solution.py:33
  14.0 2.2 %copy-start = (f32[1,8,8,4,8,512]{5,4,3,2,1,0:T(8,128)S(1)}, f32[1,8,8,4,8,512]{5,4,3,2,1,0:T(8,128)}, u32[]{:S(2)}) copy-start(f32[1,8,8,4,8,512]{5,4,3,2,1,0:T(8,128)} %param.15) | copy-start | bytes 12582916
  16.2 1.0 copy-start.12
  19.8 2.0 copy-start.3
  21.8 0.8 copy-start.10
  22.6 5.7 %copy-start.16 = (f32[16,16]{1,0:T(8,128)S(1)}, f32[16,16]{1,0:T(8,128)}, u32[]{:S(2)}) copy-start(f32[16,16]{1,0:T(8,128)} %two_ref.3) | copy-start | bytes 3076
  22.6 61.0 %all-to-all-start = ((f32[8,256,512]{2,1,0:T(8,128)}), f32[8,256,512]{2,1,0:T(8,128)}, u32[]{:S(2)}, u32[]{:S(2)}) async-start(f32[8,256,512]{2,1,0:T(8,128)} %copy-done.3), calls=%async_computation | async-start | bytes 8388608 | tf_op jit(solution)/shard_map/all_to_all | solution.py:658
  28.3 2.2 %copy-start.1 = (f32[1,8,8,4,8,512]{5,4,3,2,1,0:T(8,128)S(1)}, f32[1,8,8,4,8,512]{5,4,3,2,1,0:T(8,128)}, u32[]{:S(2)}) copy-start(f32[1,8,8,4,8,512]{5,4,3,2,1,0:T(8,128)} %param.15) | copy-start | bytes 12582916
  30.5 9.2 %copy-start.17 = (f32[16,16]{1,0:T(8,128)S(1)}, f32[16,16]{1,0:T(8,128)}, u32[]{:S(2)}) copy-start(f32[16,16]{1,0:T(8,128)} %one_ref.1) | copy-start | bytes 3076
  30.5 9.2 %copy-start.18 = (f32[8,8]{1,0:T(8,128)S(1)}, f32[8,8]{1,0:T(8,128)}, u32[]{:S(2)}) copy-start(f32[8,8]{1,0:T(8,128)} %three_ref.1) | copy-start | bytes 772
  30.5 9.2 %copy-start.19 = (f32[8,8]{1,0:T(8,128)S(1)}, f32[8,8]{1,0:T(8,128)}, u32[]{:S(2)}) copy-start(f32[8,8]{1,0:T(8,128)} %four_ref.1) | copy-start | bytes 772
  30.5 9.2 %copy-start.20 = (f32[8,8]{1,0:T(8,128)S(1)}, f32[8,8]{1,0:T(8,128)}, u32[]{:S(2)}) copy-start(f32[8,8]{1,0:T(8,128)} %five_ref.1) | copy-start | bytes 772
  30.5 9.2 %copy-start.21 = (f32[8,8]{1,0:T(8,128)S(1)}, f32[8,8]{1,0:T(8,128)}, u32[]{:S(2)}) copy-start(f32[8,8]{1,0:T(8,128)} %six_ref.1) | copy-start | bytes 772
  30.5 9.2 %copy-start.22 = (f32[8,8]{1,0:T(8,128)S(1)}, f32[8,8]{1,0:T(8,128)}, u32[]{:S(2)}) copy-start(f32[8,8]{1,0:T(8,128)} %der_ref.1) | copy-start | bytes 772
  30.5 9.1 %copy-start.23 = (f32[2,4]{1,0:T(2,128)S(1)}, f32[2,4]{1,0:T(2,128)}, u32[]{:S(2)}) copy-start(f32[2,4]{1,0:T(2,128)} %coupling_ref.1) | copy-start | bytes 100
  38.1 110.1 %collective-permute-start.5 = (f32[8,256,512]{2,1,0:T(8,128)}, f32[8,256,512]{2,1,0:T(8,128)}, u32[]{:S(2)}, u32[]{:S(2)}) collective-permute-start(f32[8,256,512]{2,1,0:T(8,128)} %crossing.1.refs_0_.__1_), channel_id=1, source_target_pairs={{0,2},{1,3},{2,0},{3,1},{4,6},{5,7},{6,4},{7,5},{8,10},{9,11},{10,... | collective-permute-start | bytes 12582920 | tf_op jit(solution)/shard_map/ppermute | solution.py:627
  49.3 0.8 copy-start.14
  50.2 1.0 copy-start.25
  51.1 1.0 copy-start.27
  52.1 0.8 copy-start.30
  52.9 1.8 copy-start.8
  54.7 115.1 %collective-permute-start.6 = (f32[8,192,512]{2,1,0:T(8,128)}, f32[8,192,512]{2,1,0:T(8,128)S(1)}, u32[]{:S(2)}, u32[]{:S(2)}) collective-permute-start(f32[8,192,512]{2,1,0:T(8,128)} %handed_on.3.refs_2_), channel_id=1, source_target_pairs={{0,8},{8,0},{16,24},{24,16},{1,9},{9,1},{17,25},{25,17},{2,10},{10... | collective-permute-start | bytes 9437192 | tf_op jit(solution)/shard_map/ppermute | solution.py:33
  81.3 88.5 %collective-permute-start.7 = (f32[8,192,512]{2,1,0:T(8,128)}, f32[8,192,512]{2,1,0:T(8,128)}, u32[]{:S(2)}, u32[]{:S(2)}) collective-permute-start(f32[8,192,512]{2,1,0:T(8,128)} %handed_on.2.refs_0_), channel_id=1, source_target_pairs={{8,16},{16,8},{9,17},{17,9},{10,18},{18,10},{11,19},{19,11},{12,20... | collective-permute-start | bytes 9437192 | tf_op jit(solution)/shard_map/ppermute | solution.py:33
  83.6 1.2 copy-start.28
  93.6 2.0 copy-start.5
  95.6 11.9 %copy-start.32 = (f32[8,8]{1,0:T(8,128)S(1)}, f32[8,8]{1,0:T(8,128)}, u32[]{:S(2)}) copy-start(f32[8,8]{1,0:T(8,128)} %beta_ref.1) | copy-start | bytes 772
  95.6 11.9 %copy-start.33 = (f32[4]{0:T(128)S(1)}, f32[4]{0:T(128)}, u32[]{:S(2)}) copy-start(f32[4]{0:T(128)} %rot_ref.1) | copy-start | bytes 52
  95.6 52.7 %all-to-all-start.1 = ((f32[8,256,512]{2,1,0:T(8,128)}), f32[8,256,512]{2,1,0:T(8,128)}, u32[]{:S(2)}, u32[]{:S(2)}) async-start(f32[8,256,512]{2,1,0:T(8,128)} %bitcast.22), calls=%async_computation.1 | async-start | bytes 8388608 | tf_op jit(solution)/shard_map/all_to_all | solution.py:660
  104.6 86.6 %collective-permute-start.8 = (f32[8,64,512]{2,1,0:T(8,128)}, f32[8,64,512]{2,1,0:T(8,128)}, u32[]{:S(2)}, u32[]{:S(2)}) collective-permute-start(f32[8,64,512]{2,1,0:T(8,128)} %collective-permute-done.4.refs_3_), channel_id=1, source_target_pairs={{0,8},{8,0},{16,24},{24,16},{1,9},{9,1},{17,25},{25,17},{2,10},{10... | collective-permute-start | bytes 3145736 | tf_op jit(solution)/shard_map/ppermute | solution.py:33
  105.8 85.4 %collective-permute-start.9 = (f32[8,64,512]{2,1,0:T(8,128)}, f32[8,64,512]{2,1,0:T(8,128)}, u32[]{:S(2)}, u32[]{:S(2)}) collective-permute-start(f32[8,64,512]{2,1,0:T(8,128)} %collective-permute-done.2.refs_1_), channel_id=1, source_target_pairs={{8,16},{16,8},{9,17},{17,9},{10,18},{18,10},{11,19},{19,11},{12,20... | collective-permute-start | bytes 3145736 | tf_op jit(solution)/shard_map/ppermute | solution.py:33
  107.5 2.2 %copy-start.2 = (f32[1,8,8,4,8,512]{5,4,3,2,1,0:T(8,128)S(1)}, f32[1,8,8,4,8,512]{5,4,3,2,1,0:T(8,128)}, u32[]{:S(2)}) copy-start(f32[1,8,8,4,8,512]{5,4,3,2,1,0:T(8,128)} %param.15) | copy-start | bytes 12582916
  109.7 2.2 %copy-start.24 = (f32[1,8,8,4,8,512]{5,4,3,2,1,0:T(8,128)S(1)}, f32[1,8,8,4,8,512]{5,4,3,2,1,0:T(8,128)}, u32[]{:S(2)}) copy-start(f32[1,8,8,4,8,512]{5,4,3,2,1,0:T(8,128)} %param.16) | copy-start | bytes 12582916
  111.9 1.2 copy-start.26
  113.1 1.0 copy-start.29
  114.1 1.0 copy-start.31
  133.3 2.0 copy-start.6
  148.3 2.2 %copy-start.7 = (f32[8,256,512]{2,1,0:T(8,128)S(1)}, f32[8,256,512]{2,1,0:T(8,128)}, u32[]{:S(2)}) copy-start(f32[8,256,512]{2,1,0:T(8,128)} %copy-done.6) | copy-start | bytes 12582916
  150.5 1.9 copy-start.9
  152.4 1.0 copy-start.13
  153.4 1.0 copy-start.15
  154.5 15.4 %copy-start.4 = (f32[8,256,512]{2,1,0:T(8,128)S(1)}, f32[8,256,512]{2,1,0:T(8,128)}, u32[]{:S(2)}) copy-start(f32[8,256,512]{2,1,0:T(8,128)} %copy-done.3) | copy-start | bytes 12582916
  154.5 15.4 %copy-start.11 = (f32[256,512]{1,0:T(8,128)S(1)}, f32[256,512]{1,0:T(8,128)}, u32[]{:S(2)}) copy-start(f32[256,512]{1,0:T(8,128)} %copy-done.10) | copy-start | bytes 1572868
where the time goes:
time: 214 us; the launch traced here: 213 us
  Pallas kernels  82.5 us (39%)
  starting transfers between devices  53 us (25%)
  local copies, waits for them, and re-layouts  33.2 us (16%)
  waiting for transfers between devices  28.5 us (13%)
  blocking collectives  12 us (6%)
  between operations  3.5 us (2%)
    ppermute x8, starting transfers between devices, pair_exchange(): return lax.ppermute(value, axis, pairs)  39.6 us
    unnamed x68, local copies, waits for them, and re-layouts  32.6 us
    pallas_call x1, Pallas kernels, local_terms(): pl.pallas_call(functools.partial(local_kernel, nvec, nblocks, len(held)),...  18.1 us
    ppermute x8, waiting for transfers between devices, pair_exchange(): return lax.ppermute(value, axis, pairs)  15.5 us
    pallas_call x1, Pallas kernels, join_terms(): pl.pallas_call(functools.partial(join_kernel, tuple(starts), len(sums)),...  15.3 us
    all_to_all x1, waiting for transfers between devices, shards(): lax.all_to_all(mode_shares, 'mode', split_axis=0, concat_axis=0, tiled=True)  13 us
    all_to_all x1, blocking collectives, shards(): lax.all_to_all(copied, ALL_AXES, split_axis=0, concat_axis=0, tiled=True)  12 us
    pallas_call x1, Pallas kernels, operators(): pl.pallas_call(functools.partial(operators_kernel, points, group), in_spe...  9.65 us
  transfers between devices with their start and end apart: 12, of which 2 were waited for; matrix products, arithmetic and copies ran while one was open for 0% of the time, Pallas kernels for 34%

commit v1 on v0

--- a/solution.py
+++ b/solution.py
@@ -114,14 +114,19 @@
     )(vec, skip_fn, *after)
 
 
-def split_kernel(start, vec_ref, out_ref, held, sems):
+def split_kernel(start, parts, vec_ref, out_ref, held, sems):
     count, rows, _ = out_ref.shape
+    size = rows // parts
+    spots = [(i, p, pl.ds(p * size, size)) for i in range(count) for p in range(parts)]
     loads = [
-        pltpu.make_async_copy(vec_ref.at[i, pl.ds(start, rows)], held.at[i], sems.at[0, i])
-        for i in range(count)
+        pltpu.make_async_copy(
+            vec_ref.at[i, pl.ds(start + p * size, size)], held.at[i, place], sems.at[0, i, p]
+        )
+        for i, p, place in spots
     ]
     stores = [
-        pltpu.make_async_copy(held.at[i], out_ref.at[i], sems.at[1, i]) for i in range(count)
+        pltpu.make_async_copy(held.at[i, place], out_ref.at[i, place], sems.at[1, i, p])
+        for i, p, place in spots
     ]
     for load in loads:
         load.start()
@@ -135,14 +140,15 @@
 def split_rows(vec, start, stop):
     nvec, _, width = vec.shape
     shape = (nvec, stop - start, width)
-    return pl.pallas_call(
-        functools.partial(split_kernel, start),
+    parts = next(p for p in (4, 2, 1) if shape[1] % (SUBLANES * p) == 0)
+    return pl.pallas_call(
+        functools.partial(split_kernel, start, parts),
         in_specs=[pl.BlockSpec(memory_space=pl.ANY)],
         out_specs=pl.BlockSpec(memory_space=pl.ANY),
         out_shape=jax.ShapeDtypeStruct(shape, jnp.float32),
         scratch_shapes=[
             pltpu.VMEM(shape, jnp.float32),
-            pltpu.SemaphoreType.DMA((2, nvec)),
+            pltpu.SemaphoreType.DMA((2, nvec, parts)),
         ],
         compiler_params=pltpu.CompilerParams(vmem_limit_bytes=FULL_VMEM_BYTES),
         cost_estimate=pl.CostEstimate(
@@ -487,38 +493,68 @@
     )(coef, work, first, second, skip_fn, vec, before)
 
 
-def small_dot(left, right):
-    terms = [left[:, k : k + 1] * right[k : k + 1, :] for k in range(right.shape[0])]
-    while len(terms) > 1:
-        terms = [sum(terms[k + 1 : k + 2], terms[k]) for k in range(0, len(terms), 2)]
-    return terms[0]
+def across(column, row):
+    return jnp.broadcast_to(column[row : row + 1, :], (SUBLANES, LANES))
+
+
+def spread_columns(matrix, start, count):
+    return [
+        jnp.broadcast_to(matrix[:, k : k + 1], (count, LANES)) for k in range(start, start + count)
+    ]
+
+
+def spread_dot(left, right):
+    count = len(left)
+    columns = []
+    for column in right:
+        terms = [left[m] * jnp.broadcast_to(column[m : m + 1, :], left[m].shape) for m in range(count)]
+        while len(terms) > 1:
+            terms = [sum(terms[k + 1 : k + 2], terms[k]) for k in range(0, len(terms), 2)]
+        columns.append(terms[0])
+    return columns
 
 
 def small_algebra(nvec, count, packed):
     packed = packed * (1.0 / count)
-    cross = packed.T[0:nvec, :]
-    cross_turned = packed[:, 0:nvec]
-    work_gram = packed[:, nvec : 2 * nvec]
-    vec_gram = packed[:, 2 * nvec : 3 * nvec]
-    total = 2.0 * cross - small_dot(vec_gram, cross)
-    total_turned = 2.0 * cross_turned - small_dot(cross_turned, vec_gram)
-    gram = work_gram - small_dot(total_turned, cross) - small_dot(cross_turned, total)
-    gram = gram + small_dot(total_turned, small_dot(vec_gram, total))
-    row = lax.broadcasted_iota(jnp.int32, (nvec, nvec), 0)
-    column = lax.broadcasted_iota(jnp.int32, (nvec, nvec), 1)
-    inverse = jnp.where(row == column, 1.0, 0.0)
-    lower = jnp.zeros((nvec, nvec), jnp.float32)
+    cross = spread_columns(packed.T[0:nvec, :], 0, nvec)
+    cross_turned = spread_columns(packed, 0, nvec)
+    gram = spread_columns(packed, nvec, nvec)
+    vec_gram = spread_columns(packed, 2 * nvec, nvec)
+    total = [2.0 * c - d for c, d in zip(cross, spread_dot(vec_gram, cross))]
+    total_turned = [2.0 * c - d for c, d in zip(cross_turned, spread_dot(cross_turned, vec_gram))]
+    inner = [d - c for c, d in zip(cross, spread_dot(vec_gram, total))]
+    gram = [
+        g - one + other
+        for g, one, other in zip(
+            gram, spread_dot(cross_turned, total), spread_dot(total_turned, inner)
+        )
+    ]
+    row = lax.broadcasted_iota(jnp.int32, (nvec, LANES), 0)
+    inverse = [jnp.where(row == k, 1.0, 0.0) for k in range(nvec)]
+    lower = []
     for at in range(nvec):
-        pivot = gram[at : at + 1, at : at + 1]
+        pivot = jnp.broadcast_to(gram[at][at : at + 1, :], (nvec, LANES))
         scale = lax.rsqrt(pivot)
         scale = scale * (1.5 - 0.5 * pivot * scale * scale)
-        scaled = gram[:, at : at + 1] * scale
-        lower = jnp.where((column == at) & (row >= at), scaled, lower)
-        pivot_row = inverse[at : at + 1, :] * scale
+        scaled = gram[at] * scale
+        lower.append(jnp.where(row >= at, scaled, 0.0))
         factor = jnp.where(row > at, scaled, 0.0)
-        inverse = jnp.where(row == at, pivot_row, inverse - factor * pivot_row)
-        gram = gram - factor * (gram[at : at + 1, :] * scale)
-    return total, lower, inverse, -small_dot(inverse, total_turned)
+        for k in range(at + 1, nvec):
+            here = jnp.broadcast_to(gram[k][at : at + 1, :], (nvec, LANES)) * scale
+            gram[k] = gram[k] - factor * here
+        for k in range(at + 1):
+            here = jnp.broadcast_to(inverse[k][at : at + 1, :], (nvec, LANES)) * scale
+            inverse[k] = jnp.where(row == at, here, inverse[k] - factor * here)
+    mixing = [-column for column in spread_dot(inverse, total_turned)]
+    return total, lower, inverse, mixing
+
+
+def gathered_columns(columns):
+    lane = lax.broadcasted_iota(jnp.int32, columns[0].shape, 1)
+    matrix = jnp.zeros_like(columns[0])
+    for k, column in enumerate(columns):
+        matrix = jnp.where(lane == k, column, matrix)
+    return matrix[:, : len(columns)]
 
 
 def basis_kernel(nvec, count, sum_ref, work_ref, vec_ref, out_ref, alpha_ref, lower_ref, coefs):
@@ -528,37 +564,33 @@
         for other in range(1, sum_ref.shape[0]):
             packed = packed + sum_ref[other]
         total, lower, inverse, mixing = small_algebra(nvec, count, packed)
-        alpha_ref[...] = total
-        lower_ref[...] = lower
-        for number, matrix in enumerate((inverse, mixing)):
-            for i in range(nvec):
-                for j in range(nvec):
-                    coefs[number, i * nvec + j] = jnp.broadcast_to(
-                        matrix[i : i + 1, j : j + 1], (SUBLANES, LANES)
-                    )
+        for number, columns in enumerate((inverse, mixing)):
+            for j in range(nvec):
+                for i in range(nvec):
+                    if number == 1 or j <= i:
+                        coefs[number, i * nvec + j] = across(columns[j], i)
+        alpha_ref[...] = gathered_columns(total)
+        lower_ref[...] = gathered_columns(lower)
 
     start = pl.multiple_of(pl.program_id(0) * out_ref.shape[1], out_ref.shape[1])
     places = tiles(*out_ref.shape[1:])
     for at in range(0, len(places), 4):
         group = places[at : at + 4]
         held = [(pl.ds(start + place.start, SUBLANES), lanes) for place, lanes in group]
-        for ours in vector_groups(nvec):
-            totals = {}
-            for number, ref in ((1, vec_ref), (0, work_ref)):
-                for j in range(nvec):
-                    outs = [i for i in ours if number == 1 or j <= i]
-                    if not outs:
+        totals = {}
+        for number, ref in ((1, vec_ref), (0, work_ref)):
+            for j in range(nvec):
+                values = [ref[(j, *place)] for place in held]
+                for i in range(nvec):
+                    if number == 0 and j > i:
                         continue
-                    values = [ref[(j, *place)] for place in held]
-                    for i in outs:
-                        coef = coefs[number, i * nvec + j]
-                        for spot, value in enumerate(values):
-                            term = coef * value
-                            here = (i, spot)
-                            totals[here] = totals[here] + term if here in totals else term
-            for i in ours:
-                for spot, place in enumerate(group):
-                    out_ref[(i, *place)] = totals[i, spot]
+                    coef = coefs[number, i * nvec + j]
+                    for spot, value in enumerate(values):
+                        term = coef * value
+                        here = (i, spot)
+                        totals[here] = totals[here] + term if here in totals else term
+        for (i, spot), value in totals.items():
+            out_ref[(i, *group[spot])] = value
 
 
 def basis_of(count, sums, work, vec, block_rows):

time: 214 us -> 214 us (level)
  transfers between devices with their start and end apart: 12 -> 12, of which waited for: 2 -> 2; matrix products, arithmetic and copies ran while one was open for 0% -> 0% of each run, Pallas kernels for 34% -> 35%
where the time goes in v1:
time: 214 us; the launch traced here: 213 us
  Pallas kernels  82.8 us (39%)
  starting transfers between devices  52.7 us (25%)
  local copies, waits for them, and re-layouts  33.2 us (16%)
  waiting for transfers between devices  28.5 us (13%)
  blocking collectives  12 us (6%)
  between operations  3.5 us (2%)
    ppermute x8, starting transfers between devices, pair_exchange(): return lax.ppermute(value, axis, pairs)  39.3 us
    unnamed x68, local copies, waits for them, and re-layouts  32.6 us
    pallas_call x1, Pallas kernels, local_terms(): pl.pallas_call(functools.partial(local_kernel, nvec, nblocks, len(held)),...  18.1 us
    ppermute x8, waiting for transfers between devices, pair_exchange(): return lax.ppermute(value, axis, pairs)  15.5 us
    pallas_call x1, Pallas kernels, join_terms(): pl.pallas_call(functools.partial(join_kernel, tuple(starts), len(sums)),...  15.3 us
    all_to_all x1, waiting for transfers between devices, shards(): lax.all_to_all(mode_shares, 'mode', split_axis=0, concat_axis=0, tiled=True)  13 us
    all_to_all x1, blocking collectives, shards(): lax.all_to_all(copied, ALL_AXES, split_axis=0, concat_axis=0, tiled=True)  12 us
    pallas_call x1, Pallas kernels, operators(): pl.pallas_call(functools.partial(operators_kernel, points, group), in_spe...  9.65 us
  transfers between devices with their start and end apart: 12, of which 2 were waited for; matrix products, arithmetic and copies ran while one was open for 0% of the time, Pallas kernels for 35%

profile of v1, /device:TPU:0, one launch (start us, length us, event | category | flops | bytes accessed | tf_op | source)
XLA Modules:
  0.0 212.9 jit_solution(8070392139650229652)
XLA Ops:
  0.6 0.5 collective-permute-start
  1.1 3.5 %split_rows.2 = f32[8,192,512]{2,1,0:T(8,128)} custom-call(f32[8,256,512]{2,1,0:T(8,128)} %bitcast.17), custom_call_target="tpu_custom_call" | custom-call | bytes 6291456 | tf_op jit(solution)/shard_map/split_rows/pallas_call | solution.py:144
  4.7 0.9 collective-permute-start.3
  5.5 5.3 %collective-permute-start.1 = (f32[8,192,512]{2,1,0:T(8,128)}, f32[8,192,512]{2,1,0:T(8,128)}, u32[]{:S(2)}, u32[]{:S(2)}) collective-permute-start(f32[8,192,512]{2,1,0:T(8,128)} %split_rows.2), channel_id=1, source_target_pairs={{0,8},{8,0},{16,24},{24,16},{1,9},{9,1},{17,25},{25,17},{2,10},{10... | collective-permute-start | bytes 9437192 | tf_op jit(solution)/shard_map/ppermute | solution.py:33
  10.8 2.4 %split_rows.3 = f32[8,64,512]{2,1,0:T(8,128)} custom-call(f32[8,256,512]{2,1,0:T(8,128)} %bitcast.18), custom_call_target="tpu_custom_call" | custom-call | bytes 2097152 | tf_op jit(solution)/shard_map/split_rows/pallas_call | solution.py:144
  13.3 1.6 collective-permute-start.4
  15.0 2.2 %copy-done = f32[1,8,8,4,8,512]{5,4,3,2,1,0:T(8,128)S(1)} copy-done((f32[1,8,8,4,8,512]{5,4,3,2,1,0:T(8,128)S(1)}, f32[1,8,8,4,8,512]{5,4,3,2,1,0:T(8,128)}, u32[]{:S(2)}) %copy-start) | copy-done | bytes 4194328
  17.2 1.0 copy-done.12
  18.2 2.6 %resident.1 = (f32[8,128]{1,0:T(8,128)S(1)}, f32[8,256,512]{2,1,0:T(8,128)S(1)}, f32[256,512]{1,0:T(8,128)S(1)}) custom-call(f32[8,256,512]{2,1,0:T(8,128)S(1)} %bitcast.19, f32[256,512]{1,0:T(8,128)S(1)} %bitcast.23, f32[8,256,512]{2,1,0:T(8,128)} %collective-permute-done.refs_1_.refs_0_), custom_call_target="tpu_custom_call" | custom-call | flops 9437184 | bytes 8388608 | tf_op jit(solution)/shard_map/resident/pallas_call | solution.py:98
  20.8 2.0 copy-done.3
  22.8 0.8 copy-done.10
  23.6 5.7 %all-to-all-start = ((f32[8,256,512]{2,1,0:T(8,128)}), f32[8,256,512]{2,1,0:T(8,128)}, u32[]{:S(2)}, u32[]{:S(2)}) async-start(f32[8,256,512]{2,1,0:T(8,128)} %copy-done.3), calls=%async_computation | async-start | bytes 8388608 | tf_op jit(solution)/shard_map/all_to_all | solution.py:690
  29.3 2.2 %copy-done.1 = f32[1,8,8,4,8,512]{5,4,3,2,1,0:T(8,128)S(1)} copy-done((f32[1,8,8,4,8,512]{5,4,3,2,1,0:T(8,128)S(1)}, f32[1,8,8,4,8,512]{5,4,3,2,1,0:T(8,128)}, u32[]{:S(2)}) %copy-start.1) | copy-done | bytes 4194328
  31.6 7.6 %crossing.1.refs_0_.__1_ = f32[8,256,512]{2,1,0:T(8,128)} custom-call(s32[3]{0:T(128)S(1)} %pad_add_fusion.at_ref, f32[16,16]{1,0:T(8,128)S(1)} %copy-done.16, f32[8,256,512]{2,1,0:T(8,128)S(1)} %bitcast.20, f32[8,256,512]{2,1,0:T(8,128)} %collective-permute-done.refs_1_.refs_0_), custom_call_target="tpu_custom_call" | custom-call | flops 16777216 | bytes 12582912 | tf_op jit(solution)/shard_map/crossing/pallas_call | solution.py:291
  39.2 1.5 collective-permute-start.5
  40.7 9.7 %operators.1 = (f32[2,256,256]{2,1,0:T(8,128)S(1)}, f32[512,512]{1,0:T(8,128)S(1)}, f32[512,512]{1,0:T(8,128)S(1)}, f32[2,256,256]{2,1,0:T(8,128)S(1)}) custom-call(s32[3]{0:T(128)S(1)} %pad_add_fusion.at_ref, f32[2,4]{1,0:T(2,128)S(1)} %copy-done.23, f32[16,16]{1,0:T(8,128)S(1)} %copy-done.17, f32[16,16]{1,0:T(8,128)S(1)} %copy-done.16, ...), custom_call_target="tpu_custom_call" | custom-call | flops 500000000 | bytes 4000000 | tf_op jit(solution)/shard_map/operators/pallas_call | solution.py:238
  50.4 0.8 copy-done.14
  51.2 1.0 copy-done.25
  52.2 1.0 copy-done.27
  53.1 0.8 copy-done.30
  53.9 1.7 copy-done.8
  55.7 26.3 %collective-permute-start.6 = (f32[8,192,512]{2,1,0:T(8,128)}, f32[8,192,512]{2,1,0:T(8,128)S(1)}, u32[]{:S(2)}, u32[]{:S(2)}) collective-permute-start(f32[8,192,512]{2,1,0:T(8,128)} %handed_on.3.refs_2_), channel_id=1, source_target_pairs={{0,8},{8,0},{16,24},{24,16},{1,9},{9,1},{17,25},{25,17},{2,10},{10... | collective-permute-start | bytes 9437192 | tf_op jit(solution)/shard_map/ppermute | solution.py:33
  82.0 2.3 %collective-permute-start.7 = (f32[8,192,512]{2,1,0:T(8,128)}, f32[8,192,512]{2,1,0:T(8,128)}, u32[]{:S(2)}, u32[]{:S(2)}) collective-permute-start(f32[8,192,512]{2,1,0:T(8,128)} %handed_on.2.refs_0_), channel_id=1, source_target_pairs={{8,16},{16,8},{9,17},{17,9},{10,18},{18,10},{11,19},{19,11},{12,20... | collective-permute-start | bytes 9437192 | tf_op jit(solution)/shard_map/ppermute | solution.py:33
  84.3 1.2 copy-done.28
  85.5 8.8 %mode_kinetic.1 = f32[2,4,256,512]{3,2,1,0:T(8,128)S(1)} custom-call(f32[2,4,256,512]{3,2,1,0:T(8,128)} %bitcast.12.in_ref, f32[512,512]{1,0:T(8,128)S(1)} %copy-done.28), custom_call_target="tpu_custom_call" | custom-call | flops 6442450944 | bytes 8388608 | tf_op jit(solution)/shard_map/mode_kinetic/pallas_call | solution.py:362
  94.4 2.0 copy-done.5
  96.4 5.7 %all-to-all-start.1 = ((f32[8,256,512]{2,1,0:T(8,128)}), f32[8,256,512]{2,1,0:T(8,128)}, u32[]{:S(2)}, u32[]{:S(2)}) async-start(f32[8,256,512]{2,1,0:T(8,128)} %bitcast.22), calls=%async_computation.1 | async-start | bytes 8388608 | tf_op jit(solution)/shard_map/all_to_all | solution.py:692
  102.1 0.6 constant_dynamic-slice_fusion.1
  105.3 1.2 collective-permute-start.8
  106.6 1.6 collective-permute-start.9
  108.2 2.2 %copy-done.2 = f32[1,8,8,4,8,512]{5,4,3,2,1,0:T(8,128)S(1)} copy-done((f32[1,8,8,4,8,512]{5,4,3,2,1,0:T(8,128)S(1)}, f32[1,8,8,4,8,512]{5,4,3,2,1,0:T(8,128)}, u32[]{:S(2)}) %copy-start.2) | copy-done | bytes 4194328
  110.4 2.2 %copy-done.24 = f32[1,8,8,4,8,512]{5,4,3,2,1,0:T(8,128)S(1)} copy-done((f32[1,8,8,4,8,512]{5,4,3,2,1,0:T(8,128)S(1)}, f32[1,8,8,4,8,512]{5,4,3,2,1,0:T(8,128)}, u32[]{:S(2)}) %copy-start.24) | copy-done | bytes 4194328
  112.6 1.2 copy-done.26
  113.8 1.0 copy-done.29
  114.9 1.0 copy-done.31
  115.9 18.1 %local_terms.1.work_ref = f32[8,256,512]{2,1,0:T(8,128)S(1)} custom-call(s32[3]{0:T(128)S(1)} %pad_add_fusion.at_ref, f32[4]{0:T(128)S(1)} %copy-done.33, f32[8,8]{1,0:T(8,128)S(1)} %copy-done.32, f32[8,256,512]{2,1,0:T(8,128)S(1)} %bitcast.21, f32[8,256,512]{2,1,0:T(8,128)} %collective-permute-done.refs_1_.refs_0_, f32[8,256,512]{2,1,0:T(8,128)S(1)} %bitcast.26, ...), custom_call_target="tpu_custom_call" | custom-call | flops 12884901888 | bytes 16777216 | tf_op jit(solution)/shard_map/local_terms/pallas_call | solution.py:327
  134.0 2.0 copy-done.6
  136.0 13.0 %all-to-all-done.1.refs_4_ = f32[8,256,512]{2,1,0:T(8,128)} async-done(((f32[8,256,512]{2,1,0:T(8,128)}), f32[8,256,512]{2,1,0:T(8,128)}, u32[]{:S(2)}, u32[]{:S(2)}) %all-to-all-start.1) | async-done | bytes 4194336 | tf_op jit(solution)/shard_map/all_to_all | solution.py:692
  149.0 2.2 %copy-done.7 = f32[8,256,512]{2,1,0:T(8,128)S(1)} copy-done((f32[8,256,512]{2,1,0:T(8,128)S(1)}, f32[8,256,512]{2,1,0:T(8,128)}, u32[]{:S(2)}) %copy-start.7) | copy-done | bytes 4194328
  151.2 1.9 copy-done.9
  153.1 1.0 copy-done.13
  154.2 1.0 copy-done.15
  155.2 15.3 %join_terms.1.work_ref = f32[8,256,512]{2,1,0:T(8,128)S(1)} custom-call(s32[3]{0:T(128)S(1)} %pad_add_fusion.at_ref, f32[8,256,512]{2,1,0:T(8,128)S(1)} %copy-done.7, f32[256,512]{1,0:T(8,128)S(1)} %bitcast.24, f32[2,256,256]{2,1,0:T(8,128)S(1)} %copy-done.15, f32[8,192,512]{2,1,0:T(8,128)} %handed_on.2.refs_0_, ...), custom_call_target="tpu_custom_call" | custom-call | flops 6442450944 | bytes 25165824 | tf_op jit(solution)/shard_map/join_terms/pallas_call | solution.py:406
  170.6 5.9 %far_terms.2 = (f32[8,256,512]{2,1,0:T(8,128)S(1)}, f32[1,8,128]{2,1,0:T(8,128)S(1)}) custom-call(f32[2]{0:T(128)S(1)} %pad_maximum_fusion.coef_ref, f32[8,256,512]{2,1,0:T(8,128)S(1)} %join_terms.1.work_ref, f32[8,192,512]{2,1,0:T(8,128)S(1)} %collective-permute-done.6.first_ref, ...), custom_call_target="tpu_custom_call", output_to_operand_aliasing={{0}: (1, {})} | custom-call | flops 18874368 | bytes 15728640 | tf_op jit(solution)/shard_map/far_terms/pallas_call | solution.py:473
  176.5 15.5 %collective-permute-done.8.first_ref = f32[8,64,512]{2,1,0:T(8,128)} collective-permute-done((f32[8,64,512]{2,1,0:T(8,128)}, f32[8,64,512]{2,1,0:T(8,128)}, u32[]{:S(2)}, u32[]{:S(2)}) %collective-permute-start.8) | collective-permute-done | bytes 1048608 | tf_op jit(solution)/shard_map/ppermute | solution.py:33
  192.0 2.6 %far_terms.3 = (f32[8,256,512]{2,1,0:T(8,128)S(1)}, f32[32,8,128]{2,1,0:T(8,128)S(1)}) custom-call(f32[2]{0:T(128)S(1)} %pad_maximum_fusion.coef_ref, f32[8,256,512]{2,1,0:T(8,128)S(1)} %get-tuple-element.24.work_ref, f32[8,64,512]{2,1,0:T(8,128)} %collective-permute-done.8.first_ref, ...), custom_call_target="tpu_custom_call", output_to_operand_aliasing={{0}: (1, {})} | custom-call | flops 6291456 | bytes 5242880 | tf_op jit(solution)/shard_map/far_terms/pallas_call | solution.py:473
  194.6 12.0 %all_to_all.15.sum_ref = f32[32,8,128]{2,1,0:T(8,128)S(1)} all-to-all(f32[32,8,128]{2,1,0:T(8,128)S(1)} %get-tuple-element.26), channel_id=1, replica_groups=mesh['ka'=4,'mode'=2,'row'=4] {'ka','mode','row'}, dimensions={0} | all-to-all | bytes 262144 | tf_op jit(solution)/shard_map/all_to_all | solution.py:720
  206.6 6.3 %basis.1 = (f32[8,256,512]{2,1,0:T(8,128)}, f32[8,8]{1,0:T(8,128)}, f32[8,8]{1,0:T(8,128)}) custom-call(f32[32,8,128]{2,1,0:T(8,128)S(1)} %all_to_all.15.sum_ref, f32[8,256,512]{2,1,0:T(8,128)S(1)} %get-tuple-element.27.work_ref, f32[8,256,512]{2,1,0:T(8,128)S(1)} %copy-done.4), custom_call_target="tpu_custom_call" | custom-call | flops 33554432 | bytes 12582912 | tf_op jit(solution)/shard_map/basis/pallas_call | solution.py:602
  (61 shorter events, 0.4 us)
Async XLA Ops:
  0.6 14.4 %collective-permute-start = (f32[8,256,512]{2,1,0:T(8,128)}, f32[8,256,512]{2,1,0:T(8,128)}, u32[]{:S(2)}, u32[]{:S(2)}) collective-permute-start(f32[8,256,512]{2,1,0:T(8,128)} %bitcast.16), channel_id=1, source_target_pairs={{0,1},{1,0},{2,3},{3,2},{4,5},{5,4},{6,7},{7,6},{8,9},{9,8},{10,11... | collective-permute-start | bytes 12582920 | tf_op jit(solution)/shard_map/ppermute | solution.py:655
  4.7 49.3 %collective-permute-start.3 = (f32[8,192,512]{2,1,0:T(8,128)}, f32[8,192,512]{2,1,0:T(8,128)S(1)}, u32[]{:S(2)}, u32[]{:S(2)}) collective-permute-start(f32[8,192,512]{2,1,0:T(8,128)} %split_rows.2), channel_id=1, source_target_pairs={{8,16},{16,8},{9,17},{17,9},{10,18},{18,10},{11,19},{19,11},{12,20... | collective-permute-start | bytes 9437192 | tf_op jit(solution)/shard_map/ppermute | solution.py:33
  5.5 76.5 %collective-permute-start.1 = (f32[8,192,512]{2,1,0:T(8,128)}, f32[8,192,512]{2,1,0:T(8,128)}, u32[]{:S(2)}, u32[]{:S(2)}) collective-permute-start(f32[8,192,512]{2,1,0:T(8,128)} %split_rows.2), channel_id=1, source_target_pairs={{0,8},{8,0},{16,24},{24,16},{1,9},{9,1},{17,25},{25,17},{2,10},{10... | collective-permute-start | bytes 9437192 | tf_op jit(solution)/shard_map/ppermute | solution.py:33
  13.2 93.4 %collective-permute-start.2 = (f32[8,64,512]{2,1,0:T(8,128)}, f32[8,64,512]{2,1,0:T(8,128)}, u32[]{:S(2)}, u32[]{:S(2)}) collective-permute-start(f32[8,64,512]{2,1,0:T(8,128)} %split_rows.3), channel_id=1, source_target_pairs={{0,8},{8,0},{16,24},{24,16},{1,9},{9,1},{17,25},{25,17},{2,10},{10... | collective-permute-start | bytes 3145736 | tf_op jit(solution)/shard_map/ppermute | solution.py:33
  13.3 92.1 %collective-permute-start.4 = (f32[8,64,512]{2,1,0:T(8,128)}, f32[8,64,512]{2,1,0:T(8,128)}, u32[]{:S(2)}, u32[]{:S(2)}) collective-permute-start(f32[8,64,512]{2,1,0:T(8,128)} %split_rows.3), channel_id=1, source_target_pairs={{8,16},{16,8},{9,17},{17,9},{10,18},{18,10},{11,19},{19,11},{12,20... | collective-permute-start | bytes 3145736 | tf_op jit(solution)/shard_map/ppermute | solution.py:33
  15.0 2.2 %copy-start = (f32[1,8,8,4,8,512]{5,4,3,2,1,0:T(8,128)S(1)}, f32[1,8,8,4,8,512]{5,4,3,2,1,0:T(8,128)}, u32[]{:S(2)}) copy-start(f32[1,8,8,4,8,512]{5,4,3,2,1,0:T(8,128)} %param.15) | copy-start | bytes 12582916
  17.2 1.0 copy-start.12
  20.8 2.0 copy-start.3
  22.8 0.8 copy-start.10
  23.6 5.7 %copy-start.16 = (f32[16,16]{1,0:T(8,128)S(1)}, f32[16,16]{1,0:T(8,128)}, u32[]{:S(2)}) copy-start(f32[16,16]{1,0:T(8,128)} %two_ref.3) | copy-start | bytes 3076
  23.6 60.7 %all-to-all-start = ((f32[8,256,512]{2,1,0:T(8,128)}), f32[8,256,512]{2,1,0:T(8,128)}, u32[]{:S(2)}, u32[]{:S(2)}) async-start(f32[8,256,512]{2,1,0:T(8,128)} %copy-done.3), calls=%async_computation | async-start | bytes 8388608 | tf_op jit(solution)/shard_map/all_to_all | solution.py:690
  29.3 2.2 %copy-start.1 = (f32[1,8,8,4,8,512]{5,4,3,2,1,0:T(8,128)S(1)}, f32[1,8,8,4,8,512]{5,4,3,2,1,0:T(8,128)}, u32[]{:S(2)}) copy-start(f32[1,8,8,4,8,512]{5,4,3,2,1,0:T(8,128)} %param.15) | copy-start | bytes 12582916
  31.5 9.2 %copy-start.17 = (f32[16,16]{1,0:T(8,128)S(1)}, f32[16,16]{1,0:T(8,128)}, u32[]{:S(2)}) copy-start(f32[16,16]{1,0:T(8,128)} %one_ref.1) | copy-start | bytes 3076
  31.5 9.2 %copy-start.18 = (f32[8,8]{1,0:T(8,128)S(1)}, f32[8,8]{1,0:T(8,128)}, u32[]{:S(2)}) copy-start(f32[8,8]{1,0:T(8,128)} %three_ref.1) | copy-start | bytes 772
  31.5 9.2 %copy-start.19 = (f32[8,8]{1,0:T(8,128)S(1)}, f32[8,8]{1,0:T(8,128)}, u32[]{:S(2)}) copy-start(f32[8,8]{1,0:T(8,128)} %four_ref.1) | copy-start | bytes 772
  31.5 9.2 %copy-start.20 = (f32[8,8]{1,0:T(8,128)S(1)}, f32[8,8]{1,0:T(8,128)}, u32[]{:S(2)}) copy-start(f32[8,8]{1,0:T(8,128)} %five_ref.1) | copy-start | bytes 772
  31.5 9.2 %copy-start.21 = (f32[8,8]{1,0:T(8,128)S(1)}, f32[8,8]{1,0:T(8,128)}, u32[]{:S(2)}) copy-start(f32[8,8]{1,0:T(8,128)} %six_ref.1) | copy-start | bytes 772
  31.5 9.2 %copy-start.22 = (f32[8,8]{1,0:T(8,128)S(1)}, f32[8,8]{1,0:T(8,128)}, u32[]{:S(2)}) copy-start(f32[8,8]{1,0:T(8,128)} %der_ref.1) | copy-start | bytes 772
  31.5 9.1 %copy-start.23 = (f32[2,4]{1,0:T(2,128)S(1)}, f32[2,4]{1,0:T(2,128)}, u32[]{:S(2)}) copy-start(f32[2,4]{1,0:T(2,128)} %coupling_ref.1) | copy-start | bytes 100
  39.2 109.9 %collective-permute-start.5 = (f32[8,256,512]{2,1,0:T(8,128)}, f32[8,256,512]{2,1,0:T(8,128)}, u32[]{:S(2)}, u32[]{:S(2)}) collective-permute-start(f32[8,256,512]{2,1,0:T(8,128)} %crossing.1.refs_0_.__1_), channel_id=1, source_target_pairs={{0,2},{1,3},{2,0},{3,1},{4,6},{5,7},{6,4},{7,5},{8,10},{9,11},{10,... | collective-permute-start | bytes 12582920 | tf_op jit(solution)/shard_map/ppermute | solution.py:659
  50.4 0.8 copy-start.14
  51.2 1.0 copy-start.25
  52.2 1.0 copy-start.27
  53.1 0.8 copy-start.30
  53.9 1.8 copy-start.8
  55.7 114.8 %collective-permute-start.6 = (f32[8,192,512]{2,1,0:T(8,128)}, f32[8,192,512]{2,1,0:T(8,128)S(1)}, u32[]{:S(2)}, u32[]{:S(2)}) collective-permute-start(f32[8,192,512]{2,1,0:T(8,128)} %handed_on.3.refs_2_), channel_id=1, source_target_pairs={{0,8},{8,0},{16,24},{24,16},{1,9},{9,1},{17,25},{25,17},{2,10},{10... | collective-permute-start | bytes 9437192 | tf_op jit(solution)/shard_map/ppermute | solution.py:33
  82.0 88.5 %collective-permute-start.7 = (f32[8,192,512]{2,1,0:T(8,128)}, f32[8,192,512]{2,1,0:T(8,128)}, u32[]{:S(2)}, u32[]{:S(2)}) collective-permute-start(f32[8,192,512]{2,1,0:T(8,128)} %handed_on.2.refs_0_), channel_id=1, source_target_pairs={{8,16},{16,8},{9,17},{17,9},{10,18},{18,10},{11,19},{19,11},{12,20... | collective-permute-start | bytes 9437192 | tf_op jit(solution)/shard_map/ppermute | solution.py:33
  84.3 1.2 copy-start.28
  94.4 2.0 copy-start.5
  96.4 11.9 %copy-start.32 = (f32[8,8]{1,0:T(8,128)S(1)}, f32[8,8]{1,0:T(8,128)}, u32[]{:S(2)}) copy-start(f32[8,8]{1,0:T(8,128)} %beta_ref.1) | copy-start | bytes 772
  96.4 11.9 %copy-start.33 = (f32[4]{0:T(128)S(1)}, f32[4]{0:T(128)}, u32[]{:S(2)}) copy-start(f32[4]{0:T(128)} %rot_ref.1) | copy-start | bytes 52
  96.4 52.7 %all-to-all-start.1 = ((f32[8,256,512]{2,1,0:T(8,128)}), f32[8,256,512]{2,1,0:T(8,128)}, u32[]{:S(2)}, u32[]{:S(2)}) async-start(f32[8,256,512]{2,1,0:T(8,128)} %bitcast.22), calls=%async_computation.1 | async-start | bytes 8388608 | tf_op jit(solution)/shard_map/all_to_all | solution.py:692
  105.3 86.6 %collective-permute-start.8 = (f32[8,64,512]{2,1,0:T(8,128)}, f32[8,64,512]{2,1,0:T(8,128)}, u32[]{:S(2)}, u32[]{:S(2)}) collective-permute-start(f32[8,64,512]{2,1,0:T(8,128)} %collective-permute-done.4.refs_3_), channel_id=1, source_target_pairs={{0,8},{8,0},{16,24},{24,16},{1,9},{9,1},{17,25},{25,17},{2,10},{10... | collective-permute-start | bytes 3145736 | tf_op jit(solution)/shard_map/ppermute | solution.py:33
  106.6 85.4 %collective-permute-start.9 = (f32[8,64,512]{2,1,0:T(8,128)}, f32[8,64,512]{2,1,0:T(8,128)}, u32[]{:S(2)}, u32[]{:S(2)}) collective-permute-start(f32[8,64,512]{2,1,0:T(8,128)} %collective-permute-done.2.refs_1_), channel_id=1, source_target_pairs={{8,16},{16,8},{9,17},{17,9},{10,18},{18,10},{11,19},{19,11},{12,20... | collective-permute-start | bytes 3145736 | tf_op jit(solution)/shard_map/ppermute | solution.py:33
  108.2 2.2 %copy-start.2 = (f32[1,8,8,4,8,512]{5,4,3,2,1,0:T(8,128)S(1)}, f32[1,8,8,4,8,512]{5,4,3,2,1,0:T(8,128)}, u32[]{:S(2)}) copy-start(f32[1,8,8,4,8,512]{5,4,3,2,1,0:T(8,128)} %param.15) | copy-start | bytes 12582916
  110.4 2.2 %copy-start.24 = (f32[1,8,8,4,8,512]{5,4,3,2,1,0:T(8,128)S(1)}, f32[1,8,8,4,8,512]{5,4,3,2,1,0:T(8,128)}, u32[]{:S(2)}) copy-start(f32[1,8,8,4,8,512]{5,4,3,2,1,0:T(8,128)} %param.16) | copy-start | bytes 12582916
  112.6 1.2 copy-start.26
  113.8 1.0 copy-start.29
  114.9 1.0 copy-start.31
  134.0 2.0 copy-start.6
  149.0 2.2 %copy-start.7 = (f32[8,256,512]{2,1,0:T(8,128)S(1)}, f32[8,256,512]{2,1,0:T(8,128)}, u32[]{:S(2)}) copy-start(f32[8,256,512]{2,1,0:T(8,128)} %copy-done.6) | copy-start | bytes 12582916
  151.2 1.9 copy-start.9
  153.1 1.0 copy-start.13
  154.2 1.0 copy-start.15
  155.2 15.4 %copy-start.4 = (f32[8,256,512]{2,1,0:T(8,128)S(1)}, f32[8,256,512]{2,1,0:T(8,128)}, u32[]{:S(2)}) copy-start(f32[8,256,512]{2,1,0:T(8,128)} %copy-done.3) | copy-start | bytes 12582916
  155.2 15.4 %copy-start.11 = (f32[256,512]{1,0:T(8,128)S(1)}, f32[256,512]{1,0:T(8,128)}, u32[]{:S(2)}) copy-start(f32[256,512]{1,0:T(8,128)} %copy-done.10) | copy-start | bytes 1572868

commit v2 on v1

--- a/solution.py
+++ b/solution.py
@@ -114,19 +114,14 @@
     )(vec, skip_fn, *after)
 
 
-def split_kernel(start, parts, vec_ref, out_ref, held, sems):
+def split_kernel(start, vec_ref, out_ref, held, sems):
     count, rows, _ = out_ref.shape
-    size = rows // parts
-    spots = [(i, p, pl.ds(p * size, size)) for i in range(count) for p in range(parts)]
     loads = [
-        pltpu.make_async_copy(
-            vec_ref.at[i, pl.ds(start + p * size, size)], held.at[i, place], sems.at[0, i, p]
-        )
-        for i, p, place in spots
+        pltpu.make_async_copy(vec_ref.at[i, pl.ds(start, rows)], held.at[i], sems.at[0, i])
+        for i in range(count)
     ]
     stores = [
-        pltpu.make_async_copy(held.at[i, place], out_ref.at[i, place], sems.at[1, i, p])
-        for i, p, place in spots
+        pltpu.make_async_copy(held.at[i], out_ref.at[i], sems.at[1, i]) for i in range(count)
     ]
     for load in loads:
         load.start()
@@ -140,15 +135,14 @@
 def split_rows(vec, start, stop):
     nvec, _, width = vec.shape
     shape = (nvec, stop - start, width)
-    parts = next(p for p in (4, 2, 1) if shape[1] % (SUBLANES * p) == 0)
-    return pl.pallas_call(
-        functools.partial(split_kernel, start, parts),
+    return pl.pallas_call(
+        functools.partial(split_kernel, start),
         in_specs=[pl.BlockSpec(memory_space=pl.ANY)],
         out_specs=pl.BlockSpec(memory_space=pl.ANY),
         out_shape=jax.ShapeDtypeStruct(shape, jnp.float32),
         scratch_shapes=[
             pltpu.VMEM(shape, jnp.float32),
-            pltpu.SemaphoreType.DMA((2, nvec, parts)),
+            pltpu.SemaphoreType.DMA((2, nvec)),
         ],
         compiler_params=pltpu.CompilerParams(vmem_limit_bytes=FULL_VMEM_BYTES),
         cost_estimate=pl.CostEstimate(
@@ -713,7 +707,7 @@
             vec,
             sums,
             start,
-            block_rows,
+            block_rows if number < len(starts) - 1 else max(block_rows // 2, SUBLANES),
             devices if number == len(starts) - 1 else 1,
         )
         sums = copied[0]

time: 214 us -> 214 us (level)
  transfers between devices with their start and end apart: 12 -> 12, of which waited for: 2 -> 2; matrix products, arithmetic and copies ran while one was open for 0% -> 0% of each run, Pallas kernels for 35% -> 34%
where the time goes in v2:
time: 214 us; the launch traced here: 213 us
  Pallas kernels  82.5 us (39%)
  starting transfers between devices  53 us (25%)
  local copies, waits for them, and re-layouts  33.2 us (16%)
  waiting for transfers between devices  28.5 us (13%)
  blocking collectives  12 us (6%)
  between operations  3.5 us (2%)
    ppermute x8, starting transfers between devices, pair_exchange(): return lax.ppermute(value, axis, pairs)  39.6 us
    unnamed x68, local copies, waits for them, and re-layouts  32.6 us
    pallas_call x1, Pallas kernels, local_terms(): pl.pallas_call(functools.partial(local_kernel, nvec, nblocks, len(held)),...  18.1 us
    ppermute x8, waiting for transfers between devices, pair_exchange(): return lax.ppermute(value, axis, pairs)  15.5 us
    pallas_call x1, Pallas kernels, join_terms(): pl.pallas_call(functools.partial(join_kernel, tuple(starts), len(sums)),...  15.3 us
    all_to_all x1, waiting for transfers between devices, shards(): lax.all_to_all(mode_shares, 'mode', split_axis=0, concat_axis=0, tiled=True)  13 us
    all_to_all x1, blocking collectives, shards(): lax.all_to_all(copied, ALL_AXES, split_axis=0, concat_axis=0, tiled=True)  12 us
    pallas_call x1, Pallas kernels, operators(): pl.pallas_call(functools.partial(operators_kernel, points, group), in_spe...  9.65 us
  transfers between devices with their start and end apart: 12, of which 2 were waited for; matrix products, arithmetic and copies ran while one was open for 0% of the time, Pallas kernels for 34%

profile of v2, /device:TPU:0, one launch (start us, length us, event | category | flops | bytes accessed | tf_op | source)
XLA Modules:
  0.0 212.8 jit_solution(14207622269948583204)
XLA Ops:
  0.6 0.5 collective-permute-start
  1.1 2.8 %split_rows.2 = f32[8,192,512]{2,1,0:T(8,128)} custom-call(f32[8,256,512]{2,1,0:T(8,128)} %bitcast.17), custom_call_target="tpu_custom_call" | custom-call | bytes 6291456 | tf_op jit(solution)/shard_map/split_rows/pallas_call | solution.py:138
  3.9 0.9 collective-permute-start.3
  4.8 5.3 %collective-permute-start.1 = (f32[8,192,512]{2,1,0:T(8,128)}, f32[8,192,512]{2,1,0:T(8,128)}, u32[]{:S(2)}, u32[]{:S(2)}) collective-permute-start(f32[8,192,512]{2,1,0:T(8,128)} %split_rows.2), channel_id=1, source_target_pairs={{0,8},{8,0},{16,24},{24,16},{1,9},{9,1},{17,25},{25,17},{2,10},{10... | collective-permute-start | bytes 9437192 | tf_op jit(solution)/shard_map/ppermute | solution.py:33
  10.1 2.1 split_rows.3
  12.2 1.6 collective-permute-start.4
  14.0 2.2 %copy-done = f32[1,8,8,4,8,512]{5,4,3,2,1,0:T(8,128)S(1)} copy-done((f32[1,8,8,4,8,512]{5,4,3,2,1,0:T(8,128)S(1)}, f32[1,8,8,4,8,512]{5,4,3,2,1,0:T(8,128)}, u32[]{:S(2)}) %copy-start) | copy-done | bytes 4194328
  16.2 1.0 copy-done.12
  17.2 2.6 %resident.1 = (f32[8,128]{1,0:T(8,128)S(1)}, f32[8,256,512]{2,1,0:T(8,128)S(1)}, f32[256,512]{1,0:T(8,128)S(1)}) custom-call(f32[8,256,512]{2,1,0:T(8,128)S(1)} %bitcast.19, f32[256,512]{1,0:T(8,128)S(1)} %bitcast.23, f32[8,256,512]{2,1,0:T(8,128)} %collective-permute-done.refs_1_.refs_0_), custom_call_target="tpu_custom_call" | custom-call | flops 9437184 | bytes 8388608 | tf_op jit(solution)/shard_map/resident/pallas_call | solution.py:98
  19.8 2.0 copy-done.3
  21.8 0.8 copy-done.10
  22.6 5.7 %all-to-all-start = ((f32[8,256,512]{2,1,0:T(8,128)}), f32[8,256,512]{2,1,0:T(8,128)}, u32[]{:S(2)}, u32[]{:S(2)}) async-start(f32[8,256,512]{2,1,0:T(8,128)} %copy-done.3), calls=%async_computation | async-start | bytes 8388608 | tf_op jit(solution)/shard_map/all_to_all | solution.py:684
  28.3 2.2 %copy-done.1 = f32[1,8,8,4,8,512]{5,4,3,2,1,0:T(8,128)S(1)} copy-done((f32[1,8,8,4,8,512]{5,4,3,2,1,0:T(8,128)S(1)}, f32[1,8,8,4,8,512]{5,4,3,2,1,0:T(8,128)}, u32[]{:S(2)}) %copy-start.1) | copy-done | bytes 4194328
  30.5 7.6 %crossing.1.refs_0_.__1_ = f32[8,256,512]{2,1,0:T(8,128)} custom-call(s32[3]{0:T(128)S(1)} %pad_add_fusion.at_ref, f32[16,16]{1,0:T(8,128)S(1)} %copy-done.16, f32[8,256,512]{2,1,0:T(8,128)S(1)} %bitcast.20, f32[8,256,512]{2,1,0:T(8,128)} %collective-permute-done.refs_1_.refs_0_), custom_call_target="tpu_custom_call" | custom-call | flops 16777216 | bytes 12582912 | tf_op jit(solution)/shard_map/crossing/pallas_call | solution.py:285
  38.1 1.5 collective-permute-start.5
  39.7 9.7 %operators.1 = (f32[2,256,256]{2,1,0:T(8,128)S(1)}, f32[512,512]{1,0:T(8,128)S(1)}, f32[512,512]{1,0:T(8,128)S(1)}, f32[2,256,256]{2,1,0:T(8,128)S(1)}) custom-call(s32[3]{0:T(128)S(1)} %pad_add_fusion.at_ref, f32[2,4]{1,0:T(2,128)S(1)} %copy-done.23, f32[16,16]{1,0:T(8,128)S(1)} %copy-done.17, f32[16,16]{1,0:T(8,128)S(1)} %copy-done.16, ...), custom_call_target="tpu_custom_call" | custom-call | flops 500000000 | bytes 4000000 | tf_op jit(solution)/shard_map/operators/pallas_call | solution.py:232
  49.3 0.8 copy-done.14
  50.2 1.0 copy-done.25
  51.1 1.0 copy-done.27
  52.1 0.8 copy-done.30
  52.9 1.7 copy-done.8
  54.7 26.6 %collective-permute-start.6 = (f32[8,192,512]{2,1,0:T(8,128)}, f32[8,192,512]{2,1,0:T(8,128)S(1)}, u32[]{:S(2)}, u32[]{:S(2)}) collective-permute-start(f32[8,192,512]{2,1,0:T(8,128)} %handed_on.3.refs_2_), channel_id=1, source_target_pairs={{0,8},{8,0},{16,24},{24,16},{1,9},{9,1},{17,25},{25,17},{2,10},{10... | collective-permute-start | bytes 9437192 | tf_op jit(solution)/shard_map/ppermute | solution.py:33
  81.3 2.3 %collective-permute-start.7 = (f32[8,192,512]{2,1,0:T(8,128)}, f32[8,192,512]{2,1,0:T(8,128)}, u32[]{:S(2)}, u32[]{:S(2)}) collective-permute-start(f32[8,192,512]{2,1,0:T(8,128)} %handed_on.2.refs_0_), channel_id=1, source_target_pairs={{8,16},{16,8},{9,17},{17,9},{10,18},{18,10},{11,19},{19,11},{12,20... | collective-permute-start | bytes 9437192 | tf_op jit(solution)/shard_map/ppermute | solution.py:33
  83.6 1.2 copy-done.28
  84.8 8.8 %mode_kinetic.1 = f32[2,4,256,512]{3,2,1,0:T(8,128)S(1)} custom-call(f32[2,4,256,512]{3,2,1,0:T(8,128)} %bitcast.12.in_ref, f32[512,512]{1,0:T(8,128)S(1)} %copy-done.28), custom_call_target="tpu_custom_call" | custom-call | flops 6442450944 | bytes 8388608 | tf_op jit(solution)/shard_map/mode_kinetic/pallas_call | solution.py:356
  93.6 2.0 copy-done.5
  95.6 5.7 %all-to-all-start.1 = ((f32[8,256,512]{2,1,0:T(8,128)}), f32[8,256,512]{2,1,0:T(8,128)}, u32[]{:S(2)}, u32[]{:S(2)}) async-start(f32[8,256,512]{2,1,0:T(8,128)} %bitcast.22), calls=%async_computation.1 | async-start | bytes 8388608 | tf_op jit(solution)/shard_map/all_to_all | solution.py:686
  101.3 0.6 constant_dynamic-slice_fusion.1
  104.6 1.2 collective-permute-start.8
  105.8 1.6 collective-permute-start.9
  107.5 2.2 %copy-done.2 = f32[1,8,8,4,8,512]{5,4,3,2,1,0:T(8,128)S(1)} copy-done((f32[1,8,8,4,8,512]{5,4,3,2,1,0:T(8,128)S(1)}, f32[1,8,8,4,8,512]{5,4,3,2,1,0:T(8,128)}, u32[]{:S(2)}) %copy-start.2) | copy-done | bytes 4194328
  109.7 2.2 %copy-done.24 = f32[1,8,8,4,8,512]{5,4,3,2,1,0:T(8,128)S(1)} copy-done((f32[1,8,8,4,8,512]{5,4,3,2,1,0:T(8,128)S(1)}, f32[1,8,8,4,8,512]{5,4,3,2,1,0:T(8,128)}, u32[]{:S(2)}) %copy-start.24) | copy-done | bytes 4194328
  111.9 1.2 copy-done.26
  113.1 1.0 copy-done.29
  114.1 1.0 copy-done.31
  115.2 18.1 %local_terms.1.work_ref = f32[8,256,512]{2,1,0:T(8,128)S(1)} custom-call(s32[3]{0:T(128)S(1)} %pad_add_fusion.at_ref, f32[4]{0:T(128)S(1)} %copy-done.33, f32[8,8]{1,0:T(8,128)S(1)} %copy-done.32, f32[8,256,512]{2,1,0:T(8,128)S(1)} %bitcast.21, f32[8,256,512]{2,1,0:T(8,128)} %collective-permute-done.refs_1_.refs_0_, f32[8,256,512]{2,1,0:T(8,128)S(1)} %bitcast.26, ...), custom_call_target="tpu_custom_call" | custom-call | flops 12884901888 | bytes 16777216 | tf_op jit(solution)/shard_map/local_terms/pallas_call | solution.py:321
  133.3 2.0 copy-done.6
  135.3 13.0 %all-to-all-done.1.refs_4_ = f32[8,256,512]{2,1,0:T(8,128)} async-done(((f32[8,256,512]{2,1,0:T(8,128)}), f32[8,256,512]{2,1,0:T(8,128)}, u32[]{:S(2)}, u32[]{:S(2)}) %all-to-all-start.1) | async-done | bytes 4194336 | tf_op jit(solution)/shard_map/all_to_all | solution.py:686
  148.3 2.2 %copy-done.7 = f32[8,256,512]{2,1,0:T(8,128)S(1)} copy-done((f32[8,256,512]{2,1,0:T(8,128)S(1)}, f32[8,256,512]{2,1,0:T(8,128)}, u32[]{:S(2)}) %copy-start.7) | copy-done | bytes 4194328
  150.5 1.9 copy-done.9
  152.4 1.0 copy-done.13
  153.4 1.0 copy-done.15
  154.5 15.3 %join_terms.1.work_ref = f32[8,256,512]{2,1,0:T(8,128)S(1)} custom-call(s32[3]{0:T(128)S(1)} %pad_add_fusion.at_ref, f32[8,256,512]{2,1,0:T(8,128)S(1)} %copy-done.7, f32[256,512]{1,0:T(8,128)S(1)} %bitcast.24, f32[2,256,256]{2,1,0:T(8,128)S(1)} %copy-done.15, f32[8,192,512]{2,1,0:T(8,128)} %handed_on.2.refs_0_, ...), custom_call_target="tpu_custom_call" | custom-call | flops 6442450944 | bytes 25165824 | tf_op jit(solution)/shard_map/join_terms/pallas_call | solution.py:400
  169.8 5.9 %far_terms.2 = (f32[8,256,512]{2,1,0:T(8,128)S(1)}, f32[1,8,128]{2,1,0:T(8,128)S(1)}) custom-call(f32[2]{0:T(128)S(1)} %pad_maximum_fusion.coef_ref, f32[8,256,512]{2,1,0:T(8,128)S(1)} %join_terms.1.work_ref, f32[8,192,512]{2,1,0:T(8,128)S(1)} %collective-permute-done.6.first_ref, ...), custom_call_target="tpu_custom_call", output_to_operand_aliasing={{0}: (1, {})} | custom-call | flops 18874368 | bytes 15728640 | tf_op jit(solution)/shard_map/far_terms/pallas_call | solution.py:467
  175.7 15.5 %collective-permute-done.8.first_ref = f32[8,64,512]{2,1,0:T(8,128)} collective-permute-done((f32[8,64,512]{2,1,0:T(8,128)}, f32[8,64,512]{2,1,0:T(8,128)}, u32[]{:S(2)}, u32[]{:S(2)}) %collective-permute-start.8) | collective-permute-done | bytes 1048608 | tf_op jit(solution)/shard_map/ppermute | solution.py:33
  191.2 3.3 %far_terms.3 = (f32[8,256,512]{2,1,0:T(8,128)S(1)}, f32[32,8,128]{2,1,0:T(8,128)S(1)}) custom-call(f32[2]{0:T(128)S(1)} %pad_maximum_fusion.coef_ref, f32[8,256,512]{2,1,0:T(8,128)S(1)} %get-tuple-element.24.work_ref, f32[8,64,512]{2,1,0:T(8,128)} %collective-permute-done.8.first_ref, ...), custom_call_target="tpu_custom_call", output_to_operand_aliasing={{0}: (1, {})} | custom-call | flops 6291456 | bytes 5242880 | tf_op jit(solution)/shard_map/far_terms/pallas_call | solution.py:467
  194.5 12.0 %all_to_all.15.sum_ref = f32[32,8,128]{2,1,0:T(8,128)S(1)} all-to-all(f32[32,8,128]{2,1,0:T(8,128)S(1)} %get-tuple-element.26), channel_id=1, replica_groups=mesh['ka'=4,'mode'=2,'row'=4] {'ka','mode','row'}, dimensions={0} | all-to-all | bytes 262144 | tf_op jit(solution)/shard_map/all_to_all | solution.py:714
  206.5 6.3 %basis.1 = (f32[8,256,512]{2,1,0:T(8,128)}, f32[8,8]{1,0:T(8,128)}, f32[8,8]{1,0:T(8,128)}) custom-call(f32[32,8,128]{2,1,0:T(8,128)S(1)} %all_to_all.15.sum_ref, f32[8,256,512]{2,1,0:T(8,128)S(1)} %get-tuple-element.27.work_ref, f32[8,256,512]{2,1,0:T(8,128)S(1)} %copy-done.4), custom_call_target="tpu_custom_call" | custom-call | flops 33554432 | bytes 12582912 | tf_op jit(solution)/shard_map/basis/pallas_call | solution.py:596
  (61 shorter events, 0.4 us)
Async XLA Ops:
  0.6 13.3 %collective-permute-start = (f32[8,256,512]{2,1,0:T(8,128)}, f32[8,256,512]{2,1,0:T(8,128)}, u32[]{:S(2)}, u32[]{:S(2)}) collective-permute-start(f32[8,256,512]{2,1,0:T(8,128)} %bitcast.16), channel_id=1, source_target_pairs={{0,1},{1,0},{2,3},{3,2},{4,5},{5,4},{6,7},{7,6},{8,9},{9,8},{10,11... | collective-permute-start | bytes 12582920 | tf_op jit(solution)/shard_map/ppermute | solution.py:649
  3.9 49.0 %collective-permute-start.3 = (f32[8,192,512]{2,1,0:T(8,128)}, f32[8,192,512]{2,1,0:T(8,128)S(1)}, u32[]{:S(2)}, u32[]{:S(2)}) collective-permute-start(f32[8,192,512]{2,1,0:T(8,128)} %split_rows.2), channel_id=1, source_target_pairs={{8,16},{16,8},{9,17},{17,9},{10,18},{18,10},{11,19},{19,11},{12,20... | collective-permute-start | bytes 9437192 | tf_op jit(solution)/shard_map/ppermute | solution.py:33
  4.8 76.5 %collective-permute-start.1 = (f32[8,192,512]{2,1,0:T(8,128)}, f32[8,192,512]{2,1,0:T(8,128)}, u32[]{:S(2)}, u32[]{:S(2)}) collective-permute-start(f32[8,192,512]{2,1,0:T(8,128)} %split_rows.2), channel_id=1, source_target_pairs={{0,8},{8,0},{16,24},{24,16},{1,9},{9,1},{17,25},{25,17},{2,10},{10... | collective-permute-start | bytes 9437192 | tf_op jit(solution)/shard_map/ppermute | solution.py:33
  12.2 93.7 %collective-permute-start.2 = (f32[8,64,512]{2,1,0:T(8,128)}, f32[8,64,512]{2,1,0:T(8,128)}, u32[]{:S(2)}, u32[]{:S(2)}) collective-permute-start(f32[8,64,512]{2,1,0:T(8,128)} %split_rows.3), channel_id=1, source_target_pairs={{0,8},{8,0},{16,24},{24,16},{1,9},{9,1},{17,25},{25,17},{2,10},{10... | collective-permute-start | bytes 3145736 | tf_op jit(solution)/shard_map/ppermute | solution.py:33
  12.2 92.4 %collective-permute-start.4 = (f32[8,64,512]{2,1,0:T(8,128)}, f32[8,64,512]{2,1,0:T(8,128)}, u32[]{:S(2)}, u32[]{:S(2)}) collective-permute-start(f32[8,64,512]{2,1,0:T(8,128)} %split_rows.3), channel_id=1, source_target_pairs={{8,16},{16,8},{9,17},{17,9},{10,18},{18,10},{11,19},{19,11},{12,20... | collective-permute-start | bytes 3145736 | tf_op jit(solution)/shard_map/ppermute | solution.py:33
  14.0 2.2 %copy-start = (f32[1,8,8,4,8,512]{5,4,3,2,1,0:T(8,128)S(1)}, f32[1,8,8,4,8,512]{5,4,3,2,1,0:T(8,128)}, u32[]{:S(2)}) copy-start(f32[1,8,8,4,8,512]{5,4,3,2,1,0:T(8,128)} %param.15) | copy-start | bytes 12582916
  16.2 1.0 copy-start.12
  19.8 2.0 copy-start.3
  21.8 0.8 copy-start.10
  22.6 5.7 %copy-start.16 = (f32[16,16]{1,0:T(8,128)S(1)}, f32[16,16]{1,0:T(8,128)}, u32[]{:S(2)}) copy-start(f32[16,16]{1,0:T(8,128)} %two_ref.3) | copy-start | bytes 3076
  22.6 61.0 %all-to-all-start = ((f32[8,256,512]{2,1,0:T(8,128)}), f32[8,256,512]{2,1,0:T(8,128)}, u32[]{:S(2)}, u32[]{:S(2)}) async-start(f32[8,256,512]{2,1,0:T(8,128)} %copy-done.3), calls=%async_computation | async-start | bytes 8388608 | tf_op jit(solution)/shard_map/all_to_all | solution.py:684
  28.3 2.2 %copy-start.1 = (f32[1,8,8,4,8,512]{5,4,3,2,1,0:T(8,128)S(1)}, f32[1,8,8,4,8,512]{5,4,3,2,1,0:T(8,128)}, u32[]{:S(2)}) copy-start(f32[1,8,8,4,8,512]{5,4,3,2,1,0:T(8,128)} %param.15) | copy-start | bytes 12582916
  30.5 9.2 %copy-start.17 = (f32[16,16]{1,0:T(8,128)S(1)}, f32[16,16]{1,0:T(8,128)}, u32[]{:S(2)}) copy-start(f32[16,16]{1,0:T(8,128)} %one_ref.1) | copy-start | bytes 3076
  30.5 9.2 %copy-start.18 = (f32[8,8]{1,0:T(8,128)S(1)}, f32[8,8]{1,0:T(8,128)}, u32[]{:S(2)}) copy-start(f32[8,8]{1,0:T(8,128)} %three_ref.1) | copy-start | bytes 772
  30.5 9.2 %copy-start.19 = (f32[8,8]{1,0:T(8,128)S(1)}, f32[8,8]{1,0:T(8,128)}, u32[]{:S(2)}) copy-start(f32[8,8]{1,0:T(8,128)} %four_ref.1) | copy-start | bytes 772
  30.5 9.2 %copy-start.20 = (f32[8,8]{1,0:T(8,128)S(1)}, f32[8,8]{1,0:T(8,128)}, u32[]{:S(2)}) copy-start(f32[8,8]{1,0:T(8,128)} %five_ref.1) | copy-start | bytes 772
  30.5 9.2 %copy-start.21 = (f32[8,8]{1,0:T(8,128)S(1)}, f32[8,8]{1,0:T(8,128)}, u32[]{:S(2)}) copy-start(f32[8,8]{1,0:T(8,128)} %six_ref.1) | copy-start | bytes 772
  30.5 9.2 %copy-start.22 = (f32[8,8]{1,0:T(8,128)S(1)}, f32[8,8]{1,0:T(8,128)}, u32[]{:S(2)}) copy-start(f32[8,8]{1,0:T(8,128)} %der_ref.1) | copy-start | bytes 772
  30.5 9.1 %copy-start.23 = (f32[2,4]{1,0:T(2,128)S(1)}, f32[2,4]{1,0:T(2,128)}, u32[]{:S(2)}) copy-start(f32[2,4]{1,0:T(2,128)} %coupling_ref.1) | copy-start | bytes 100
  38.1 110.1 %collective-permute-start.5 = (f32[8,256,512]{2,1,0:T(8,128)}, f32[8,256,512]{2,1,0:T(8,128)}, u32[]{:S(2)}, u32[]{:S(2)}) collective-permute-start(f32[8,256,512]{2,1,0:T(8,128)} %crossing.1.refs_0_.__1_), channel_id=1, source_target_pairs={{0,2},{1,3},{2,0},{3,1},{4,6},{5,7},{6,4},{7,5},{8,10},{9,11},{10,... | collective-permute-start | bytes 12582920 | tf_op jit(solution)/shard_map/ppermute | solution.py:653
  49.3 0.8 copy-start.14
  50.2 1.0 copy-start.25
  51.1 1.0 copy-start.27
  52.1 0.8 copy-start.30
  52.9 1.8 copy-start.8
  54.7 115.1 %collective-permute-start.6 = (f32[8,192,512]{2,1,0:T(8,128)}, f32[8,192,512]{2,1,0:T(8,128)S(1)}, u32[]{:S(2)}, u32[]{:S(2)}) collective-permute-start(f32[8,192,512]{2,1,0:T(8,128)} %handed_on.3.refs_2_), channel_id=1, source_target_pairs={{0,8},{8,0},{16,24},{24,16},{1,9},{9,1},{17,25},{25,17},{2,10},{10... | collective-permute-start | bytes 9437192 | tf_op jit(solution)/shard_map/ppermute | solution.py:33
  81.3 88.5 %collective-permute-start.7 = (f32[8,192,512]{2,1,0:T(8,128)}, f32[8,192,512]{2,1,0:T(8,128)}, u32[]{:S(2)}, u32[]{:S(2)}) collective-permute-start(f32[8,192,512]{2,1,0:T(8,128)} %handed_on.2.refs_0_), channel_id=1, source_target_pairs={{8,16},{16,8},{9,17},{17,9},{10,18},{18,10},{11,19},{19,11},{12,20... | collective-permute-start | bytes 9437192 | tf_op jit(solution)/shard_map/ppermute | solution.py:33
  83.6 1.2 copy-start.28
  93.6 2.0 copy-start.5
  95.6 11.9 %copy-start.32 = (f32[8,8]{1,0:T(8,128)S(1)}, f32[8,8]{1,0:T(8,128)}, u32[]{:S(2)}) copy-start(f32[8,8]{1,0:T(8,128)} %beta_ref.1) | copy-start | bytes 772
  95.6 11.9 %copy-start.33 = (f32[4]{0:T(128)S(1)}, f32[4]{0:T(128)}, u32[]{:S(2)}) copy-start(f32[4]{0:T(128)} %rot_ref.1) | copy-start | bytes 52
  95.6 52.7 %all-to-all-start.1 = ((f32[8,256,512]{2,1,0:T(8,128)}), f32[8,256,512]{2,1,0:T(8,128)}, u32[]{:S(2)}, u32[]{:S(2)}) async-start(f32[8,256,512]{2,1,0:T(8,128)} %bitcast.22), calls=%async_computation.1 | async-start | bytes 8388608 | tf_op jit(solution)/shard_map/all_to_all | solution.py:686
  104.6 86.6 %collective-permute-start.8 = (f32[8,64,512]{2,1,0:T(8,128)}, f32[8,64,512]{2,1,0:T(8,128)}, u32[]{:S(2)}, u32[]{:S(2)}) collective-permute-start(f32[8,64,512]{2,1,0:T(8,128)} %collective-permute-done.4.refs_3_), channel_id=1, source_target_pairs={{0,8},{8,0},{16,24},{24,16},{1,9},{9,1},{17,25},{25,17},{2,10},{10... | collective-permute-start | bytes 3145736 | tf_op jit(solution)/shard_map/ppermute | solution.py:33
  105.8 85.4 %collective-permute-start.9 = (f32[8,64,512]{2,1,0:T(8,128)}, f32[8,64,512]{2,1,0:T(8,128)}, u32[]{:S(2)}, u32[]{:S(2)}) collective-permute-start(f32[8,64,512]{2,1,0:T(8,128)} %collective-permute-done.2.refs_1_), channel_id=1, source_target_pairs={{8,16},{16,8},{9,17},{17,9},{10,18},{18,10},{11,19},{19,11},{12,20... | collective-permute-start | bytes 3145736 | tf_op jit(solution)/shard_map/ppermute | solution.py:33
  107.5 2.2 %copy-start.2 = (f32[1,8,8,4,8,512]{5,4,3,2,1,0:T(8,128)S(1)}, f32[1,8,8,4,8,512]{5,4,3,2,1,0:T(8,128)}, u32[]{:S(2)}) copy-start(f32[1,8,8,4,8,512]{5,4,3,2,1,0:T(8,128)} %param.15) | copy-start | bytes 12582916
  109.7 2.2 %copy-start.24 = (f32[1,8,8,4,8,512]{5,4,3,2,1,0:T(8,128)S(1)}, f32[1,8,8,4,8,512]{5,4,3,2,1,0:T(8,128)}, u32[]{:S(2)}) copy-start(f32[1,8,8,4,8,512]{5,4,3,2,1,0:T(8,128)} %param.16) | copy-start | bytes 12582916
  111.9 1.2 copy-start.26
  113.1 1.0 copy-start.29
  114.1 1.0 copy-start.31
  133.3 2.0 copy-start.6
  148.3 2.2 %copy-start.7 = (f32[8,256,512]{2,1,0:T(8,128)S(1)}, f32[8,256,512]{2,1,0:T(8,128)}, u32[]{:S(2)}) copy-start(f32[8,256,512]{2,1,0:T(8,128)} %copy-done.6) | copy-start | bytes 12582916
  150.5 1.9 copy-start.9
  152.4 1.0 copy-start.13
  153.4 1.0 copy-start.15
  154.5 15.4 %copy-start.4 = (f32[8,256,512]{2,1,0:T(8,128)S(1)}, f32[8,256,512]{2,1,0:T(8,128)}, u32[]{:S(2)}) copy-start(f32[8,256,512]{2,1,0:T(8,128)} %copy-done.3) | copy-start | bytes 12582916
  154.5 15.4 %copy-start.11 = (f32[256,512]{1,0:T(8,128)S(1)}, f32[256,512]{1,0:T(8,128)}, u32[]{:S(2)}) copy-start(f32[256,512]{1,0:T(8,128)} %copy-done.10) | copy-start | bytes 1572868

commit v3 on v2

--- a/solution.py
+++ b/solution.py
@@ -551,55 +551,72 @@
     return matrix[:, : len(columns)]
 
 
-def basis_kernel(nvec, count, sum_ref, work_ref, vec_ref, out_ref, alpha_ref, lower_ref, coefs):
-    @pl.when(pl.program_id(0) == 0)
-    def _():
-        packed = sum_ref[0]
-        for other in range(1, sum_ref.shape[0]):
-            packed = packed + sum_ref[other]
-        total, lower, inverse, mixing = small_algebra(nvec, count, packed)
-        for number, columns in enumerate((inverse, mixing)):
-            for j in range(nvec):
-                for i in range(nvec):
-                    if number == 1 or j <= i:
-                        coefs[number, i * nvec + j] = across(columns[j], i)
-        alpha_ref[...] = gathered_columns(total)
-        lower_ref[...] = gathered_columns(lower)
-
-    start = pl.multiple_of(pl.program_id(0) * out_ref.shape[1], out_ref.shape[1])
-    places = tiles(*out_ref.shape[1:])
-    for at in range(0, len(places), 4):
-        group = places[at : at + 4]
-        held = [(pl.ds(start + place.start, SUBLANES), lanes) for place, lanes in group]
-        totals = {}
-        for number, ref in ((1, vec_ref), (0, work_ref)):
-            for j in range(nvec):
-                values = [ref[(j, *place)] for place in held]
-                for i in range(nvec):
-                    if number == 0 and j > i:
-                        continue
-                    coef = coefs[number, i * nvec + j]
-                    for spot, value in enumerate(values):
-                        term = coef * value
-                        here = (i, spot)
-                        totals[here] = totals[here] + term if here in totals else term
-        for (i, spot), value in totals.items():
-            out_ref[(i, *group[spot])] = value
+def basis_kernel(
+    nvec, count, block_rows, sum_ref, work_ref, vec_ref, out_ref, alpha_ref, lower_ref, coefs, held, sems
+):
+    packed = sum_ref[0]
+    for other in range(1, sum_ref.shape[0]):
+        packed = packed + sum_ref[other]
+    total, lower, inverse, mixing = small_algebra(nvec, count, packed)
+    for number, columns in enumerate((inverse, mixing)):
+        for j in range(nvec):
+            for i in range(nvec):
+                if number == 1 or j <= i:
+                    coefs[number, i * nvec + j] = across(columns[j], i)
+    alpha_ref[...] = gathered_columns(total)
+    lower_ref[...] = gathered_columns(lower)
+    rows, width = held.shape[1:]
+    blocks = rows // block_rows
+
+    def copy_out(step):
+        place = pl.ds(pl.multiple_of(step * block_rows, block_rows), block_rows)
+        return pltpu.make_async_copy(held.at[:, place], out_ref.at[:, place], sems.at[step])
+
+    def some_rows(step, _):
+        start = pl.multiple_of(step * block_rows, block_rows)
+        places = [
+            (pl.ds(start + place.start, SUBLANES), lanes)
+            for place, lanes in tiles(block_rows, width)
+        ]
+        for at in range(0, len(places), 4):
+            group = places[at : at + 4]
+            totals = {}
+            for number, ref in ((1, vec_ref), (0, work_ref)):
+                for j in range(nvec):
+                    values = [ref[(j, *place)] for place in group]
+                    for i in range(nvec):
+                        if number == 0 and j > i:
+                            continue
+                        coef = coefs[number, i * nvec + j]
+                        for spot, value in enumerate(values):
+                            term = coef * value
+                            here = (i, spot)
+                            totals[here] = totals[here] + term if here in totals else term
+            for (i, spot), value in totals.items():
+                held[(i, *group[spot])] = value
+        copy_out(step).start()
+        return 0
+
+    lax.fori_loop(0, blocks, some_rows, 0)
+    for step in range(blocks):
+        copy_out(step).wait()
 
 
 def basis_of(count, sums, work, vec, block_rows):
     nvec, rows, width = work.shape
-    block = pl.BlockSpec((nvec, block_rows, width), lambda s: (0, s, 0))
     small = jax.ShapeDtypeStruct((nvec, nvec), jnp.float32)
     whole = pl.BlockSpec(memory_space=pltpu.VMEM)
     work, vec = (pltpu.with_memory_space_constraint(array, pltpu.VMEM) for array in (work, vec))
     return pl.pallas_call(
-        functools.partial(basis_kernel, nvec, count),
-        grid=(rows // block_rows,),
+        functools.partial(basis_kernel, nvec, count, block_rows),
         in_specs=[whole, whole, whole],
-        out_specs=[block, whole_spec(small.shape), whole_spec(small.shape)],
+        out_specs=[pl.BlockSpec(memory_space=pl.ANY), whole, whole],
         out_shape=[jax.ShapeDtypeStruct(work.shape, jnp.float32), small, small],
-        scratch_shapes=[pltpu.VMEM((2, nvec * nvec, SUBLANES, LANES), jnp.float32)],
+        scratch_shapes=[
+            pltpu.VMEM((2, nvec * nvec, SUBLANES, LANES), jnp.float32),
+            pltpu.VMEM(work.shape, jnp.float32),
+            pltpu.SemaphoreType.DMA((rows // block_rows,)),
+        ],
         compiler_params=pltpu.CompilerParams(vmem_limit_bytes=SMALL_VMEM_BYTES),
         cost_estimate=pl.CostEstimate(
             flops=4 * nvec * work.size, bytes_accessed=12 * work.size, transcendentals=0
@@ -707,7 +724,7 @@
             vec,
             sums,
             start,
-            block_rows if number < len(starts) - 1 else max(block_rows // 2, SUBLANES),
+            block_rows,
             devices if number == len(starts) - 1 else 1,
         )
         sums = copied[0]

time: 214 us -> 213 us (level)
  no operation moved by 1% of the time
where the time goes in v3:
time: 213 us; the launch traced here: 212 us
  Pallas kernels  81.6 us (38%)
  starting transfers between devices  53 us (25%)
  local copies, waits for them, and re-layouts  33.2 us (16%)
  waiting for transfers between devices  28.5 us (13%)
  blocking collectives  12 us (6%)
  between operations  3.66 us (2%)
    ppermute x8, starting transfers between devices, pair_exchange(): return lax.ppermute(value, axis, pairs)  39.6 us
    unnamed x68, local copies, waits for them, and re-layouts  32.6 us
    pallas_call x1, Pallas kernels, local_terms(): pl.pallas_call(functools.partial(local_kernel, nvec, nblocks, len(held)),...  18.1 us
    ppermute x8, waiting for transfers between devices, pair_exchange(): return lax.ppermute(value, axis, pairs)  15.5 us
    pallas_call x1, Pallas kernels, join_terms(): pl.pallas_call(functools.partial(join_kernel, tuple(starts), len(sums)),...  15.3 us
    all_to_all x1, waiting for transfers between devices, shards(): lax.all_to_all(mode_shares, 'mode', split_axis=0, concat_axis=0, tiled=True)  13 us
    all_to_all x1, blocking collectives, shards(): lax.all_to_all(copied, ALL_AXES, split_axis=0, concat_axis=0, tiled=True)  12 us
    pallas_call x1, Pallas kernels, operators(): pl.pallas_call(functools.partial(operators_kernel, points, group), in_spe...  9.65 us
  transfers between devices with their start and end apart: 12, of which 2 were waited for; matrix products, arithmetic and copies ran while one was open for 0% of the time, Pallas kernels for 34%

profile of v3, /device:TPU:0, one launch (start us, length us, event | category | flops | bytes accessed | tf_op | source)
XLA Modules:
  0.0 212.1 jit_solution(15259444236145871238)
XLA Ops:
  0.6 0.5 collective-permute-start
  1.1 2.8 %split_rows.2 = f32[8,192,512]{2,1,0:T(8,128)} custom-call(f32[8,256,512]{2,1,0:T(8,128)} %bitcast.17), custom_call_target="tpu_custom_call" | custom-call | bytes 6291456 | tf_op jit(solution)/shard_map/split_rows/pallas_call | solution.py:138
  3.9 0.9 collective-permute-start.3
  4.8 5.3 %collective-permute-start.1 = (f32[8,192,512]{2,1,0:T(8,128)}, f32[8,192,512]{2,1,0:T(8,128)}, u32[]{:S(2)}, u32[]{:S(2)}) collective-permute-start(f32[8,192,512]{2,1,0:T(8,128)} %split_rows.2), channel_id=1, source_target_pairs={{0,8},{8,0},{16,24},{24,16},{1,9},{9,1},{17,25},{25,17},{2,10},{10... | collective-permute-start | bytes 9437192 | tf_op jit(solution)/shard_map/ppermute | solution.py:33
  10.1 2.1 split_rows.3
  12.2 1.6 collective-permute-start.4
  14.0 2.2 %copy-done = f32[1,8,8,4,8,512]{5,4,3,2,1,0:T(8,128)S(1)} copy-done((f32[1,8,8,4,8,512]{5,4,3,2,1,0:T(8,128)S(1)}, f32[1,8,8,4,8,512]{5,4,3,2,1,0:T(8,128)}, u32[]{:S(2)}) %copy-start) | copy-done | bytes 4194328
  16.2 1.0 copy-done.12
  17.2 2.6 %resident.1 = (f32[8,128]{1,0:T(8,128)S(1)}, f32[8,256,512]{2,1,0:T(8,128)S(1)}, f32[256,512]{1,0:T(8,128)S(1)}) custom-call(f32[8,256,512]{2,1,0:T(8,128)S(1)} %bitcast.19, f32[256,512]{1,0:T(8,128)S(1)} %bitcast.23, f32[8,256,512]{2,1,0:T(8,128)} %collective-permute-done.refs_1_.refs_0_), custom_call_target="tpu_custom_call" | custom-call | flops 9437184 | bytes 8388608 | tf_op jit(solution)/shard_map/resident/pallas_call | solution.py:98
  19.8 2.0 copy-done.3
  21.8 0.8 copy-done.10
  22.6 5.7 %all-to-all-start = ((f32[8,256,512]{2,1,0:T(8,128)}), f32[8,256,512]{2,1,0:T(8,128)}, u32[]{:S(2)}, u32[]{:S(2)}) async-start(f32[8,256,512]{2,1,0:T(8,128)} %copy-done.3), calls=%async_computation | async-start | bytes 8388608 | tf_op jit(solution)/shard_map/all_to_all | solution.py:701
  28.3 2.2 %copy-done.1 = f32[1,8,8,4,8,512]{5,4,3,2,1,0:T(8,128)S(1)} copy-done((f32[1,8,8,4,8,512]{5,4,3,2,1,0:T(8,128)S(1)}, f32[1,8,8,4,8,512]{5,4,3,2,1,0:T(8,128)}, u32[]{:S(2)}) %copy-start.1) | copy-done | bytes 4194328
  30.5 7.6 %crossing.1.refs_0_.__1_ = f32[8,256,512]{2,1,0:T(8,128)} custom-call(s32[3]{0:T(128)S(1)} %pad_add_fusion.at_ref, f32[16,16]{1,0:T(8,128)S(1)} %copy-done.16, f32[8,256,512]{2,1,0:T(8,128)S(1)} %bitcast.20, f32[8,256,512]{2,1,0:T(8,128)} %collective-permute-done.refs_1_.refs_0_), custom_call_target="tpu_custom_call" | custom-call | flops 16777216 | bytes 12582912 | tf_op jit(solution)/shard_map/crossing/pallas_call | solution.py:285
  38.1 1.5 collective-permute-start.5
  39.7 9.7 %operators.1 = (f32[2,256,256]{2,1,0:T(8,128)S(1)}, f32[512,512]{1,0:T(8,128)S(1)}, f32[512,512]{1,0:T(8,128)S(1)}, f32[2,256,256]{2,1,0:T(8,128)S(1)}) custom-call(s32[3]{0:T(128)S(1)} %pad_add_fusion.at_ref, f32[2,4]{1,0:T(2,128)S(1)} %copy-done.23, f32[16,16]{1,0:T(8,128)S(1)} %copy-done.17, f32[16,16]{1,0:T(8,128)S(1)} %copy-done.16, ...), custom_call_target="tpu_custom_call" | custom-call | flops 500000000 | bytes 4000000 | tf_op jit(solution)/shard_map/operators/pallas_call | solution.py:232
  49.3 0.8 copy-done.14
  50.2 1.0 copy-done.25
  51.1 1.0 copy-done.27
  52.1 0.8 copy-done.30
  52.9 1.7 copy-done.8
  54.7 26.6 %collective-permute-start.6 = (f32[8,192,512]{2,1,0:T(8,128)}, f32[8,192,512]{2,1,0:T(8,128)S(1)}, u32[]{:S(2)}, u32[]{:S(2)}) collective-permute-start(f32[8,192,512]{2,1,0:T(8,128)} %handed_on.3.refs_2_), channel_id=1, source_target_pairs={{0,8},{8,0},{16,24},{24,16},{1,9},{9,1},{17,25},{25,17},{2,10},{10... | collective-permute-start | bytes 9437192 | tf_op jit(solution)/shard_map/ppermute | solution.py:33
  81.3 2.3 %collective-permute-start.7 = (f32[8,192,512]{2,1,0:T(8,128)}, f32[8,192,512]{2,1,0:T(8,128)}, u32[]{:S(2)}, u32[]{:S(2)}) collective-permute-start(f32[8,192,512]{2,1,0:T(8,128)} %handed_on.2.refs_0_), channel_id=1, source_target_pairs={{8,16},{16,8},{9,17},{17,9},{10,18},{18,10},{11,19},{19,11},{12,20... | collective-permute-start | bytes 9437192 | tf_op jit(solution)/shard_map/ppermute | solution.py:33
  83.6 1.2 copy-done.28
  84.8 8.8 %mode_kinetic.1 = f32[2,4,256,512]{3,2,1,0:T(8,128)S(1)} custom-call(f32[2,4,256,512]{3,2,1,0:T(8,128)} %bitcast.12.in_ref, f32[512,512]{1,0:T(8,128)S(1)} %copy-done.28), custom_call_target="tpu_custom_call" | custom-call | flops 6442450944 | bytes 8388608 | tf_op jit(solution)/shard_map/mode_kinetic/pallas_call | solution.py:356
  93.6 2.0 copy-done.5
  95.6 5.7 %all-to-all-start.1 = ((f32[8,256,512]{2,1,0:T(8,128)}), f32[8,256,512]{2,1,0:T(8,128)}, u32[]{:S(2)}, u32[]{:S(2)}) async-start(f32[8,256,512]{2,1,0:T(8,128)} %bitcast.22), calls=%async_computation.1 | async-start | bytes 8388608 | tf_op jit(solution)/shard_map/all_to_all | solution.py:703
  101.3 0.6 constant_dynamic-slice_fusion.1
  104.6 1.2 collective-permute-start.8
  105.8 1.6 collective-permute-start.9
  107.5 2.2 %copy-done.2 = f32[1,8,8,4,8,512]{5,4,3,2,1,0:T(8,128)S(1)} copy-done((f32[1,8,8,4,8,512]{5,4,3,2,1,0:T(8,128)S(1)}, f32[1,8,8,4,8,512]{5,4,3,2,1,0:T(8,128)}, u32[]{:S(2)}) %copy-start.2) | copy-done | bytes 4194328
  109.7 2.2 %copy-done.24 = f32[1,8,8,4,8,512]{5,4,3,2,1,0:T(8,128)S(1)} copy-done((f32[1,8,8,4,8,512]{5,4,3,2,1,0:T(8,128)S(1)}, f32[1,8,8,4,8,512]{5,4,3,2,1,0:T(8,128)}, u32[]{:S(2)}) %copy-start.24) | copy-done | bytes 4194328
  111.9 1.2 copy-done.26
  113.1 1.0 copy-done.29
  114.1 1.0 copy-done.31
  115.2 18.1 %local_terms.1.work_ref = f32[8,256,512]{2,1,0:T(8,128)S(1)} custom-call(s32[3]{0:T(128)S(1)} %pad_add_fusion.at_ref, f32[4]{0:T(128)S(1)} %copy-done.33, f32[8,8]{1,0:T(8,128)S(1)} %copy-done.32, f32[8,256,512]{2,1,0:T(8,128)S(1)} %bitcast.21, f32[8,256,512]{2,1,0:T(8,128)} %collective-permute-done.refs_1_.refs_0_, f32[8,256,512]{2,1,0:T(8,128)S(1)} %bitcast.26, ...), custom_call_target="tpu_custom_call" | custom-call | flops 12884901888 | bytes 16777216 | tf_op jit(solution)/shard_map/local_terms/pallas_call | solution.py:321
  133.3 2.0 copy-done.6
  135.3 13.0 %all-to-all-done.1.refs_4_ = f32[8,256,512]{2,1,0:T(8,128)} async-done(((f32[8,256,512]{2,1,0:T(8,128)}), f32[8,256,512]{2,1,0:T(8,128)}, u32[]{:S(2)}, u32[]{:S(2)}) %all-to-all-start.1) | async-done | bytes 4194336 | tf_op jit(solution)/shard_map/all_to_all | solution.py:703
  148.3 2.2 %copy-done.7 = f32[8,256,512]{2,1,0:T(8,128)S(1)} copy-done((f32[8,256,512]{2,1,0:T(8,128)S(1)}, f32[8,256,512]{2,1,0:T(8,128)}, u32[]{:S(2)}) %copy-start.7) | copy-done | bytes 4194328
  150.5 1.9 copy-done.9
  152.4 1.0 copy-done.13
  153.4 1.0 copy-done.15
  154.5 15.3 %join_terms.1.work_ref = f32[8,256,512]{2,1,0:T(8,128)S(1)} custom-call(s32[3]{0:T(128)S(1)} %pad_add_fusion.at_ref, f32[8,256,512]{2,1,0:T(8,128)S(1)} %copy-done.7, f32[256,512]{1,0:T(8,128)S(1)} %bitcast.24, f32[2,256,256]{2,1,0:T(8,128)S(1)} %copy-done.15, f32[8,192,512]{2,1,0:T(8,128)} %handed_on.2.refs_0_, ...), custom_call_target="tpu_custom_call" | custom-call | flops 6442450944 | bytes 25165824 | tf_op jit(solution)/shard_map/join_terms/pallas_call | solution.py:400
  169.8 5.9 %far_terms.2 = (f32[8,256,512]{2,1,0:T(8,128)S(1)}, f32[1,8,128]{2,1,0:T(8,128)S(1)}) custom-call(f32[2]{0:T(128)S(1)} %pad_maximum_fusion.coef_ref, f32[8,256,512]{2,1,0:T(8,128)S(1)} %join_terms.1.work_ref, f32[8,192,512]{2,1,0:T(8,128)S(1)} %collective-permute-done.6.first_ref, ...), custom_call_target="tpu_custom_call", output_to_operand_aliasing={{0}: (1, {})} | custom-call | flops 18874368 | bytes 15728640 | tf_op jit(solution)/shard_map/far_terms/pallas_call | solution.py:467
  175.7 15.5 %collective-permute-done.8.first_ref = f32[8,64,512]{2,1,0:T(8,128)} collective-permute-done((f32[8,64,512]{2,1,0:T(8,128)}, f32[8,64,512]{2,1,0:T(8,128)}, u32[]{:S(2)}, u32[]{:S(2)}) %collective-permute-start.8) | collective-permute-done | bytes 1048608 | tf_op jit(solution)/shard_map/ppermute | solution.py:33
  191.2 2.6 %far_terms.3 = (f32[8,256,512]{2,1,0:T(8,128)S(1)}, f32[32,8,128]{2,1,0:T(8,128)S(1)}) custom-call(f32[2]{0:T(128)S(1)} %pad_maximum_fusion.coef_ref, f32[8,256,512]{2,1,0:T(8,128)S(1)} %get-tuple-element.24.work_ref, f32[8,64,512]{2,1,0:T(8,128)} %collective-permute-done.8.first_ref, ...), custom_call_target="tpu_custom_call", output_to_operand_aliasing={{0}: (1, {})} | custom-call | flops 6291456 | bytes 5242880 | tf_op jit(solution)/shard_map/far_terms/pallas_call | solution.py:467
  193.8 12.0 %all_to_all.15.sum_ref = f32[32,8,128]{2,1,0:T(8,128)S(1)} all-to-all(f32[32,8,128]{2,1,0:T(8,128)S(1)} %get-tuple-element.26), channel_id=1, replica_groups=mesh['ka'=4,'mode'=2,'row'=4] {'ka','mode','row'}, dimensions={0} | all-to-all | bytes 262144 | tf_op jit(solution)/shard_map/all_to_all | solution.py:731
  205.8 6.1 %basis.1 = (f32[8,256,512]{2,1,0:T(8,128)}, f32[8,8]{1,0:T(8,128)}, f32[8,8]{1,0:T(8,128)}) custom-call(f32[32,8,128]{2,1,0:T(8,128)S(1)} %all_to_all.15.sum_ref, f32[8,256,512]{2,1,0:T(8,128)S(1)} %get-tuple-element.27.work_ref, f32[8,256,512]{2,1,0:T(8,128)S(1)} %copy-done.4), custom_call_target="tpu_custom_call" | custom-call | flops 33554432 | bytes 12582912 | tf_op jit(solution)/shard_map/basis/pallas_call | solution.py:610
  (61 shorter events, 0.4 us)
Async XLA Ops:
  0.6 13.3 %collective-permute-start = (f32[8,256,512]{2,1,0:T(8,128)}, f32[8,256,512]{2,1,0:T(8,128)}, u32[]{:S(2)}, u32[]{:S(2)}) collective-permute-start(f32[8,256,512]{2,1,0:T(8,128)} %bitcast.16), channel_id=1, source_target_pairs={{0,1},{1,0},{2,3},{3,2},{4,5},{5,4},{6,7},{7,6},{8,9},{9,8},{10,11... | collective-permute-start | bytes 12582920 | tf_op jit(solution)/shard_map/ppermute | solution.py:666
  3.9 49.0 %collective-permute-start.3 = (f32[8,192,512]{2,1,0:T(8,128)}, f32[8,192,512]{2,1,0:T(8,128)S(1)}, u32[]{:S(2)}, u32[]{:S(2)}) collective-permute-start(f32[8,192,512]{2,1,0:T(8,128)} %split_rows.2), channel_id=1, source_target_pairs={{8,16},{16,8},{9,17},{17,9},{10,18},{18,10},{11,19},{19,11},{12,20... | collective-permute-start | bytes 9437192 | tf_op jit(solution)/shard_map/ppermute | solution.py:33
  4.8 76.5 %collective-permute-start.1 = (f32[8,192,512]{2,1,0:T(8,128)}, f32[8,192,512]{2,1,0:T(8,128)}, u32[]{:S(2)}, u32[]{:S(2)}) collective-permute-start(f32[8,192,512]{2,1,0:T(8,128)} %split_rows.2), channel_id=1, source_target_pairs={{0,8},{8,0},{16,24},{24,16},{1,9},{9,1},{17,25},{25,17},{2,10},{10... | collective-permute-start | bytes 9437192 | tf_op jit(solution)/shard_map/ppermute | solution.py:33
  12.2 93.7 %collective-permute-start.2 = (f32[8,64,512]{2,1,0:T(8,128)}, f32[8,64,512]{2,1,0:T(8,128)}, u32[]{:S(2)}, u32[]{:S(2)}) collective-permute-start(f32[8,64,512]{2,1,0:T(8,128)} %split_rows.3), channel_id=1, source_target_pairs={{0,8},{8,0},{16,24},{24,16},{1,9},{9,1},{17,25},{25,17},{2,10},{10... | collective-permute-start | bytes 3145736 | tf_op jit(solution)/shard_map/ppermute | solution.py:33
  12.2 92.4 %collective-permute-start.4 = (f32[8,64,512]{2,1,0:T(8,128)}, f32[8,64,512]{2,1,0:T(8,128)}, u32[]{:S(2)}, u32[]{:S(2)}) collective-permute-start(f32[8,64,512]{2,1,0:T(8,128)} %split_rows.3), channel_id=1, source_target_pairs={{8,16},{16,8},{9,17},{17,9},{10,18},{18,10},{11,19},{19,11},{12,20... | collective-permute-start | bytes 3145736 | tf_op jit(solution)/shard_map/ppermute | solution.py:33
  14.0 2.2 %copy-start = (f32[1,8,8,4,8,512]{5,4,3,2,1,0:T(8,128)S(1)}, f32[1,8,8,4,8,512]{5,4,3,2,1,0:T(8,128)}, u32[]{:S(2)}) copy-start(f32[1,8,8,4,8,512]{5,4,3,2,1,0:T(8,128)} %param.15) | copy-start | bytes 12582916
  16.2 1.0 copy-start.12
  19.8 2.0 copy-start.3
  21.8 0.8 copy-start.10
  22.6 5.7 %copy-start.16 = (f32[16,16]{1,0:T(8,128)S(1)}, f32[16,16]{1,0:T(8,128)}, u32[]{:S(2)}) copy-start(f32[16,16]{1,0:T(8,128)} %two_ref.3) | copy-start | bytes 3076
  22.6 61.0 %all-to-all-start = ((f32[8,256,512]{2,1,0:T(8,128)}), f32[8,256,512]{2,1,0:T(8,128)}, u32[]{:S(2)}, u32[]{:S(2)}) async-start(f32[8,256,512]{2,1,0:T(8,128)} %copy-done.3), calls=%async_computation | async-start | bytes 8388608 | tf_op jit(solution)/shard_map/all_to_all | solution.py:701
  28.3 2.2 %copy-start.1 = (f32[1,8,8,4,8,512]{5,4,3,2,1,0:T(8,128)S(1)}, f32[1,8,8,4,8,512]{5,4,3,2,1,0:T(8,128)}, u32[]{:S(2)}) copy-start(f32[1,8,8,4,8,512]{5,4,3,2,1,0:T(8,128)} %param.15) | copy-start | bytes 12582916
  30.5 9.2 %copy-start.17 = (f32[16,16]{1,0:T(8,128)S(1)}, f32[16,16]{1,0:T(8,128)}, u32[]{:S(2)}) copy-start(f32[16,16]{1,0:T(8,128)} %one_ref.1) | copy-start | bytes 3076
  30.5 9.2 %copy-start.18 = (f32[8,8]{1,0:T(8,128)S(1)}, f32[8,8]{1,0:T(8,128)}, u32[]{:S(2)}) copy-start(f32[8,8]{1,0:T(8,128)} %three_ref.1) | copy-start | bytes 772
  30.5 9.2 %copy-start.19 = (f32[8,8]{1,0:T(8,128)S(1)}, f32[8,8]{1,0:T(8,128)}, u32[]{:S(2)}) copy-start(f32[8,8]{1,0:T(8,128)} %four_ref.1) | copy-start | bytes 772
  30.5 9.2 %copy-start.20 = (f32[8,8]{1,0:T(8,128)S(1)}, f32[8,8]{1,0:T(8,128)}, u32[]{:S(2)}) copy-start(f32[8,8]{1,0:T(8,128)} %five_ref.1) | copy-start | bytes 772
  30.5 9.2 %copy-start.21 = (f32[8,8]{1,0:T(8,128)S(1)}, f32[8,8]{1,0:T(8,128)}, u32[]{:S(2)}) copy-start(f32[8,8]{1,0:T(8,128)} %six_ref.1) | copy-start | bytes 772
  30.5 9.2 %copy-start.22 = (f32[8,8]{1,0:T(8,128)S(1)}, f32[8,8]{1,0:T(8,128)}, u32[]{:S(2)}) copy-start(f32[8,8]{1,0:T(8,128)} %der_ref.1) | copy-start | bytes 772
  30.5 9.1 %copy-start.23 = (f32[2,4]{1,0:T(2,128)S(1)}, f32[2,4]{1,0:T(2,128)}, u32[]{:S(2)}) copy-start(f32[2,4]{1,0:T(2,128)} %coupling_ref.1) | copy-start | bytes 100
  38.1 110.1 %collective-permute-start.5 = (f32[8,256,512]{2,1,0:T(8,128)}, f32[8,256,512]{2,1,0:T(8,128)}, u32[]{:S(2)}, u32[]{:S(2)}) collective-permute-start(f32[8,256,512]{2,1,0:T(8,128)} %crossing.1.refs_0_.__1_), channel_id=1, source_target_pairs={{0,2},{1,3},{2,0},{3,1},{4,6},{5,7},{6,4},{7,5},{8,10},{9,11},{10,... | collective-permute-start | bytes 12582920 | tf_op jit(solution)/shard_map/ppermute | solution.py:670
  49.3 0.8 copy-start.14
  50.2 1.0 copy-start.25
  51.1 1.0 copy-start.27
  52.1 0.8 copy-start.30
  52.9 1.8 copy-start.8
  54.7 115.1 %collective-permute-start.6 = (f32[8,192,512]{2,1,0:T(8,128)}, f32[8,192,512]{2,1,0:T(8,128)S(1)}, u32[]{:S(2)}, u32[]{:S(2)}) collective-permute-start(f32[8,192,512]{2,1,0:T(8,128)} %handed_on.3.refs_2_), channel_id=1, source_target_pairs={{0,8},{8,0},{16,24},{24,16},{1,9},{9,1},{17,25},{25,17},{2,10},{10... | collective-permute-start | bytes 9437192 | tf_op jit(solution)/shard_map/ppermute | solution.py:33
  81.3 88.5 %collective-permute-start.7 = (f32[8,192,512]{2,1,0:T(8,128)}, f32[8,192,512]{2,1,0:T(8,128)}, u32[]{:S(2)}, u32[]{:S(2)}) collective-permute-start(f32[8,192,512]{2,1,0:T(8,128)} %handed_on.2.refs_0_), channel_id=1, source_target_pairs={{8,16},{16,8},{9,17},{17,9},{10,18},{18,10},{11,19},{19,11},{12,20... | collective-permute-start | bytes 9437192 | tf_op jit(solution)/shard_map/ppermute | solution.py:33
  83.6 1.2 copy-start.28
  93.6 2.0 copy-start.5
  95.6 11.9 %copy-start.32 = (f32[8,8]{1,0:T(8,128)S(1)}, f32[8,8]{1,0:T(8,128)}, u32[]{:S(2)}) copy-start(f32[8,8]{1,0:T(8,128)} %beta_ref.1) | copy-start | bytes 772
  95.6 11.9 %copy-start.33 = (f32[4]{0:T(128)S(1)}, f32[4]{0:T(128)}, u32[]{:S(2)}) copy-start(f32[4]{0:T(128)} %rot_ref.1) | copy-start | bytes 52
  95.6 52.7 %all-to-all-start.1 = ((f32[8,256,512]{2,1,0:T(8,128)}), f32[8,256,512]{2,1,0:T(8,128)}, u32[]{:S(2)}, u32[]{:S(2)}) async-start(f32[8,256,512]{2,1,0:T(8,128)} %bitcast.22), calls=%async_computation.1 | async-start | bytes 8388608 | tf_op jit(solution)/shard_map/all_to_all | solution.py:703
  104.6 86.6 %collective-permute-start.8 = (f32[8,64,512]{2,1,0:T(8,128)}, f32[8,64,512]{2,1,0:T(8,128)}, u32[]{:S(2)}, u32[]{:S(2)}) collective-permute-start(f32[8,64,512]{2,1,0:T(8,128)} %collective-permute-done.4.refs_3_), channel_id=1, source_target_pairs={{0,8},{8,0},{16,24},{24,16},{1,9},{9,1},{17,25},{25,17},{2,10},{10... | collective-permute-start | bytes 3145736 | tf_op jit(solution)/shard_map/ppermute | solution.py:33
  105.8 85.4 %collective-permute-start.9 = (f32[8,64,512]{2,1,0:T(8,128)}, f32[8,64,512]{2,1,0:T(8,128)}, u32[]{:S(2)}, u32[]{:S(2)}) collective-permute-start(f32[8,64,512]{2,1,0:T(8,128)} %collective-permute-done.2.refs_1_), channel_id=1, source_target_pairs={{8,16},{16,8},{9,17},{17,9},{10,18},{18,10},{11,19},{19,11},{12,20... | collective-permute-start | bytes 3145736 | tf_op jit(solution)/shard_map/ppermute | solution.py:33
  107.5 2.2 %copy-start.2 = (f32[1,8,8,4,8,512]{5,4,3,2,1,0:T(8,128)S(1)}, f32[1,8,8,4,8,512]{5,4,3,2,1,0:T(8,128)}, u32[]{:S(2)}) copy-start(f32[1,8,8,4,8,512]{5,4,3,2,1,0:T(8,128)} %param.15) | copy-start | bytes 12582916
  109.7 2.2 %copy-start.24 = (f32[1,8,8,4,8,512]{5,4,3,2,1,0:T(8,128)S(1)}, f32[1,8,8,4,8,512]{5,4,3,2,1,0:T(8,128)}, u32[]{:S(2)}) copy-start(f32[1,8,8,4,8,512]{5,4,3,2,1,0:T(8,128)} %param.16) | copy-start | bytes 12582916
  111.9 1.2 copy-start.26
  113.1 1.0 copy-start.29
  114.1 1.0 copy-start.31
  133.3 2.0 copy-start.6
  148.3 2.2 %copy-start.7 = (f32[8,256,512]{2,1,0:T(8,128)S(1)}, f32[8,256,512]{2,1,0:T(8,128)}, u32[]{:S(2)}) copy-start(f32[8,256,512]{2,1,0:T(8,128)} %copy-done.6) | copy-start | bytes 12582916
  150.5 1.9 copy-start.9
  152.4 1.0 copy-start.13
  153.4 1.0 copy-start.15
  154.5 15.4 %copy-start.4 = (f32[8,256,512]{2,1,0:T(8,128)S(1)}, f32[8,256,512]{2,1,0:T(8,128)}, u32[]{:S(2)}) copy-start(f32[8,256,512]{2,1,0:T(8,128)} %copy-done.3) | copy-start | bytes 12582916
  154.5 15.4 %copy-start.11 = (f32[256,512]{1,0:T(8,128)S(1)}, f32[256,512]{1,0:T(8,128)}, u32[]{:S(2)}) copy-start(f32[256,512]{1,0:T(8,128)} %copy-done.10) | copy-start | bytes 1572868

commit v4 on v3

--- a/solution.py
+++ b/solution.py
@@ -25,12 +25,21 @@
     return pl.BlockSpec(shape, lambda *_: (0,) * len(shape))
 
 
+def pairing(peers, first):
+    return [(low, low + 1) for low in range(first, peers - 1, 2)]
+
+
 def pair_exchange(value, axis, first):
+    pairs = pairing(lax.axis_size(axis), first)
+    return lax.ppermute(value, axis, pairs + [(high, low) for low, high in pairs])
+
+
+def pair_forward(value, axis, first):
     peers = lax.axis_size(axis)
-    pairs = []
-    for low in range(first, peers - 1, 2):
-        pairs += [(low, low + 1), (low + 1, low)]
-    return lax.ppermute(value, axis, pairs)
+    holders = {member for pair in pairing(peers, 1 - first) for member in pair}
+    pairs = pairing(peers, first)
+    pairs = pairs + [(high, low) for low, high in pairs]
+    return lax.ppermute(value, axis, [pair for pair in pairs if pair[0] in holders])
 
 
 def vector_groups(nvec):
@@ -687,8 +696,8 @@
     )
     near_first[0] = handed_on(near_first[0], HOP_WEIGHT, [*row_parts, mode_mat])
     near_second[0] = handed_on(near_second[0], HOP_WEIGHT, [*row_parts, mode_mat])
-    far_first = [pair_exchange(part, "ka", 0) for part in near_second]
-    far_second = [pair_exchange(part, "ka", 1) for part in near_first]
+    far_first = [pair_forward(part, "ka", 0) for part in near_second]
+    far_second = [pair_forward(part, "ka", 1) for part in near_first]
     lower_two = jnp.maximum(block_index - 2, 0)
     far_above, far_below = coupling[1, block_index], coupling[1, lower_two]
     even = block_index % 2 == 0

time: 213 us -> 213 us (level)
  waiting for transfers between devices: 28.5 us -> 53.7 us
  starting transfers between devices: 53 us -> 27.8 us
    ppermute x8, starting transfers between devices: 39.6 us -> 14.4 us  [the longest x4 7.87 us: pair_exchange(): lax.ppermute(value, axis, pairs + [(high, low) for low, high in pairs])]
    ppermute x8, waiting for transfers between devices: 15.5 us -> 40.6 us  [the longest x4 23.3 us: pair_exchange(): lax.ppermute(value, axis, pairs + [(high, low) for low, high in pairs])]
  transfers between devices with their start and end apart: 12 -> 12, of which waited for: 2 -> 4; matrix products, arithmetic and copies ran while one was open for 0% -> 0% of each run, Pallas kernels for 34% -> 34%
where the time goes in v4:
time: 213 us; the launch traced here: 212 us
  Pallas kernels  81.6 us (38%)
  waiting for transfers between devices  53.7 us (25%)
  local copies, waits for them, and re-layouts  33.2 us (16%)
  starting transfers between devices  27.8 us (13%)
  blocking collectives  11.7 us (5%)
  between operations  3.65 us (2%)
    unnamed x68, local copies, waits for them, and re-layouts  32.6 us
    ppermute x4, waiting for transfers between devices, pair_exchange(): lax.ppermute(value, axis, pairs + [(high, low) for low, high in pairs])  23.3 us
    pallas_call x1, Pallas kernels, local_terms(): pl.pallas_call(functools.partial(local_kernel, nvec, nblocks, len(held)),...  18.1 us
    ppermute x4, waiting for transfers between devices, pair_forward(): lax.ppermute(value, axis, [pair for pair in pairs if pair[0] in holders])  17.3 us
    pallas_call x1, Pallas kernels, join_terms(): pl.pallas_call(functools.partial(join_kernel, tuple(starts), len(sums)),...  15.3 us
    all_to_all x1, waiting for transfers between devices, shards(): lax.all_to_all(mode_shares, 'mode', split_axis=0, concat_axis=0, tiled=True)  13.1 us
    all_to_all x1, blocking collectives, shards(): lax.all_to_all(copied, ALL_AXES, split_axis=0, concat_axis=0, tiled=True)  11.7 us
    pallas_call x1, Pallas kernels, operators(): pl.pallas_call(functools.partial(operators_kernel, points, group), in_spe...  9.65 us
  transfers between devices with their start and end apart: 12, of which 4 were waited for; matrix products, arithmetic and copies ran while one was open for 0% of the time, Pallas kernels for 34%

profile of v4, /device:TPU:0, one launch (start us, length us, event | category | flops | bytes accessed | tf_op | source)
XLA Modules:
  0.0 211.8 jit_solution(13341054603699013981)
XLA Ops:
  1.1 2.8 %split_rows.2 = f32[8,192,512]{2,1,0:T(8,128)} custom-call(f32[8,256,512]{2,1,0:T(8,128)} %bitcast.17), custom_call_target="tpu_custom_call" | custom-call | bytes 6291456 | tf_op jit(solution)/shard_map/split_rows/pallas_call | solution.py:147
  3.9 0.9 collective-permute-start.3
  4.8 5.3 %collective-permute-start.1 = (f32[8,192,512]{2,1,0:T(8,128)}, f32[8,192,512]{2,1,0:T(8,128)}, u32[]{:S(2)}, u32[]{:S(2)}) collective-permute-start(f32[8,192,512]{2,1,0:T(8,128)} %split_rows.2), channel_id=1, source_target_pairs={{0,8},{16,24},{8,0},{24,16},{1,9},{17,25},{9,1},{25,17},{2,10},{18... | collective-permute-start | bytes 9437192 | tf_op jit(solution)/shard_map/ppermute | solution.py:34
  10.1 2.1 split_rows.3
  12.2 1.6 collective-permute-start.4
  14.0 2.2 %copy-done = f32[1,8,8,4,8,512]{5,4,3,2,1,0:T(8,128)S(1)} copy-done((f32[1,8,8,4,8,512]{5,4,3,2,1,0:T(8,128)S(1)}, f32[1,8,8,4,8,512]{5,4,3,2,1,0:T(8,128)}, u32[]{:S(2)}) %copy-start) | copy-done | bytes 4194328
  16.2 1.0 copy-done.12
  17.2 2.6 %resident.1 = (f32[8,128]{1,0:T(8,128)S(1)}, f32[8,256,512]{2,1,0:T(8,128)S(1)}, f32[256,512]{1,0:T(8,128)S(1)}) custom-call(f32[8,256,512]{2,1,0:T(8,128)S(1)} %bitcast.19, f32[256,512]{1,0:T(8,128)S(1)} %bitcast.23, f32[8,256,512]{2,1,0:T(8,128)} %collective-permute-done.refs_1_.refs_0_), custom_call_target="tpu_custom_call" | custom-call | flops 9437184 | bytes 8388608 | tf_op jit(solution)/shard_map/resident/pallas_call | solution.py:107
  19.8 2.0 copy-done.3
  21.8 0.8 copy-done.10
  22.6 5.7 %all-to-all-start = ((f32[8,256,512]{2,1,0:T(8,128)}), f32[8,256,512]{2,1,0:T(8,128)}, u32[]{:S(2)}, u32[]{:S(2)}) async-start(f32[8,256,512]{2,1,0:T(8,128)} %copy-done.3), calls=%async_computation | async-start | bytes 8388608 | tf_op jit(solution)/shard_map/all_to_all | solution.py:710
  28.3 2.2 %copy-done.1 = f32[1,8,8,4,8,512]{5,4,3,2,1,0:T(8,128)S(1)} copy-done((f32[1,8,8,4,8,512]{5,4,3,2,1,0:T(8,128)S(1)}, f32[1,8,8,4,8,512]{5,4,3,2,1,0:T(8,128)}, u32[]{:S(2)}) %copy-start.1) | copy-done | bytes 4194328
  30.5 7.6 %crossing.1.refs_0_.__1_ = f32[8,256,512]{2,1,0:T(8,128)} custom-call(s32[3]{0:T(128)S(1)} %pad_add_fusion.at_ref, f32[16,16]{1,0:T(8,128)S(1)} %copy-done.16, f32[8,256,512]{2,1,0:T(8,128)S(1)} %bitcast.20, f32[8,256,512]{2,1,0:T(8,128)} %collective-permute-done.refs_1_.refs_0_), custom_call_target="tpu_custom_call" | custom-call | flops 16777216 | bytes 12582912 | tf_op jit(solution)/shard_map/crossing/pallas_call | solution.py:294
  38.1 1.5 collective-permute-start.5
  39.7 9.7 %operators.1 = (f32[2,256,256]{2,1,0:T(8,128)S(1)}, f32[512,512]{1,0:T(8,128)S(1)}, f32[512,512]{1,0:T(8,128)S(1)}, f32[2,256,256]{2,1,0:T(8,128)S(1)}) custom-call(s32[3]{0:T(128)S(1)} %pad_add_fusion.at_ref, f32[2,4]{1,0:T(2,128)S(1)} %copy-done.23, f32[16,16]{1,0:T(8,128)S(1)} %copy-done.17, f32[16,16]{1,0:T(8,128)S(1)} %copy-done.16, ...), custom_call_target="tpu_custom_call" | custom-call | flops 500000000 | bytes 4000000 | tf_op jit(solution)/shard_map/operators/pallas_call | solution.py:241
  49.3 0.8 copy-done.14
  50.2 1.0 copy-done.25
  51.1 1.0 copy-done.27
  52.1 0.8 copy-done.30
  52.9 1.7 copy-done.8
  54.7 1.3 collective-permute-start.6
  56.0 23.3 %collective-permute-done.1.__0_ = f32[8,192,512]{2,1,0:T(8,128)} collective-permute-done((f32[8,192,512]{2,1,0:T(8,128)}, f32[8,192,512]{2,1,0:T(8,128)}, u32[]{:S(2)}, u32[]{:S(2)}) %collective-permute-start.1) | collective-permute-done | bytes 3145760 | tf_op jit(solution)/shard_map/ppermute | solution.py:34
  79.3 2.3 %collective-permute-start.7 = (f32[8,192,512]{2,1,0:T(8,128)}, f32[8,192,512]{2,1,0:T(8,128)}, u32[]{:S(2)}, u32[]{:S(2)}) collective-permute-start(f32[8,192,512]{2,1,0:T(8,128)} %handed_on.2.refs_0_), channel_id=1, source_target_pairs={{8,16},{16,8},{9,17},{17,9},{10,18},{18,10},{11,19},{19,11},{12,20... | collective-permute-start | bytes 9437192 | tf_op jit(solution)/shard_map/ppermute | solution.py:42
  81.6 1.2 copy-done.28
  82.8 8.8 %mode_kinetic.1 = f32[2,4,256,512]{3,2,1,0:T(8,128)S(1)} custom-call(f32[2,4,256,512]{3,2,1,0:T(8,128)} %bitcast.12.in_ref, f32[512,512]{1,0:T(8,128)S(1)} %copy-done.28), custom_call_target="tpu_custom_call" | custom-call | flops 6442450944 | bytes 8388608 | tf_op jit(solution)/shard_map/mode_kinetic/pallas_call | solution.py:365
  91.6 2.0 copy-done.5
  93.6 5.7 %all-to-all-start.1 = ((f32[8,256,512]{2,1,0:T(8,128)}), f32[8,256,512]{2,1,0:T(8,128)}, u32[]{:S(2)}, u32[]{:S(2)}) async-start(f32[8,256,512]{2,1,0:T(8,128)} %bitcast.22), calls=%async_computation.1 | async-start | bytes 8388608 | tf_op jit(solution)/shard_map/all_to_all | solution.py:712
  102.6 1.3 collective-permute-start.8
  103.9 1.7 collective-permute-start.9
  105.6 2.2 %copy-done.2 = f32[1,8,8,4,8,512]{5,4,3,2,1,0:T(8,128)S(1)} copy-done((f32[1,8,8,4,8,512]{5,4,3,2,1,0:T(8,128)S(1)}, f32[1,8,8,4,8,512]{5,4,3,2,1,0:T(8,128)}, u32[]{:S(2)}) %copy-start.2) | copy-done | bytes 4194328
  107.7 2.2 %copy-done.24 = f32[1,8,8,4,8,512]{5,4,3,2,1,0:T(8,128)S(1)} copy-done((f32[1,8,8,4,8,512]{5,4,3,2,1,0:T(8,128)S(1)}, f32[1,8,8,4,8,512]{5,4,3,2,1,0:T(8,128)}, u32[]{:S(2)}) %copy-start.24) | copy-done | bytes 4194328
  109.9 1.2 copy-done.26
  111.2 1.0 copy-done.29
  112.2 1.0 copy-done.31
  113.2 18.1 %local_terms.1.work_ref = f32[8,256,512]{2,1,0:T(8,128)S(1)} custom-call(s32[3]{0:T(128)S(1)} %pad_add_fusion.at_ref, f32[4]{0:T(128)S(1)} %copy-done.33, f32[8,8]{1,0:T(8,128)S(1)} %copy-done.32, f32[8,256,512]{2,1,0:T(8,128)S(1)} %bitcast.21, f32[8,256,512]{2,1,0:T(8,128)} %collective-permute-done.refs_1_.refs_0_, f32[8,256,512]{2,1,0:T(8,128)S(1)} %bitcast.26, ...), custom_call_target="tpu_custom_call" | custom-call | flops 12884901888 | bytes 16777216 | tf_op jit(solution)/shard_map/local_terms/pallas_call | solution.py:330
  131.4 2.0 copy-done.6
  133.4 13.1 %all-to-all-done.1.refs_4_ = f32[8,256,512]{2,1,0:T(8,128)} async-done(((f32[8,256,512]{2,1,0:T(8,128)}), f32[8,256,512]{2,1,0:T(8,128)}, u32[]{:S(2)}, u32[]{:S(2)}) %all-to-all-start.1) | async-done | bytes 4194336 | tf_op jit(solution)/shard_map/all_to_all | solution.py:712
  146.5 2.2 %copy-done.7 = f32[8,256,512]{2,1,0:T(8,128)S(1)} copy-done((f32[8,256,512]{2,1,0:T(8,128)S(1)}, f32[8,256,512]{2,1,0:T(8,128)}, u32[]{:S(2)}) %copy-start.7) | copy-done | bytes 4194328
  148.7 1.9 copy-done.9
  150.6 1.0 copy-done.13
  151.6 1.0 copy-done.15
  152.6 15.3 %join_terms.1.work_ref = f32[8,256,512]{2,1,0:T(8,128)S(1)} custom-call(s32[3]{0:T(128)S(1)} %pad_add_fusion.at_ref, f32[8,256,512]{2,1,0:T(8,128)S(1)} %copy-done.7, f32[256,512]{1,0:T(8,128)S(1)} %bitcast.24, f32[2,256,256]{2,1,0:T(8,128)S(1)} %copy-done.15, f32[8,192,512]{2,1,0:T(8,128)} %handed_on.2.refs_0_, ...), custom_call_target="tpu_custom_call" | custom-call | flops 6442450944 | bytes 25165824 | tf_op jit(solution)/shard_map/join_terms/pallas_call | solution.py:409
  168.0 1.1 collective-permute-done.6.first_ref
  169.0 5.9 %far_terms.2 = (f32[8,256,512]{2,1,0:T(8,128)S(1)}, f32[1,8,128]{2,1,0:T(8,128)S(1)}) custom-call(f32[2]{0:T(128)S(1)} %pad_maximum_fusion.coef_ref, f32[8,256,512]{2,1,0:T(8,128)S(1)} %join_terms.1.work_ref, f32[8,192,512]{2,1,0:T(8,128)S(1)} %collective-permute-done.6.first_ref, ...), custom_call_target="tpu_custom_call", output_to_operand_aliasing={{0}: (1, {})} | custom-call | flops 18874368 | bytes 15728640 | tf_op jit(solution)/shard_map/far_terms/pallas_call | solution.py:476
  175.0 16.2 %collective-permute-done.8.first_ref = f32[8,64,512]{2,1,0:T(8,128)} collective-permute-done((f32[8,64,512]{2,1,0:T(8,128)}, f32[8,64,512]{2,1,0:T(8,128)}, u32[]{:S(2)}, u32[]{:S(2)}) %collective-permute-start.8) | collective-permute-done | bytes 1048608 | tf_op jit(solution)/shard_map/ppermute | solution.py:42
  191.2 2.6 %far_terms.3 = (f32[8,256,512]{2,1,0:T(8,128)S(1)}, f32[32,8,128]{2,1,0:T(8,128)S(1)}) custom-call(f32[2]{0:T(128)S(1)} %pad_maximum_fusion.coef_ref, f32[8,256,512]{2,1,0:T(8,128)S(1)} %get-tuple-element.24.work_ref, f32[8,64,512]{2,1,0:T(8,128)} %collective-permute-done.8.first_ref, ...), custom_call_target="tpu_custom_call", output_to_operand_aliasing={{0}: (1, {})} | custom-call | flops 6291456 | bytes 5242880 | tf_op jit(solution)/shard_map/far_terms/pallas_call | solution.py:476
  193.8 11.7 %all_to_all.15.sum_ref = f32[32,8,128]{2,1,0:T(8,128)S(1)} all-to-all(f32[32,8,128]{2,1,0:T(8,128)S(1)} %get-tuple-element.26), channel_id=1, replica_groups=mesh['ka'=4,'mode'=2,'row'=4] {'ka','mode','row'}, dimensions={0} | all-to-all | bytes 262144 | tf_op jit(solution)/shard_map/all_to_all | solution.py:740
  205.5 6.1 %basis.1 = (f32[8,256,512]{2,1,0:T(8,128)}, f32[8,8]{1,0:T(8,128)}, f32[8,8]{1,0:T(8,128)}) custom-call(f32[32,8,128]{2,1,0:T(8,128)S(1)} %all_to_all.15.sum_ref, f32[8,256,512]{2,1,0:T(8,128)S(1)} %get-tuple-element.27.work_ref, f32[8,256,512]{2,1,0:T(8,128)S(1)} %copy-done.4), custom_call_target="tpu_custom_call" | custom-call | flops 33554432 | bytes 12582912 | tf_op jit(solution)/shard_map/basis/pallas_call | solution.py:619
  (61 shorter events, 1.5 us)
Async XLA Ops:
  0.6 13.3 %collective-permute-start = (f32[8,256,512]{2,1,0:T(8,128)}, f32[8,256,512]{2,1,0:T(8,128)}, u32[]{:S(2)}, u32[]{:S(2)}) collective-permute-start(f32[8,256,512]{2,1,0:T(8,128)} %bitcast.16), channel_id=1, source_target_pairs={{0,1},{1,0},{2,3},{3,2},{4,5},{5,4},{6,7},{7,6},{8,9},{9,8},{10,11... | collective-permute-start | bytes 12582920 | tf_op jit(solution)/shard_map/ppermute | solution.py:675
  3.9 49.0 %collective-permute-start.3 = (f32[8,192,512]{2,1,0:T(8,128)}, f32[8,192,512]{2,1,0:T(8,128)S(1)}, u32[]{:S(2)}, u32[]{:S(2)}) collective-permute-start(f32[8,192,512]{2,1,0:T(8,128)} %split_rows.2), channel_id=1, source_target_pairs={{8,16},{16,8},{9,17},{17,9},{10,18},{18,10},{11,19},{19,11},{12,20... | collective-permute-start | bytes 9437192 | tf_op jit(solution)/shard_map/ppermute | solution.py:34
  4.8 74.5 %collective-permute-start.1 = (f32[8,192,512]{2,1,0:T(8,128)}, f32[8,192,512]{2,1,0:T(8,128)}, u32[]{:S(2)}, u32[]{:S(2)}) collective-permute-start(f32[8,192,512]{2,1,0:T(8,128)} %split_rows.2), channel_id=1, source_target_pairs={{0,8},{16,24},{8,0},{24,16},{1,9},{17,25},{9,1},{25,17},{2,10},{18... | collective-permute-start | bytes 9437192 | tf_op jit(solution)/shard_map/ppermute | solution.py:34
  12.2 91.7 %collective-permute-start.2 = (f32[8,64,512]{2,1,0:T(8,128)}, f32[8,64,512]{2,1,0:T(8,128)}, u32[]{:S(2)}, u32[]{:S(2)}) collective-permute-start(f32[8,64,512]{2,1,0:T(8,128)} %split_rows.3), channel_id=1, source_target_pairs={{0,8},{16,24},{8,0},{24,16},{1,9},{17,25},{9,1},{25,17},{2,10},{18... | collective-permute-start | bytes 3145736 | tf_op jit(solution)/shard_map/ppermute | solution.py:34
  12.2 90.4 %collective-permute-start.4 = (f32[8,64,512]{2,1,0:T(8,128)}, f32[8,64,512]{2,1,0:T(8,128)}, u32[]{:S(2)}, u32[]{:S(2)}) collective-permute-start(f32[8,64,512]{2,1,0:T(8,128)} %split_rows.3), channel_id=1, source_target_pairs={{8,16},{16,8},{9,17},{17,9},{10,18},{18,10},{11,19},{19,11},{12,20... | collective-permute-start | bytes 3145736 | tf_op jit(solution)/shard_map/ppermute | solution.py:34
  14.0 2.2 %copy-start = (f32[1,8,8,4,8,512]{5,4,3,2,1,0:T(8,128)S(1)}, f32[1,8,8,4,8,512]{5,4,3,2,1,0:T(8,128)}, u32[]{:S(2)}) copy-start(f32[1,8,8,4,8,512]{5,4,3,2,1,0:T(8,128)} %param.15) | copy-start | bytes 12582916
  16.2 1.0 copy-start.12
  19.8 2.0 copy-start.3
  21.8 0.8 copy-start.10
  22.6 5.7 %copy-start.16 = (f32[16,16]{1,0:T(8,128)S(1)}, f32[16,16]{1,0:T(8,128)}, u32[]{:S(2)}) copy-start(f32[16,16]{1,0:T(8,128)} %two_ref.3) | copy-start | bytes 3076
  22.6 59.0 %all-to-all-start = ((f32[8,256,512]{2,1,0:T(8,128)}), f32[8,256,512]{2,1,0:T(8,128)}, u32[]{:S(2)}, u32[]{:S(2)}) async-start(f32[8,256,512]{2,1,0:T(8,128)} %copy-done.3), calls=%async_computation | async-start | bytes 8388608 | tf_op jit(solution)/shard_map/all_to_all | solution.py:710
  28.3 2.2 %copy-start.1 = (f32[1,8,8,4,8,512]{5,4,3,2,1,0:T(8,128)S(1)}, f32[1,8,8,4,8,512]{5,4,3,2,1,0:T(8,128)}, u32[]{:S(2)}) copy-start(f32[1,8,8,4,8,512]{5,4,3,2,1,0:T(8,128)} %param.15) | copy-start | bytes 12582916
  30.5 9.2 %copy-start.17 = (f32[16,16]{1,0:T(8,128)S(1)}, f32[16,16]{1,0:T(8,128)}, u32[]{:S(2)}) copy-start(f32[16,16]{1,0:T(8,128)} %one_ref.1) | copy-start | bytes 3076
  30.5 9.2 %copy-start.18 = (f32[8,8]{1,0:T(8,128)S(1)}, f32[8,8]{1,0:T(8,128)}, u32[]{:S(2)}) copy-start(f32[8,8]{1,0:T(8,128)} %three_ref.1) | copy-start | bytes 772
  30.5 9.2 %copy-start.19 = (f32[8,8]{1,0:T(8,128)S(1)}, f32[8,8]{1,0:T(8,128)}, u32[]{:S(2)}) copy-start(f32[8,8]{1,0:T(8,128)} %four_ref.1) | copy-start | bytes 772
  30.5 9.2 %copy-start.20 = (f32[8,8]{1,0:T(8,128)S(1)}, f32[8,8]{1,0:T(8,128)}, u32[]{:S(2)}) copy-start(f32[8,8]{1,0:T(8,128)} %five_ref.1) | copy-start | bytes 772
  30.5 9.2 %copy-start.21 = (f32[8,8]{1,0:T(8,128)S(1)}, f32[8,8]{1,0:T(8,128)}, u32[]{:S(2)}) copy-start(f32[8,8]{1,0:T(8,128)} %six_ref.1) | copy-start | bytes 772
  30.5 9.2 %copy-start.22 = (f32[8,8]{1,0:T(8,128)S(1)}, f32[8,8]{1,0:T(8,128)}, u32[]{:S(2)}) copy-start(f32[8,8]{1,0:T(8,128)} %der_ref.1) | copy-start | bytes 772
  30.5 9.1 %copy-start.23 = (f32[2,4]{1,0:T(2,128)S(1)}, f32[2,4]{1,0:T(2,128)}, u32[]{:S(2)}) copy-start(f32[2,4]{1,0:T(2,128)} %coupling_ref.1) | copy-start | bytes 100
  38.1 108.3 %collective-permute-start.5 = (f32[8,256,512]{2,1,0:T(8,128)}, f32[8,256,512]{2,1,0:T(8,128)}, u32[]{:S(2)}, u32[]{:S(2)}) collective-permute-start(f32[8,256,512]{2,1,0:T(8,128)} %crossing.1.refs_0_.__1_), channel_id=1, source_target_pairs={{0,2},{1,3},{2,0},{3,1},{4,6},{5,7},{6,4},{7,5},{8,10},{9,11},{10,... | collective-permute-start | bytes 12582920 | tf_op jit(solution)/shard_map/ppermute | solution.py:679
  49.3 0.8 copy-start.14
  50.2 1.0 copy-start.25
  51.1 1.0 copy-start.27
  52.1 0.8 copy-start.30
  52.9 1.8 copy-start.8
  54.7 114.4 %collective-permute-start.6 = (f32[8,192,512]{2,1,0:T(8,128)}, f32[8,192,512]{2,1,0:T(8,128)S(1)}, u32[]{:S(2)}, u32[]{:S(2)}) collective-permute-start(f32[8,192,512]{2,1,0:T(8,128)} %handed_on.3.refs_2_), channel_id=1, source_target_pairs={{16,24},{8,0},{17,25},{9,1},{18,26},{10,2},{19,27},{11,3},{20,28},... | collective-permute-start | bytes 9437192 | tf_op jit(solution)/shard_map/ppermute | solution.py:42
  79.3 89.8 %collective-permute-start.7 = (f32[8,192,512]{2,1,0:T(8,128)}, f32[8,192,512]{2,1,0:T(8,128)}, u32[]{:S(2)}, u32[]{:S(2)}) collective-permute-start(f32[8,192,512]{2,1,0:T(8,128)} %handed_on.2.refs_0_), channel_id=1, source_target_pairs={{8,16},{16,8},{9,17},{17,9},{10,18},{18,10},{11,19},{19,11},{12,20... | collective-permute-start | bytes 9437192 | tf_op jit(solution)/shard_map/ppermute | solution.py:42
  81.6 1.2 copy-start.28
  91.6 2.0 copy-start.5
  93.6 11.9 %copy-start.32 = (f32[8,8]{1,0:T(8,128)S(1)}, f32[8,8]{1,0:T(8,128)}, u32[]{:S(2)}) copy-start(f32[8,8]{1,0:T(8,128)} %beta_ref.1) | copy-start | bytes 772
  93.6 11.9 %copy-start.33 = (f32[4]{0:T(128)S(1)}, f32[4]{0:T(128)}, u32[]{:S(2)}) copy-start(f32[4]{0:T(128)} %rot_ref.1) | copy-start | bytes 52
  93.6 52.9 %all-to-all-start.1 = ((f32[8,256,512]{2,1,0:T(8,128)}), f32[8,256,512]{2,1,0:T(8,128)}, u32[]{:S(2)}, u32[]{:S(2)}) async-start(f32[8,256,512]{2,1,0:T(8,128)} %bitcast.22), calls=%async_computation.1 | async-start | bytes 8388608 | tf_op jit(solution)/shard_map/all_to_all | solution.py:712
  102.6 88.6 %collective-permute-start.8 = (f32[8,64,512]{2,1,0:T(8,128)}, f32[8,64,512]{2,1,0:T(8,128)}, u32[]{:S(2)}, u32[]{:S(2)}) collective-permute-start(f32[8,64,512]{2,1,0:T(8,128)} %collective-permute-done.4.refs_3_), channel_id=1, source_target_pairs={{16,24},{8,0},{17,25},{9,1},{18,26},{10,2},{19,27},{11,3},{20,28},... | collective-permute-start | bytes 3145736 | tf_op jit(solution)/shard_map/ppermute | solution.py:42
  103.9 87.3 %collective-permute-start.9 = (f32[8,64,512]{2,1,0:T(8,128)}, f32[8,64,512]{2,1,0:T(8,128)}, u32[]{:S(2)}, u32[]{:S(2)}) collective-permute-start(f32[8,64,512]{2,1,0:T(8,128)} %collective-permute-done.2.refs_1_), channel_id=1, source_target_pairs={{8,16},{16,8},{9,17},{17,9},{10,18},{18,10},{11,19},{19,11},{12,20... | collective-permute-start | bytes 3145736 | tf_op jit(solution)/shard_map/ppermute | solution.py:42
  105.6 2.2 %copy-start.2 = (f32[1,8,8,4,8,512]{5,4,3,2,1,0:T(8,128)S(1)}, f32[1,8,8,4,8,512]{5,4,3,2,1,0:T(8,128)}, u32[]{:S(2)}) copy-start(f32[1,8,8,4,8,512]{5,4,3,2,1,0:T(8,128)} %param.15) | copy-start | bytes 12582916
  107.7 2.2 %copy-start.24 = (f32[1,8,8,4,8,512]{5,4,3,2,1,0:T(8,128)S(1)}, f32[1,8,8,4,8,512]{5,4,3,2,1,0:T(8,128)}, u32[]{:S(2)}) copy-start(f32[1,8,8,4,8,512]{5,4,3,2,1,0:T(8,128)} %param.16) | copy-start | bytes 12582916
  109.9 1.2 copy-start.26
  111.2 1.0 copy-start.29
  112.2 1.0 copy-start.31
  131.3 2.0 copy-start.6
  146.5 2.2 %copy-start.7 = (f32[8,256,512]{2,1,0:T(8,128)S(1)}, f32[8,256,512]{2,1,0:T(8,128)}, u32[]{:S(2)}) copy-start(f32[8,256,512]{2,1,0:T(8,128)} %copy-done.6) | copy-start | bytes 12582916
  148.7 1.9 copy-start.9
  150.5 1.0 copy-start.13
  151.6 1.0 copy-start.15
  152.6 16.4 %copy-start.4 = (f32[8,256,512]{2,1,0:T(8,128)S(1)}, f32[8,256,512]{2,1,0:T(8,128)}, u32[]{:S(2)}) copy-start(f32[8,256,512]{2,1,0:T(8,128)} %copy-done.3) | copy-start | bytes 12582916
  152.6 16.4 %copy-start.11 = (f32[256,512]{1,0:T(8,128)S(1)}, f32[256,512]{1,0:T(8,128)}, u32[]{:S(2)}) copy-start(f32[256,512]{1,0:T(8,128)} %copy-done.10) | copy-start | bytes 1572868

commit v5 on v3

--- a/solution.py
+++ b/solution.py
@@ -116,12 +116,14 @@
 
 def split_kernel(start, vec_ref, out_ref, held, sems):
     count, rows, _ = out_ref.shape
+    size = 2 - count % 2
+    spots = [(i // size, pl.ds(i, size)) for i in range(0, count, size)]
     loads = [
-        pltpu.make_async_copy(vec_ref.at[i, pl.ds(start, rows)], held.at[i], sems.at[0, i])
-        for i in range(count)
+        pltpu.make_async_copy(vec_ref.at[some, pl.ds(start, rows)], held.at[some], sems.at[0, i])
+        for i, some in spots
     ]
     stores = [
-        pltpu.make_async_copy(held.at[i], out_ref.at[i], sems.at[1, i]) for i in range(count)
+        pltpu.make_async_copy(held.at[some], out_ref.at[some], sems.at[1, i]) for i, some in spots
     ]
     for load in loads:
         load.start()
@@ -724,7 +726,7 @@
             vec,
             sums,
             start,
-            block_rows,
+            block_rows if number < len(starts) - 1 else stops[number] - start,
             devices if number == len(starts) - 1 else 1,
         )
         sums = copied[0]

time: 213 us -> 214 us (level)
  no operation moved by 1% of the time
where the time goes in v5:
time: 214 us; the launch traced here: 213 us
  Pallas kernels  82 us (38%)
  starting transfers between devices  53 us (25%)
  local copies, waits for them, and re-layouts  33.2 us (16%)
  waiting for transfers between devices  28.5 us (13%)
  blocking collectives  12 us (6%)
  between operations  3.65 us (2%)
    ppermute x8, starting transfers between devices, pair_exchange(): return lax.ppermute(value, axis, pairs)  39.6 us
    unnamed x68, local copies, waits for them, and re-layouts  32.6 us
    pallas_call x1, Pallas kernels, local_terms(): pl.pallas_call(functools.partial(local_kernel, nvec, nblocks, len(held)),...  18.1 us
    ppermute x8, waiting for transfers between devices, pair_exchange(): return lax.ppermute(value, axis, pairs)  15.5 us
    pallas_call x1, Pallas kernels, join_terms(): pl.pallas_call(functools.partial(join_kernel, tuple(starts), len(sums)),...  15.3 us
    all_to_all x1, waiting for transfers between devices, shards(): lax.all_to_all(mode_shares, 'mode', split_axis=0, concat_axis=0, tiled=True)  13 us
    all_to_all x1, blocking collectives, shards(): lax.all_to_all(copied, ALL_AXES, split_axis=0, concat_axis=0, tiled=True)  12 us
    pallas_call x1, Pallas kernels, operators(): pl.pallas_call(functools.partial(operators_kernel, points, group), in_spe...  9.65 us
  transfers between devices with their start and end apart: 12, of which 2 were waited for; matrix products, arithmetic and copies ran while one was open for 0% of the time, Pallas kernels for 34%

profile of v5, /device:TPU:0, one launch (start us, length us, event | category | flops | bytes accessed | tf_op | source)
XLA Modules:
  0.0 212.5 jit_solution(1701476128036239545)
XLA Ops:
  0.6 0.5 collective-permute-start
  1.1 2.9 %split_rows.2 = f32[8,192,512]{2,1,0:T(8,128)} custom-call(f32[8,256,512]{2,1,0:T(8,128)} %bitcast.17), custom_call_target="tpu_custom_call" | custom-call | bytes 6291456 | tf_op jit(solution)/shard_map/split_rows/pallas_call | solution.py:140
  4.1 0.9 collective-permute-start.3
  4.9 5.3 %collective-permute-start.1 = (f32[8,192,512]{2,1,0:T(8,128)}, f32[8,192,512]{2,1,0:T(8,128)}, u32[]{:S(2)}, u32[]{:S(2)}) collective-permute-start(f32[8,192,512]{2,1,0:T(8,128)} %split_rows.2), channel_id=1, source_target_pairs={{0,8},{8,0},{16,24},{24,16},{1,9},{9,1},{17,25},{25,17},{2,10},{10... | collective-permute-start | bytes 9437192 | tf_op jit(solution)/shard_map/ppermute | solution.py:33
  10.2 2.1 split_rows.3
  12.4 1.6 collective-permute-start.4
  14.1 2.2 %copy-done = f32[1,8,8,4,8,512]{5,4,3,2,1,0:T(8,128)S(1)} copy-done((f32[1,8,8,4,8,512]{5,4,3,2,1,0:T(8,128)S(1)}, f32[1,8,8,4,8,512]{5,4,3,2,1,0:T(8,128)}, u32[]{:S(2)}) %copy-start) | copy-done | bytes 4194328
  16.3 1.0 copy-done.12
  17.3 2.6 %resident.1 = (f32[8,128]{1,0:T(8,128)S(1)}, f32[8,256,512]{2,1,0:T(8,128)S(1)}, f32[256,512]{1,0:T(8,128)S(1)}) custom-call(f32[8,256,512]{2,1,0:T(8,128)S(1)} %bitcast.19, f32[256,512]{1,0:T(8,128)S(1)} %bitcast.23, f32[8,256,512]{2,1,0:T(8,128)} %collective-permute-done.refs_1_.refs_0_), custom_call_target="tpu_custom_call" | custom-call | flops 9437184 | bytes 8388608 | tf_op jit(solution)/shard_map/resident/pallas_call | solution.py:98
  19.9 2.0 copy-done.3
  21.9 0.8 copy-done.10
  22.7 5.7 %all-to-all-start = ((f32[8,256,512]{2,1,0:T(8,128)}), f32[8,256,512]{2,1,0:T(8,128)}, u32[]{:S(2)}, u32[]{:S(2)}) async-start(f32[8,256,512]{2,1,0:T(8,128)} %copy-done.3), calls=%async_computation | async-start | bytes 8388608 | tf_op jit(solution)/shard_map/all_to_all | solution.py:703
  28.4 2.2 %copy-done.1 = f32[1,8,8,4,8,512]{5,4,3,2,1,0:T(8,128)S(1)} copy-done((f32[1,8,8,4,8,512]{5,4,3,2,1,0:T(8,128)S(1)}, f32[1,8,8,4,8,512]{5,4,3,2,1,0:T(8,128)}, u32[]{:S(2)}) %copy-start.1) | copy-done | bytes 4194328
  30.7 7.6 %crossing.1.refs_0_.__1_ = f32[8,256,512]{2,1,0:T(8,128)} custom-call(s32[3]{0:T(128)S(1)} %pad_add_fusion.at_ref, f32[16,16]{1,0:T(8,128)S(1)} %copy-done.16, f32[8,256,512]{2,1,0:T(8,128)S(1)} %bitcast.20, f32[8,256,512]{2,1,0:T(8,128)} %collective-permute-done.refs_1_.refs_0_), custom_call_target="tpu_custom_call" | custom-call | flops 16777216 | bytes 12582912 | tf_op jit(solution)/shard_map/crossing/pallas_call | solution.py:287
  38.3 1.5 collective-permute-start.5
  39.8 9.7 %operators.1 = (f32[2,256,256]{2,1,0:T(8,128)S(1)}, f32[512,512]{1,0:T(8,128)S(1)}, f32[512,512]{1,0:T(8,128)S(1)}, f32[2,256,256]{2,1,0:T(8,128)S(1)}) custom-call(s32[3]{0:T(128)S(1)} %pad_add_fusion.at_ref, f32[2,4]{1,0:T(2,128)S(1)} %copy-done.23, f32[16,16]{1,0:T(8,128)S(1)} %copy-done.17, f32[16,16]{1,0:T(8,128)S(1)} %copy-done.16, ...), custom_call_target="tpu_custom_call" | custom-call | flops 500000000 | bytes 4000000 | tf_op jit(solution)/shard_map/operators/pallas_call | solution.py:234
  49.5 0.8 copy-done.14
  50.3 1.0 copy-done.25
  51.3 1.0 copy-done.27
  52.2 0.8 copy-done.30
  53.1 1.7 copy-done.8
  54.8 26.6 %collective-permute-start.6 = (f32[8,192,512]{2,1,0:T(8,128)}, f32[8,192,512]{2,1,0:T(8,128)S(1)}, u32[]{:S(2)}, u32[]{:S(2)}) collective-permute-start(f32[8,192,512]{2,1,0:T(8,128)} %handed_on.3.refs_2_), channel_id=1, source_target_pairs={{0,8},{8,0},{16,24},{24,16},{1,9},{9,1},{17,25},{25,17},{2,10},{10... | collective-permute-start | bytes 9437192 | tf_op jit(solution)/shard_map/ppermute | solution.py:33
  81.4 2.3 %collective-permute-start.7 = (f32[8,192,512]{2,1,0:T(8,128)}, f32[8,192,512]{2,1,0:T(8,128)}, u32[]{:S(2)}, u32[]{:S(2)}) collective-permute-start(f32[8,192,512]{2,1,0:T(8,128)} %handed_on.2.refs_0_), channel_id=1, source_target_pairs={{8,16},{16,8},{9,17},{17,9},{10,18},{18,10},{11,19},{19,11},{12,20... | collective-permute-start | bytes 9437192 | tf_op jit(solution)/shard_map/ppermute | solution.py:33
  83.7 1.2 copy-done.28
  84.9 8.9 %mode_kinetic.1 = f32[2,4,256,512]{3,2,1,0:T(8,128)S(1)} custom-call(f32[2,4,256,512]{3,2,1,0:T(8,128)} %bitcast.12.in_ref, f32[512,512]{1,0:T(8,128)S(1)} %copy-done.28), custom_call_target="tpu_custom_call" | custom-call | flops 6442450944 | bytes 8388608 | tf_op jit(solution)/shard_map/mode_kinetic/pallas_call | solution.py:358
  93.8 2.0 copy-done.5
  95.8 5.7 %all-to-all-start.1 = ((f32[8,256,512]{2,1,0:T(8,128)}), f32[8,256,512]{2,1,0:T(8,128)}, u32[]{:S(2)}, u32[]{:S(2)}) async-start(f32[8,256,512]{2,1,0:T(8,128)} %bitcast.22), calls=%async_computation.1 | async-start | bytes 8388608 | tf_op jit(solution)/shard_map/all_to_all | solution.py:705
  101.5 0.6 constant_dynamic-slice_fusion.1
  104.7 1.2 collective-permute-start.8
  106.0 1.6 collective-permute-start.9
  107.6 2.2 %copy-done.2 = f32[1,8,8,4,8,512]{5,4,3,2,1,0:T(8,128)S(1)} copy-done((f32[1,8,8,4,8,512]{5,4,3,2,1,0:T(8,128)S(1)}, f32[1,8,8,4,8,512]{5,4,3,2,1,0:T(8,128)}, u32[]{:S(2)}) %copy-start.2) | copy-done | bytes 4194328
  109.8 2.2 %copy-done.24 = f32[1,8,8,4,8,512]{5,4,3,2,1,0:T(8,128)S(1)} copy-done((f32[1,8,8,4,8,512]{5,4,3,2,1,0:T(8,128)S(1)}, f32[1,8,8,4,8,512]{5,4,3,2,1,0:T(8,128)}, u32[]{:S(2)}) %copy-start.24) | copy-done | bytes 4194328
  112.0 1.2 copy-done.26
  113.2 1.0 copy-done.29
  114.3 1.0 copy-done.31
  115.3 18.1 %local_terms.1.work_ref = f32[8,256,512]{2,1,0:T(8,128)S(1)} custom-call(s32[3]{0:T(128)S(1)} %pad_add_fusion.at_ref, f32[4]{0:T(128)S(1)} %copy-done.33, f32[8,8]{1,0:T(8,128)S(1)} %copy-done.32, f32[8,256,512]{2,1,0:T(8,128)S(1)} %bitcast.21, f32[8,256,512]{2,1,0:T(8,128)} %collective-permute-done.refs_1_.refs_0_, f32[8,256,512]{2,1,0:T(8,128)S(1)} %bitcast.26, ...), custom_call_target="tpu_custom_call" | custom-call | flops 12884901888 | bytes 16777216 | tf_op jit(solution)/shard_map/local_terms/pallas_call | solution.py:323
  133.4 2.0 copy-done.6
  135.4 13.0 %all-to-all-done.1.refs_4_ = f32[8,256,512]{2,1,0:T(8,128)} async-done(((f32[8,256,512]{2,1,0:T(8,128)}), f32[8,256,512]{2,1,0:T(8,128)}, u32[]{:S(2)}, u32[]{:S(2)}) %all-to-all-start.1) | async-done | bytes 4194336 | tf_op jit(solution)/shard_map/all_to_all | solution.py:705
  148.4 2.2 %copy-done.7 = f32[8,256,512]{2,1,0:T(8,128)S(1)} copy-done((f32[8,256,512]{2,1,0:T(8,128)S(1)}, f32[8,256,512]{2,1,0:T(8,128)}, u32[]{:S(2)}) %copy-start.7) | copy-done | bytes 4194328
  150.6 1.9 copy-done.9
  152.5 1.0 copy-done.13
  153.6 1.0 copy-done.15
  154.6 15.3 %join_terms.1.work_ref = f32[8,256,512]{2,1,0:T(8,128)S(1)} custom-call(s32[3]{0:T(128)S(1)} %pad_add_fusion.at_ref, f32[8,256,512]{2,1,0:T(8,128)S(1)} %copy-done.7, f32[256,512]{1,0:T(8,128)S(1)} %bitcast.24, f32[2,256,256]{2,1,0:T(8,128)S(1)} %copy-done.15, f32[8,192,512]{2,1,0:T(8,128)} %handed_on.2.refs_0_, ...), custom_call_target="tpu_custom_call" | custom-call | flops 6442450944 | bytes 25165824 | tf_op jit(solution)/shard_map/join_terms/pallas_call | solution.py:402
  170.0 5.9 %far_terms.2 = (f32[8,256,512]{2,1,0:T(8,128)S(1)}, f32[1,8,128]{2,1,0:T(8,128)S(1)}) custom-call(f32[2]{0:T(128)S(1)} %pad_maximum_fusion.coef_ref, f32[8,256,512]{2,1,0:T(8,128)S(1)} %join_terms.1.work_ref, f32[8,192,512]{2,1,0:T(8,128)S(1)} %collective-permute-done.6.first_ref, ...), custom_call_target="tpu_custom_call", output_to_operand_aliasing={{0}: (1, {})} | custom-call | flops 18874368 | bytes 15728640 | tf_op jit(solution)/shard_map/far_terms/pallas_call | solution.py:469
  175.9 15.5 %collective-permute-done.8.first_ref = f32[8,64,512]{2,1,0:T(8,128)} collective-permute-done((f32[8,64,512]{2,1,0:T(8,128)}, f32[8,64,512]{2,1,0:T(8,128)}, u32[]{:S(2)}, u32[]{:S(2)}) %collective-permute-start.8) | collective-permute-done | bytes 1048608 | tf_op jit(solution)/shard_map/ppermute | solution.py:33
  191.3 2.9 %far_terms.3 = (f32[8,256,512]{2,1,0:T(8,128)S(1)}, f32[32,8,128]{2,1,0:T(8,128)S(1)}) custom-call(f32[2]{0:T(128)S(1)} %pad_maximum_fusion.coef_ref, f32[8,256,512]{2,1,0:T(8,128)S(1)} %get-tuple-element.24.work_ref, f32[8,64,512]{2,1,0:T(8,128)} %collective-permute-done.8.first_ref, ...), custom_call_target="tpu_custom_call", output_to_operand_aliasing={{0}: (1, {})} | custom-call | flops 6291456 | bytes 5242880 | tf_op jit(solution)/shard_map/far_terms/pallas_call | solution.py:469
  194.2 12.0 %all_to_all.15.sum_ref = f32[32,8,128]{2,1,0:T(8,128)S(1)} all-to-all(f32[32,8,128]{2,1,0:T(8,128)S(1)} %get-tuple-element.26), channel_id=1, replica_groups=mesh['ka'=4,'mode'=2,'row'=4] {'ka','mode','row'}, dimensions={0} | all-to-all | bytes 262144 | tf_op jit(solution)/shard_map/all_to_all | solution.py:733
  206.2 6.1 %basis.1 = (f32[8,256,512]{2,1,0:T(8,128)}, f32[8,8]{1,0:T(8,128)}, f32[8,8]{1,0:T(8,128)}) custom-call(f32[32,8,128]{2,1,0:T(8,128)S(1)} %all_to_all.15.sum_ref, f32[8,256,512]{2,1,0:T(8,128)S(1)} %get-tuple-element.27.work_ref, f32[8,256,512]{2,1,0:T(8,128)S(1)} %copy-done.4), custom_call_target="tpu_custom_call" | custom-call | flops 33554432 | bytes 12582912 | tf_op jit(solution)/shard_map/basis/pallas_call | solution.py:612
  (61 shorter events, 0.4 us)
Async XLA Ops:
  0.6 13.5 %collective-permute-start = (f32[8,256,512]{2,1,0:T(8,128)}, f32[8,256,512]{2,1,0:T(8,128)}, u32[]{:S(2)}, u32[]{:S(2)}) collective-permute-start(f32[8,256,512]{2,1,0:T(8,128)} %bitcast.16), channel_id=1, source_target_pairs={{0,1},{1,0},{2,3},{3,2},{4,5},{5,4},{6,7},{7,6},{8,9},{9,8},{10,11... | collective-permute-start | bytes 12582920 | tf_op jit(solution)/shard_map/ppermute | solution.py:668
  4.1 49.0 %collective-permute-start.3 = (f32[8,192,512]{2,1,0:T(8,128)}, f32[8,192,512]{2,1,0:T(8,128)S(1)}, u32[]{:S(2)}, u32[]{:S(2)}) collective-permute-start(f32[8,192,512]{2,1,0:T(8,128)} %split_rows.2), channel_id=1, source_target_pairs={{8,16},{16,8},{9,17},{17,9},{10,18},{18,10},{11,19},{19,11},{12,20... | collective-permute-start | bytes 9437192 | tf_op jit(solution)/shard_map/ppermute | solution.py:33
  4.9 76.5 %collective-permute-start.1 = (f32[8,192,512]{2,1,0:T(8,128)}, f32[8,192,512]{2,1,0:T(8,128)}, u32[]{:S(2)}, u32[]{:S(2)}) collective-permute-start(f32[8,192,512]{2,1,0:T(8,128)} %split_rows.2), channel_id=1, source_target_pairs={{0,8},{8,0},{16,24},{24,16},{1,9},{9,1},{17,25},{25,17},{2,10},{10... | collective-permute-start | bytes 9437192 | tf_op jit(solution)/shard_map/ppermute | solution.py:33
  12.3 93.7 %collective-permute-start.2 = (f32[8,64,512]{2,1,0:T(8,128)}, f32[8,64,512]{2,1,0:T(8,128)}, u32[]{:S(2)}, u32[]{:S(2)}) collective-permute-start(f32[8,64,512]{2,1,0:T(8,128)} %split_rows.3), channel_id=1, source_target_pairs={{0,8},{8,0},{16,24},{24,16},{1,9},{9,1},{17,25},{25,17},{2,10},{10... | collective-permute-start | bytes 3145736 | tf_op jit(solution)/shard_map/ppermute | solution.py:33
  12.4 92.4 %collective-permute-start.4 = (f32[8,64,512]{2,1,0:T(8,128)}, f32[8,64,512]{2,1,0:T(8,128)}, u32[]{:S(2)}, u32[]{:S(2)}) collective-permute-start(f32[8,64,512]{2,1,0:T(8,128)} %split_rows.3), channel_id=1, source_target_pairs={{8,16},{16,8},{9,17},{17,9},{10,18},{18,10},{11,19},{19,11},{12,20... | collective-permute-start | bytes 3145736 | tf_op jit(solution)/shard_map/ppermute | solution.py:33
  14.1 2.2 %copy-start = (f32[1,8,8,4,8,512]{5,4,3,2,1,0:T(8,128)S(1)}, f32[1,8,8,4,8,512]{5,4,3,2,1,0:T(8,128)}, u32[]{:S(2)}) copy-start(f32[1,8,8,4,8,512]{5,4,3,2,1,0:T(8,128)} %param.15) | copy-start | bytes 12582916
  16.3 1.0 copy-start.12
  19.9 2.0 copy-start.3
  21.9 0.8 copy-start.10
  22.7 5.7 %copy-start.16 = (f32[16,16]{1,0:T(8,128)S(1)}, f32[16,16]{1,0:T(8,128)}, u32[]{:S(2)}) copy-start(f32[16,16]{1,0:T(8,128)} %two_ref.3) | copy-start | bytes 3076
  22.7 61.0 %all-to-all-start = ((f32[8,256,512]{2,1,0:T(8,128)}), f32[8,256,512]{2,1,0:T(8,128)}, u32[]{:S(2)}, u32[]{:S(2)}) async-start(f32[8,256,512]{2,1,0:T(8,128)} %copy-done.3), calls=%async_computation | async-start | bytes 8388608 | tf_op jit(solution)/shard_map/all_to_all | solution.py:703
  28.4 2.2 %copy-start.1 = (f32[1,8,8,4,8,512]{5,4,3,2,1,0:T(8,128)S(1)}, f32[1,8,8,4,8,512]{5,4,3,2,1,0:T(8,128)}, u32[]{:S(2)}) copy-start(f32[1,8,8,4,8,512]{5,4,3,2,1,0:T(8,128)} %param.15) | copy-start | bytes 12582916
  30.6 9.2 %copy-start.17 = (f32[16,16]{1,0:T(8,128)S(1)}, f32[16,16]{1,0:T(8,128)}, u32[]{:S(2)}) copy-start(f32[16,16]{1,0:T(8,128)} %one_ref.1) | copy-start | bytes 3076
  30.6 9.2 %copy-start.18 = (f32[8,8]{1,0:T(8,128)S(1)}, f32[8,8]{1,0:T(8,128)}, u32[]{:S(2)}) copy-start(f32[8,8]{1,0:T(8,128)} %three_ref.1) | copy-start | bytes 772
  30.6 9.2 %copy-start.19 = (f32[8,8]{1,0:T(8,128)S(1)}, f32[8,8]{1,0:T(8,128)}, u32[]{:S(2)}) copy-start(f32[8,8]{1,0:T(8,128)} %four_ref.1) | copy-start | bytes 772
  30.6 9.2 %copy-start.20 = (f32[8,8]{1,0:T(8,128)S(1)}, f32[8,8]{1,0:T(8,128)}, u32[]{:S(2)}) copy-start(f32[8,8]{1,0:T(8,128)} %five_ref.1) | copy-start | bytes 772
  30.6 9.2 %copy-start.21 = (f32[8,8]{1,0:T(8,128)S(1)}, f32[8,8]{1,0:T(8,128)}, u32[]{:S(2)}) copy-start(f32[8,8]{1,0:T(8,128)} %six_ref.1) | copy-start | bytes 772
  30.6 9.2 %copy-start.22 = (f32[8,8]{1,0:T(8,128)S(1)}, f32[8,8]{1,0:T(8,128)}, u32[]{:S(2)}) copy-start(f32[8,8]{1,0:T(8,128)} %der_ref.1) | copy-start | bytes 772
  30.6 9.1 %copy-start.23 = (f32[2,4]{1,0:T(2,128)S(1)}, f32[2,4]{1,0:T(2,128)}, u32[]{:S(2)}) copy-start(f32[2,4]{1,0:T(2,128)} %coupling_ref.1) | copy-start | bytes 100
  38.3 110.2 %collective-permute-start.5 = (f32[8,256,512]{2,1,0:T(8,128)}, f32[8,256,512]{2,1,0:T(8,128)}, u32[]{:S(2)}, u32[]{:S(2)}) collective-permute-start(f32[8,256,512]{2,1,0:T(8,128)} %crossing.1.refs_0_.__1_), channel_id=1, source_target_pairs={{0,2},{1,3},{2,0},{3,1},{4,6},{5,7},{6,4},{7,5},{8,10},{9,11},{10,... | collective-permute-start | bytes 12582920 | tf_op jit(solution)/shard_map/ppermute | solution.py:672
  49.5 0.8 copy-start.14
  50.3 1.0 copy-start.25
  51.3 1.0 copy-start.27
  52.2 0.8 copy-start.30
  53.1 1.8 copy-start.8
  54.8 115.1 %collective-permute-start.6 = (f32[8,192,512]{2,1,0:T(8,128)}, f32[8,192,512]{2,1,0:T(8,128)S(1)}, u32[]{:S(2)}, u32[]{:S(2)}) collective-permute-start(f32[8,192,512]{2,1,0:T(8,128)} %handed_on.3.refs_2_), channel_id=1, source_target_pairs={{0,8},{8,0},{16,24},{24,16},{1,9},{9,1},{17,25},{25,17},{2,10},{10... | collective-permute-start | bytes 9437192 | tf_op jit(solution)/shard_map/ppermute | solution.py:33
  81.4 88.5 %collective-permute-start.7 = (f32[8,192,512]{2,1,0:T(8,128)}, f32[8,192,512]{2,1,0:T(8,128)}, u32[]{:S(2)}, u32[]{:S(2)}) collective-permute-start(f32[8,192,512]{2,1,0:T(8,128)} %handed_on.2.refs_0_), channel_id=1, source_target_pairs={{8,16},{16,8},{9,17},{17,9},{10,18},{18,10},{11,19},{19,11},{12,20... | collective-permute-start | bytes 9437192 | tf_op jit(solution)/shard_map/ppermute | solution.py:33
  83.7 1.2 copy-start.28
  93.8 2.0 copy-start.5
  95.8 11.9 %copy-start.32 = (f32[8,8]{1,0:T(8,128)S(1)}, f32[8,8]{1,0:T(8,128)}, u32[]{:S(2)}) copy-start(f32[8,8]{1,0:T(8,128)} %beta_ref.1) | copy-start | bytes 772
  95.8 11.9 %copy-start.33 = (f32[4]{0:T(128)S(1)}, f32[4]{0:T(128)}, u32[]{:S(2)}) copy-start(f32[4]{0:T(128)} %rot_ref.1) | copy-start | bytes 52
  95.8 52.7 %all-to-all-start.1 = ((f32[8,256,512]{2,1,0:T(8,128)}), f32[8,256,512]{2,1,0:T(8,128)}, u32[]{:S(2)}, u32[]{:S(2)}) async-start(f32[8,256,512]{2,1,0:T(8,128)} %bitcast.22), calls=%async_computation.1 | async-start | bytes 8388608 | tf_op jit(solution)/shard_map/all_to_all | solution.py:705
  104.7 86.6 %collective-permute-start.8 = (f32[8,64,512]{2,1,0:T(8,128)}, f32[8,64,512]{2,1,0:T(8,128)}, u32[]{:S(2)}, u32[]{:S(2)}) collective-permute-start(f32[8,64,512]{2,1,0:T(8,128)} %collective-permute-done.4.refs_3_), channel_id=1, source_target_pairs={{0,8},{8,0},{16,24},{24,16},{1,9},{9,1},{17,25},{25,17},{2,10},{10... | collective-permute-start | bytes 3145736 | tf_op jit(solution)/shard_map/ppermute | solution.py:33
  106.0 85.4 %collective-permute-start.9 = (f32[8,64,512]{2,1,0:T(8,128)}, f32[8,64,512]{2,1,0:T(8,128)}, u32[]{:S(2)}, u32[]{:S(2)}) collective-permute-start(f32[8,64,512]{2,1,0:T(8,128)} %collective-permute-done.2.refs_1_), channel_id=1, source_target_pairs={{8,16},{16,8},{9,17},{17,9},{10,18},{18,10},{11,19},{19,11},{12,20... | collective-permute-start | bytes 3145736 | tf_op jit(solution)/shard_map/ppermute | solution.py:33
  107.6 2.2 %copy-start.2 = (f32[1,8,8,4,8,512]{5,4,3,2,1,0:T(8,128)S(1)}, f32[1,8,8,4,8,512]{5,4,3,2,1,0:T(8,128)}, u32[]{:S(2)}) copy-start(f32[1,8,8,4,8,512]{5,4,3,2,1,0:T(8,128)} %param.15) | copy-start | bytes 12582916
  109.8 2.2 %copy-start.24 = (f32[1,8,8,4,8,512]{5,4,3,2,1,0:T(8,128)S(1)}, f32[1,8,8,4,8,512]{5,4,3,2,1,0:T(8,128)}, u32[]{:S(2)}) copy-start(f32[1,8,8,4,8,512]{5,4,3,2,1,0:T(8,128)} %param.16) | copy-start | bytes 12582916
  112.0 1.2 copy-start.26
  113.2 1.0 copy-start.29
  114.3 1.0 copy-start.31
  133.4 2.0 copy-start.6
  148.4 2.2 %copy-start.7 = (f32[8,256,512]{2,1,0:T(8,128)S(1)}, f32[8,256,512]{2,1,0:T(8,128)}, u32[]{:S(2)}) copy-start(f32[8,256,512]{2,1,0:T(8,128)} %copy-done.6) | copy-start | bytes 12582916
  150.6 1.9 copy-start.9
  152.5 1.0 copy-start.13
  153.6 1.0 copy-start.15
  154.6 15.4 %copy-start.4 = (f32[8,256,512]{2,1,0:T(8,128)S(1)}, f32[8,256,512]{2,1,0:T(8,128)}, u32[]{:S(2)}) copy-start(f32[8,256,512]{2,1,0:T(8,128)} %copy-done.3) | copy-start | bytes 12582916
  154.6 15.4 %copy-start.11 = (f32[256,512]{1,0:T(8,128)S(1)}, f32[256,512]{1,0:T(8,128)}, u32[]{:S(2)}) copy-start(f32[256,512]{1,0:T(8,128)} %copy-done.10) | copy-start | bytes 1572868
